TPU v7x, 32 devices: a whole 2x2x4 slice. The times are simulated.
32 devices in a mesh: grp: 4 (over x, core), blk: 8 (over z, y).
Axes of the slice: x: 2, y: 2, z: 4, core: 2. Of those that a mesh axis runs over, the one named last changes fastest.
Arguments:
- block_input: bfloat16 [4, 1024, 2048], P('grp', 'blk'), may hold values from -6 to 6
- doc_lens: int32 [4, 8], P('grp'), may hold values from 1 to 1024, as said below
- norm_attn: bfloat16 [2048], P('blk'), may hold values from 0.5 to 1.5
- w_qkv: bfloat16 [2048, 6144], P('blk'), may hold values from -0.125 to 0.125
- w_out: bfloat16 [2048, 2048], P('blk'), may hold values from -2 to 2
- norm_mlp: bfloat16 [2048], P('blk'), may hold values from 0.5 to 1.5
- w_gate: bfloat16 [2048, 5632], P('blk'), may hold values from -0.125 to 0.125
- w_up: bfloat16 [2048, 5632], P('blk'), may hold values from -0.125 to 0.125
- w_down: bfloat16 [5632, 2048], P('blk'), may hold values from -0.078125 to 0.078125
- cot: bfloat16 [4, 1024, 2048], P('grp', 'blk'), may hold values from -6 to 6
Outputs:
- block_out: bfloat16 [4, 1024, 2048], P('grp', 'blk')
- x_grad: bfloat16 [4, 1024, 2048], P('grp', 'blk')
- grad_norm_attn: float32 [2048], P('blk')
- grad_qkv: float32 [2048, 6144], P('blk')
- grad_out: float32 [2048, 2048], P('blk')
- grad_norm_mlp: float32 [2048], P('blk')
- grad_gate: float32 [2048, 5632], P('blk')
- grad_up: float32 [2048, 5632], P('blk')
- grad_down: float32 [5632, 2048], P('blk')
Inputs may be any that keep to these rules, and one draw needn't show every extreme that they name: `doc_lens`: each row lists the lengths of 8 documents packed in order over its stream; they sum to 1024, and one of them begins within the first 128 positions and ends within the last 128.
All inputs are finite; a program needn't handle non-finite values.
Results may differ from a plain program's by a relative error of at most 0.023.
Values may be sent and summed in bfloat16 or wider, within the bound.
A program may use at most 640 MiB of HBM per device.

v0:
```python
import math

import jax
import jax.numpy as jnp
from jax import lax
from jax.sharding import PartitionSpec as P

HEADS = 16
HEAD = 128


EPS = 1e-05
NEGATIVE = -1e30


def angle_tables(places):
    half_size = HEAD // 2
    freqs = jnp.exp(jnp.arange(half_size, dtype=jnp.float32) * (-2.0 * math.log(10000.0) / HEAD))
    angles = places.astype(jnp.float32)[:, None] * freqs
    return (jnp.cos(angles)[:, None, :], jnp.sin(angles)[:, None, :])


def rotate(tensor, cosine, sine_part):
    half_size = HEAD // 2
    first_half = tensor[..., :half_size]
    second_half = tensor[..., half_size:]
    return jnp.concatenate(
        [
            first_half * cosine - second_half * sine_part,
            second_half * cosine + first_half * sine_part,
        ],
        axis=-1,
    )


def unrotate(tensor, cosine, sine_part):
    half_size = HEAD // 2
    first_half = tensor[..., :half_size]
    second_half = tensor[..., half_size:]
    return jnp.concatenate(
        [
            first_half * cosine + second_half * sine_part,
            second_half * cosine - first_half * sine_part,
        ],
        axis=-1,
    )


def segment_of(places, starts):
    return jnp.sum((starts[None, :] <= places[:, None]).astype(jnp.int32), axis=1) - 1


def start_of(places, starts):
    return jnp.max(jnp.where(starts[None, :] <= places[:, None], starts[None, :], 0), axis=1)


def contract_rows(left, right):
    return lax.dot_general(
        left, right, (((1,), (1,)), ((), ())), preferred_element_type=jnp.float32
    )


def weight_term(left, right):

    def term(start, count):
        return lax.dot_general(
            left, right, (((0,), (0,)), ((), ())), preferred_element_type=jnp.float32
        )

    return term


def shard_grad(term_fn, shard_rows):
    shared = lax.psum_scatter(
        term_fn(jnp.int32(0), shard_rows * lax.axis_size("blk")).astype(jnp.bfloat16),
        "blk",
        scatter_dimension=0,
        tiled=True,
    )
    return lax.psum(shared, "grp").astype(jnp.float32)


def per_device(block_input, doc_lens, norm_attn, w_qkv, w_out, norm_mlp, w_gate, w_up, w_down, cot):
    tok_rows = block_input.shape[1]
    width = block_input.shape[2]
    score_scale = HEAD ** (-0.5)
    shards = (norm_attn, w_qkv, w_out, norm_mlp, w_gate, w_up, w_down)
    gathered = (
        lax.all_gather(shards[0], "blk", axis=0, tiled=True),
        lax.all_gather(shards[1], "blk", axis=0, tiled=True),
        lax.all_gather(shards[2], "blk", axis=0, tiled=True),
        lax.all_gather(shards[3], "blk", axis=0, tiled=True),
        lax.all_gather(shards[4], "blk", axis=0, tiled=True),
        lax.all_gather(shards[5], "blk", axis=0, tiled=True),
        lax.all_gather(shards[6], "blk", axis=0, tiled=True),
    )
    gain_one, weight_qkv, weight_out, gain_two, weight_gate, weight_up, weight_down = gathered
    place_rows = lax.axis_index("blk") * tok_rows + jnp.arange(tok_rows, dtype=jnp.int32)
    lengths = doc_lens[0]
    starts = jnp.cumsum(lengths) - lengths
    query_seg = segment_of(place_rows, starts)
    cosine, sine_part = angle_tables(place_rows - start_of(place_rows, starts))
    x_float = block_input[0].astype(jnp.float32)
    inv_one = lax.rsqrt(jnp.mean(x_float * x_float, axis=-1, keepdims=True) + EPS)
    normed_one = (x_float * inv_one * gain_one.astype(jnp.float32)).astype(jnp.bfloat16)
    projected = jnp.dot(normed_one, weight_qkv, preferred_element_type=jnp.float32)
    heads_all = projected.reshape(tok_rows, 3, HEADS, HEAD)
    queries = rotate(heads_all[:, 0], cosine, sine_part).astype(jnp.bfloat16)
    keys_own = rotate(heads_all[:, 1], cosine, sine_part).astype(jnp.bfloat16)
    values_own = heads_all[:, 2].astype(jnp.bfloat16)

    def pair_mask(count):
        key_places = jnp.arange(count, dtype=jnp.int32)
        key_seg = segment_of(key_places, starts)
        return (query_seg[:, None] == key_seg[None, :]) & (
            key_places[None, :] <= place_rows[:, None]
        )

    piece = (
        lax.all_gather(keys_own, "blk", axis=0, tiled=True),
        lax.all_gather(values_own, "blk", axis=0, tiled=True),
    )
    count = piece[0].shape[0]
    row_peak = jnp.full((HEADS, tok_rows), NEGATIVE, jnp.float32)
    key_piece, value_piece = piece
    count = key_piece.shape[0]
    allowed = pair_mask(count)[None]
    scores = (
        jnp.einsum("qhd,khd->hqk", queries, key_piece, preferred_element_type=jnp.float32)
        * score_scale
    )
    scores = jnp.where(allowed, scores, NEGATIVE)
    new_peak = jnp.maximum(row_peak, jnp.max(scores, axis=-1))
    weights_now = jnp.where(allowed, jnp.exp(scores - new_peak[..., None]), 0.0)
    row_total = jnp.sum(weights_now, axis=-1)
    accum = jnp.einsum(
        "hqk,khd->hqd",
        weights_now.astype(jnp.bfloat16),
        value_piece,
        preferred_element_type=jnp.float32,
    )
    row_peak, row_total, accum = (new_peak, row_total, accum)
    log_total = row_peak + jnp.log(row_total)
    attended = (accum / row_total[..., None]).transpose(1, 0, 2)
    attended_b = attended.reshape(tok_rows, width).astype(jnp.bfloat16)
    resid = x_float + jnp.dot(attended_b, weight_out, preferred_element_type=jnp.float32)
    inv_two = lax.rsqrt(jnp.mean(resid * resid, axis=-1, keepdims=True) + EPS)
    normed_two = (resid * inv_two * gain_two.astype(jnp.float32)).astype(jnp.bfloat16)
    gate_proj = jnp.dot(normed_two, weight_gate, preferred_element_type=jnp.float32)
    up_proj = jnp.dot(normed_two, weight_up, preferred_element_type=jnp.float32)
    sigmoid_gate = jax.nn.sigmoid(gate_proj)
    swish = gate_proj * sigmoid_gate
    hidden = (swish * up_proj).astype(jnp.bfloat16)
    block_out = (resid + jnp.dot(hidden, weight_down, preferred_element_type=jnp.float32)).astype(
        jnp.bfloat16
    )
    again = (
        lax.all_gather(shards[0], "blk", axis=0, tiled=True),
        lax.all_gather(shards[1], "blk", axis=0, tiled=True),
        lax.all_gather(shards[2], "blk", axis=0, tiled=True),
        lax.all_gather(shards[3], "blk", axis=0, tiled=True),
        lax.all_gather(shards[4], "blk", axis=0, tiled=True),
        lax.all_gather(shards[5], "blk", axis=0, tiled=True),
        lax.all_gather(shards[6], "blk", axis=0, tiled=True),
    )
    back_gain_one, back_qkv, back_out, back_gain_two, back_gate, back_up, back_down = again
    seed = cot[0]
    seed_float = seed.astype(jnp.float32)
    dhidden = contract_rows(seed, back_down)
    dgate = (dhidden * up_proj * sigmoid_gate * (1.0 + gate_proj * (1.0 - sigmoid_gate))).astype(
        jnp.bfloat16
    )
    dup = (dhidden * swish).astype(jnp.bfloat16)
    dnormed_two = contract_rows(dgate, back_gate) + contract_rows(dup, back_up)
    a_two = dnormed_two * back_gain_two.astype(jnp.float32)
    dresid = (
        seed_float
        + inv_two * a_two
        - resid * inv_two**3 * jnp.mean(a_two * resid, axis=-1, keepdims=True)
    )
    dresid_b = dresid.astype(jnp.bfloat16)
    dattended = (
        contract_rows(dresid_b, back_out).astype(jnp.bfloat16).reshape(tok_rows, HEADS, HEAD)
    )
    delta = jnp.sum(dattended.astype(jnp.float32) * attended, axis=-1).T
    piece = (
        lax.all_gather(keys_own, "blk", axis=0, tiled=True),
        lax.all_gather(values_own, "blk", axis=0, tiled=True),
    )
    count = piece[0].shape[0]
    key_piece, value_piece = piece
    count = key_piece.shape[0]
    score_count = key_piece.shape[0]
    allowed = pair_mask(score_count)[None]
    scores = (
        jnp.einsum("qhd,khd->hqk", queries, key_piece, preferred_element_type=jnp.float32)
        * score_scale
    )
    probs = jnp.where(allowed, jnp.exp(scores - log_total[..., None]), 0.0)
    dprobs = jnp.einsum("qhd,khd->hqk", dattended, value_piece, preferred_element_type=jnp.float32)
    dscores = (probs * (dprobs - delta[..., None])).astype(jnp.bfloat16)
    probs, dscores = (probs, dscores)
    dquery_acc = score_scale * jnp.einsum(
        "hqk,khd->hqd", dscores, key_piece, preferred_element_type=jnp.float32
    )
    dkeys = score_scale * jnp.einsum(
        "hqk,qhd->khd", dscores, queries, preferred_element_type=jnp.float32
    )
    dvalues = jnp.einsum(
        "hqk,qhd->khd", probs.astype(jnp.bfloat16), dattended, preferred_element_type=jnp.float32
    )
    stacked = jnp.concatenate([dkeys.reshape(count, width), dvalues.reshape(count, width)], axis=1)
    grads_buffer = stacked
    dquery_acc, grads_buffer = (dquery_acc, grads_buffer)
    own_grads = lax.psum_scatter(
        grads_buffer.astype(jnp.bfloat16), "blk", scatter_dimension=0, tiled=True
    ).astype(jnp.float32)
    dkey = unrotate(own_grads[:, :width].reshape(tok_rows, HEADS, HEAD), cosine, sine_part)
    dvalue = own_grads[:, width:].reshape(tok_rows, HEADS, HEAD)
    dquery = unrotate(dquery_acc.transpose(1, 0, 2), cosine, sine_part)
    dqkv = (
        jnp.stack([dquery, dkey, dvalue], axis=1).reshape(tok_rows, 3 * width).astype(jnp.bfloat16)
    )
    dnormed_one = contract_rows(dqkv, back_qkv)
    a_one = dnormed_one * back_gain_one.astype(jnp.float32)
    x_grad = (
        dresid
        + inv_one * a_one
        - x_float * inv_one**3 * jnp.mean(a_one * x_float, axis=-1, keepdims=True)
    ).astype(jnp.bfloat16)
    width_rows = norm_attn.shape[0]
    gain_terms = jnp.stack(
        [
            jnp.sum(dnormed_one * x_float * inv_one, axis=0),
            jnp.sum(dnormed_two * resid * inv_two, axis=0),
        ],
        axis=1,
    )

    def gain_slice(start, count):
        return gain_terms

    grad_down = shard_grad(weight_term(hidden, seed), w_down.shape[0])
    grad_gate = shard_grad(weight_term(normed_two, dgate), width_rows)
    grad_up = shard_grad(weight_term(normed_two, dup), width_rows)
    grad_out = shard_grad(weight_term(attended_b, dresid_b), width_rows)
    grad_qkv = shard_grad(weight_term(normed_one, dqkv), width_rows)
    gain_grads = shard_grad(gain_slice, width_rows)
    return (
        block_out[None],
        x_grad[None],
        gain_grads[:, 0],
        grad_qkv,
        grad_out,
        gain_grads[:, 1],
        grad_gate,
        grad_up,
        grad_down,
    )


def solution(mesh):
    return jax.shard_map(
        per_device,
        mesh=mesh,
        in_specs=(
            P("grp", "blk", None),
            P("grp", None),
            P("blk"),
            P("blk", None),
            P("blk", None),
            P("blk"),
            P("blk", None),
            P("blk", None),
            P("blk", None),
            P("grp", "blk", None),
        ),
        out_specs=(
            P("grp", "blk", None),
            P("grp", "blk", None),
            P("blk"),
            P("blk", None),
            P("blk", None),
            P("blk"),
            P("blk", None),
            P("blk", None),
            P("blk", None),
        ),
        check_vma=False,
    )
```

profile of v0, /device:TPU:1, one launch (start us, length us, event | category | flops | bytes accessed | tf_op | source)
XLA Modules:
  0.0 4387.7 jit_solution(13569372776182603494)
XLA Ops:
  8.6 18.7 all-gather.1
  28.9 1.2 fusion.37
  30.9 461.3 %all-gather.11.cloned.1.call-done = bf16[2048,6144]{1,0:T(8,128)(2,1)} async-done(((bf16[256,6144]{1,0:T(8,128)(2,1)}), bf16[2048,6144]{1,0:T(8,128)(2,1)}) %all-gather.11.cloned.1.call-update) | async-done | bytes 25165840 | tf_op jit(solution)/shard_map/all_gather | solution.py:90
  492.2 32.3 copy.37
  524.5 11.9 fusion.52
  536.6 1.0 subtract_convert_fusion.1
  541.9 15.9 all-gather.2
  558.2 55.0 %all-gather.13.cloned.1.call-done = bf16[1024,16,128]{0,2,1:T(8,128)(2,1)} async-done(((bf16[128,16,128]{0,2,1:T(8,128)(2,1)}), bf16[1024,16,128]{0,2,1:T(8,128)(2,1)}) %all-gather.13.cloned.1.call-update) | async-done | bytes 4194320 | tf_op jit(solution)/shard_map/all_gather | solution.py:120
  613.2 4.2 select_reduce_fusion
  617.4 3.2 copy-done
  620.6 2.7 fusion.1
  623.4 65.7 %all-gather.23.cloned.1.call-done = bf16[1024,1,16,128]{0,3,2,1:T(8,128)(2,1)} async-done(((bf16[128,1,16,128]{0,3,2,1:T(8,128)(2,1)}), bf16[1024,1,16,128]{0,3,2,1:T(8,128)(2,1)}) %all-gather.23.cloned.1.call-update) | async-done | bytes 4194320 | tf_op jit(solution)/shard_map/all_gather | solution.py:121
  689.1 8.2 fusion.74
  697.2 116.9 %all-gather.15.cloned.1.call-done = bf16[2048,2048]{1,0:T(8,128)(2,1)} async-done(((bf16[256,2048]{1,0:T(8,128)(2,1)}), bf16[2048,2048]{1,0:T(8,128)(2,1)}) %all-gather.15.cloned.1.call-update) | async-done | bytes 8388624 | tf_op jit(solution)/shard_map/all_gather | solution.py:91
  814.2 4.7 multiply_reduce_fusion.3
  819.6 435.7 %all-gather.19.cloned.1.call-done = bf16[2048,5632]{1,0:T(8,128)(2,1)} async-done(((bf16[256,5632]{1,0:T(8,128)(2,1)}), bf16[2048,5632]{1,0:T(8,128)(2,1)}) %all-gather.19.cloned.1.call-update) | async-done | bytes 23068688 | tf_op jit(solution)/shard_map/all_gather | solution.py:94
  1255.3 12.3 fusion.76
  1267.6 430.2 %all-gather.17.cloned.1.call-done = bf16[2048,5632]{1,0:T(8,128)(2,1)} async-done(((bf16[256,5632]{1,0:T(8,128)(2,1)}), bf16[2048,5632]{1,0:T(8,128)(2,1)}) %all-gather.17.cloned.1.call-update) | async-done | bytes 23068688 | tf_op jit(solution)/shard_map/all_gather | solution.py:93
  1697.8 12.3 fusion.75
  1710.1 430.3 %all-gather.21.cloned.1.call-done = bf16[5632,2048]{1,0:T(8,128)(2,1)} async-done(((bf16[704,2048]{1,0:T(8,128)(2,1)}), bf16[5632,2048]{1,0:T(8,128)(2,1)}) %all-gather.21.cloned.1.call-update) | async-done | bytes 23068688 | tf_op jit(solution)/shard_map/all_gather | solution.py:95
  2140.5 15.2 multiply_convert_fusion.2
  2155.7 12.3 fusion.77
  2167.9 13.7 multiply_reduce_fusion
  2181.7 1.7 multiply_subtract_fusion
  2183.4 7.4 convolution_convert_fusion.5
  2190.8 2.0 copy.40
  2192.9 1.5 multiply_reduce_fusion.1
  2194.4 7.9 fusion.22
  2202.3 5.8 multiply_convert_fusion.1
  2208.1 2.0 copy-done.4
  2210.2 3.3 multiply_convert_fusion
  2213.4 7.7 pad_maximum_fusion
  2221.1 12.0 copy.48
  2233.2 6.6 convolution_convert_fusion.4
  2239.8 1.0 copy-done.15
  2240.8 12.4 convolution_convert_fusion
  2253.3 12.6 convolution_convert_fusion.1
  2265.9 12.5 convolution_convert_fusion.2
  2278.5 4.8 fusion.27
  2283.3 99.0 %reduce-scatter.22.cloned.1.call-done = bf16[128,4096]{1,0:T(8,128)(2,1)} async-done(((bf16[1024,4096]{1,0:T(8,128)(2,1)}), bf16[128,4096]{1,0:T(8,128)(2,1)}) %reduce-scatter.22.cloned.1.call-update) | async-done | bytes 1048592
  2382.3 2.1 slice.70
  2384.4 2.5 copy.53
  2386.9 1.1 slice.73
  2388.0 1.0 copy.52
  2389.0 1.5 multiply_add_fusion.1
  2390.6 1.2 maximum_convert_fusion
  2391.8 12.0 convolution_convert_fusion.3
  2404.6 14.8 fusion.43
  2419.4 1.1 copy.50
  2420.6 113.8 %reduce-scatter.14.cloned.1.call-done = bf16[256,2048]{1,0:T(8,128)(2,1)} async-done(((bf16[2048,2048]{1,0:T(8,128)(2,1)}), bf16[256,2048]{1,0:T(8,128)(2,1)}) %reduce-scatter.14.cloned.1.call-update) | async-done | bytes 1048592 | tf_op jit(solution)/shard_map/reduce_scatter | solution.py:74
  2534.4 375.8 %reduce-scatter.20.cloned.1.call-done = bf16[704,2048]{1,0:T(8,128)(2,1)} async-done(((bf16[5632,2048]{1,0:T(8,128)(2,1)}), bf16[704,2048]{1,0:T(8,128)(2,1)}) %reduce-scatter.20.cloned.1.call-update) | async-done | bytes 2883600 | tf_op jit(solution)/shard_map/reduce_scatter | solution.py:74
  2910.1 376.6 %reduce-scatter.18.cloned.1.call-done = bf16[256,5632]{1,0:T(8,128)(2,1)} async-done(((bf16[2048,5632]{1,0:T(8,128)(2,1)}), bf16[256,5632]{1,0:T(8,128)(2,1)}) %reduce-scatter.18.cloned.1.call-update) | async-done | bytes 2883600 | tf_op jit(solution)/shard_map/reduce_scatter | solution.py:74
  3286.7 375.9 %reduce-scatter.16.cloned.1.call-done = bf16[256,5632]{1,0:T(8,128)(2,1)} async-done(((bf16[2048,5632]{1,0:T(8,128)(2,1)}), bf16[256,5632]{1,0:T(8,128)(2,1)}) %reduce-scatter.16.cloned.1.call-update) | async-done | bytes 2883600 | tf_op jit(solution)/shard_map/reduce_scatter | solution.py:74
  3662.6 406.9 %reduce-scatter.12.cloned.1.call-done = bf16[256,6144]{1,0:T(8,128)(2,1)} async-done(((bf16[2048,6144]{1,0:T(8,128)(2,1)}), bf16[256,6144]{1,0:T(8,128)(2,1)}) %reduce-scatter.12.cloned.1.call-update) | async-done | bytes 3145744 | tf_op jit(solution)/shard_map/reduce_scatter | solution.py:74
  4069.7 12.1 fusion.26
  4081.8 1.1 fusion.51
  4082.9 49.6 %reduce-scatter.24.cloned.1.call-done = bf16[256,2]{1,0:T(8,128)(2,1)} async-done(((bf16[2048,2]{1,0:T(8,128)(2,1)}), bf16[256,2]{1,0:T(8,128)(2,1)}) %reduce-scatter.24.cloned.1.call-update) | async-done | bytes 1040
  4133.4 7.6 psum.42
  4141.6 221.1 %all-reduce.3.cloned.1.call-done = (bf16[256,6144]{1,0:T(8,128)(2,1)}, bf16[256,2048]{1,0:T(8,128)(2,1)}, bf16[256,5632]{1,0:T(8,128)(2,1)}, bf16[256,5632]{1,0:T(8,128)(2,1)}, bf16[704,2048]{1,0:T(8,128)(2,1)}) async-done(((bf16[256,6144]{1,0:T(8,128)(2,1)}, bf16[256,2048]{1,0:T(8,128)(2,1)}, bf16[256,5632]{1,0:T(8,128)(2,1)}, bf16[256,5632]{1,0:T(8,128)(2,1)}, bf16[704,2048]{1,0:T(8,128)(2,1)}), ...) | async-done | bytes 12845072 | tf_op jit(solution)/shard_map/psum | solution.py:80
  4362.7 2.9 convert_element_type.174
  4365.7 5.3 convert_element_type.172
  4371.0 3.2 convert_element_type.176
  4374.2 3.2 convert_element_type.178
  4377.4 3.3 convert_element_type.180
  (120 shorter events, 12.0 us)
Async XLA Ops:
  7.2 485.0 %all-gather.11.cloned.1.call-start = ((), (), s32[]{:S(2)}) async-start(), calls=%async_computation.7 | async-start | bytes 28311552 | tf_op jit(solution)/shard_map/all_gather | solution.py:90
  7.9 605.3 %all-gather.13.cloned.1.call-start = ((), (), s32[]{:S(2)}) async-start(), calls=%async_computation.8 | async-start | bytes 4718592 | tf_op jit(solution)/shard_map/all_gather | solution.py:120
  27.3 497.1 %copy-start.16 = (f32[8,1,256]{2,1,0:T(1,128)}, f32[8,1,256]{2,1,0:T(1,128)S(1)}, u32[]{:S(2)}) copy-start(f32[8,1,256]{2,1,0:T(1,128)S(1)} %convert_element_type.182) | copy-start | bytes 24580
  30.7 493.8 %copy-start.22 = (f32[128]{0:T(128)}, f32[128]{0:T(128)S(1)}, u32[]{:S(2)}) copy-start(f32[128]{0:T(128)S(1)} %get-tuple-element.42) | copy-start | bytes 1540
  30.9 505.7 %copy-start.18 = (f32[128,64]{0,1:T(8,128)}, f32[128,64]{0,1:T(8,128)S(1)}, u32[]{:S(2)}) copy-start(f32[128,64]{0,1:T(8,128)S(1)} %get-tuple-element.39) | copy-start | bytes 98308
  30.9 505.7 %copy-start.20 = (f32[128,64]{0,1:T(8,128)}, f32[128,64]{0,1:T(8,128)S(1)}, u32[]{:S(2)}) copy-start(f32[128,64]{0,1:T(8,128)S(1)} %get-tuple-element.40) | copy-start | bytes 98308
  538.4 3.5 copy-start.30
  538.4 150.6 %all-gather.23.cloned.1.call-start = ((), (), s32[]{:S(2)}) async-start(), calls=%async_computation.18 | async-start | bytes 4718592 | tf_op jit(solution)/shard_map/all_gather | solution.py:121
  539.4 73.8 %copy-start.12 = (bf16[128,16,64]{0,2,1:T(8,128)(2,1)S(1)}, bf16[128,16,64]{0,2,1:T(8,128)(2,1)}, u32[]{:S(2)}) copy-start(bf16[128,16,64]{0,2,1:T(8,128)(2,1)} %get-tuple-element.30) | copy-start | bytes 786436
  539.4 274.8 %all-gather.15.cloned.1.call-start = ((), (), s32[]{:S(2)}) async-start(), calls=%async_computation.9 | async-start | bytes 9437184 | tf_op jit(solution)/shard_map/all_gather | solution.py:91
  540.0 715.3 %all-gather.19.cloned.1.call-start = ((), (), s32[]{:S(2)}) async-start(), calls=%async_computation.11 | async-start | bytes 25952256 | tf_op jit(solution)/shard_map/all_gather | solution.py:94
  540.6 1157.2 %all-gather.17.cloned.1.call-start = ((), (), s32[]{:S(2)}) async-start(), calls=%async_computation.10 | async-start | bytes 25952256 | tf_op jit(solution)/shard_map/all_gather | solution.py:93
  541.1 1599.3 %all-gather.21.cloned.1.call-start = ((), (), s32[]{:S(2)}) async-start(), calls=%async_computation.12 | async-start | bytes 25952256 | tf_op jit(solution)/shard_map/all_gather | solution.py:95
  541.9 1840.4 %reduce-scatter.22.cloned.1.call-start = ((), (), s32[]{:S(2)}) async-start(), calls=%async_computation.19 | async-start | bytes 9437184
  617.3 3.3 copy-start
  689.1 125.1 %copy-start.1 = (bf16[1,128,2048]{2,1,0:T(8,128)(2,1)S(1)}, bf16[1,128,2048]{2,1,0:T(8,128)(2,1)}, u32[]{:S(2)}) copy-start(bf16[1,128,2048]{2,1,0:T(8,128)(2,1)} %param.10) | copy-start | bytes 1572868
  697.2 121.7 %copy-start.6 = (bf16[128,16,128]{0,2,1:T(8,128)(2,1)}, bf16[128,16,128]{0,2,1:T(8,128)(2,1)S(1)}, u32[]{:S(2)}) copy-start(bf16[128,16,128]{0,2,1:T(8,128)(2,1)S(1)} %get-tuple-element.47) | copy-start | bytes 1572868
  819.5 448.1 %copy-start.25 = (f32[128]{0:T(128)}, f32[128]{0:T(128)S(1)}, u32[]{:S(2)}) copy-start(f32[128]{0:T(128)S(1)} %get-tuple-element.44) | copy-start | bytes 1540
  1267.6 872.8 %copy-start.14 = (bf16[1,128,2048]{2,1,0:T(8,128)(2,1)S(1)}, bf16[1,128,2048]{2,1,0:T(8,128)(2,1)}, u32[]{:S(2)}) copy-start(bf16[1,128,2048]{2,1,0:T(8,128)(2,1)} %param.19) | copy-start | bytes 1572868
  2155.6 12.3 copy-start.5
  2155.6 12.3 copy-start.26
  2167.9 13.7 copy-start.28
  2183.4 49.8 %copy-start.2 = (f32[128,2048]{1,0:T(8,128)}, f32[128,2048]{1,0:T(8,128)S(1)}, u32[]{:S(2)}) copy-start(f32[128,2048]{1,0:T(8,128)S(1)} %multiply_subtract_fusion) | copy-start | bytes 3145732
  2194.3 7.9 copy-start.7
  2194.4 7.9 copy-start.29
  2202.3 7.9 copy-start.13
  2208.1 2.0 copy-start.4
  2233.1 301.3 %reduce-scatter.14.cloned.1.call-start = ((), (), s32[]{:S(2)}) async-start(), calls=%async_computation.14 | async-start | bytes 9437184 | tf_op jit(solution)/shard_map/reduce_scatter | solution.py:74
  2239.8 1.1 copy-start.15
  2239.8 670.3 %reduce-scatter.20.cloned.1.call-start = ((), (), s32[]{:S(2)}) async-start(), calls=%async_computation.17 | async-start | bytes 25952256 | tf_op jit(solution)/shard_map/reduce_scatter | solution.py:74
  2253.2 1033.5 %reduce-scatter.18.cloned.1.call-start = ((), (), s32[]{:S(2)}) async-start(), calls=%async_computation.16 | async-start | bytes 25952256 | tf_op jit(solution)/shard_map/reduce_scatter | solution.py:74
  2265.9 1396.8 %reduce-scatter.16.cloned.1.call-start = ((), (), s32[]{:S(2)}) async-start(), calls=%async_computation.15 | async-start | bytes 25952256 | tf_op jit(solution)/shard_map/reduce_scatter | solution.py:74
  2278.4 110.6 %copy-start.19 = (f32[128,64]{0,1:T(8,128)S(1)}, f32[128,64]{0,1:T(8,128)}, u32[]{:S(2)}) copy-start(f32[128,64]{0,1:T(8,128)} %copy-done.18) | copy-start | bytes 98308
  2278.4 110.6 %copy-start.21 = (f32[128,64]{0,1:T(8,128)S(1)}, f32[128,64]{0,1:T(8,128)}, u32[]{:S(2)}) copy-start(f32[128,64]{0,1:T(8,128)} %copy-done.20) | copy-start | bytes 98308
  2278.4 1791.1 %reduce-scatter.12.cloned.1.call-start = ((), (), s32[]{:S(2)}) async-start(), calls=%async_computation.13 | async-start | bytes 28311552 | tf_op jit(solution)/shard_map/reduce_scatter | solution.py:74
  2386.9 4.9 copy-start.17
  2386.9 4.9 copy-start.23
  2403.9 0.7 copy-start.24
  2403.9 1728.6 %reduce-scatter.24.cloned.1.call-start = ((), (), s32[]{:S(2)}) async-start(), calls=%async_computation.20 | async-start | bytes 589824
  2420.5 1942.2 %all-reduce.3.cloned.1.call-start = ((), (), s32[]{:S(2)}) async-start(), calls=%async_computation.21 | async-start | bytes 25690112 | tf_op jit(solution)/shard_map/psum | solution.py:80
  4069.6 12.1 copy-start.3
  4069.6 12.1 copy-start.8
  4069.6 12.1 copy-start.27
  4362.7 8.3 copy-start.11
  4371.0 3.2 copy-start.10
  4374.2 3.2 copy-start.9
Sparse Core Ops, SparseCore 0:
  9.5 482.6 all-gather.10
  538.5 74.6 all-gather.12
  615.8 73.1 all-gather.22
  691.0 123.1 all-gather.14
  815.6 439.6 all-gather.18
  1256.7 441.0 all-gather.16
  1699.3 441.0 all-gather.20
  2233.2 149.0 reduce-scatter.21
  2386.4 147.9 reduce-scatter.13
  2538.1 371.9 reduce-scatter.19
  2914.0 372.6 reduce-scatter.17
  3290.5 372.1 reduce-scatter.15
  3666.5 403.0 reduce-scatter.11
  4073.4 59.0 reduce-scatter.23
  4135.6 227.0 all-reduce.2
where the time goes:
time: 4400 us; the launch traced here: 4390 us
  waiting for transfers between devices  4020 us (91%)
  matrix products  207 us (5%)
  local copies, waits for them, and re-layouts  64.3 us (1%)
    reduce_scatter x5, waiting for transfers between devices, shard_grad(): lax.psum_scatter(term_fn(jnp.int32(0), shard_rows * lax.axis_size('blk'))...  1650 us
    all_gather x1, waiting for transfers between devices, per_device(): lax.all_gather(shards[1], 'blk', axis=0, tiled=True)  461 us
    all_gather x1, waiting for transfers between devices, per_device(): lax.all_gather(shards[5], 'blk', axis=0, tiled=True)  436 us
    all_gather x1, waiting for transfers between devices, per_device(): lax.all_gather(shards[6], 'blk', axis=0, tiled=True)  430 us
    all_gather x1, waiting for transfers between devices, per_device(): lax.all_gather(shards[4], 'blk', axis=0, tiled=True)  430 us
    psum x1, waiting for transfers between devices, shard_grad(): return lax.psum(shared, 'grp').astype(jnp.float32)  221 us
    unnamed x17, waiting for transfers between devices  152 us
    all_gather x1, waiting for transfers between devices, per_device(): lax.all_gather(shards[2], 'blk', axis=0, tiled=True)  117 us
  transfers between devices with their start and end apart: 15, of which 15 were waited for; matrix products, arithmetic and copies ran while one was open for 3% of the time, Pallas kernels for 0%

commit v1 on v0

--- a/solution.py
+++ b/solution.py
@@ -80,7 +80,7 @@
     return lax.psum(shared, "grp").astype(jnp.float32)
 
 
-def per_device(block_input, doc_lens, norm_attn, w_qkv, w_out, norm_mlp, w_gate, w_up, w_down, cot):
+def per_device_gather(block_input, doc_lens, norm_attn, w_qkv, w_out, norm_mlp, w_gate, w_up, w_down, cot):
     tok_rows = block_input.shape[1]
     width = block_input.shape[2]
     score_scale = HEAD ** (-0.5)
@@ -259,9 +259,178 @@
     )
 
 
+def split_columns(shard, parts):
+    rows, columns = shard.shape
+    n = lax.axis_size("blk")
+    cut = shard.reshape(rows, parts, n, columns // (parts * n)).transpose(2, 0, 1, 3)
+    mixed = lax.all_to_all(cut, "blk", split_axis=0, concat_axis=0, tiled=True)
+    return mixed.reshape(n * rows, columns // n)
+
+
+def merge_columns(grad, parts):
+    rows, columns = grad.shape
+    n = lax.axis_size("blk")
+    cut = grad.reshape(n, rows // n, columns)
+    mixed = lax.all_to_all(cut, "blk", split_axis=0, concat_axis=0, tiled=True)
+    mixed = mixed.reshape(n, rows // n, parts, columns // parts).transpose(1, 2, 0, 3)
+    return mixed.reshape(rows // n, columns * n)
+
+
+def gather_rows(block):
+    return lax.all_gather(block, "blk", axis=0, tiled=True)
+
+
+def scatter_rows(partial):
+    return lax.psum_scatter(
+        partial.astype(jnp.bfloat16), "blk", scatter_dimension=0, tiled=True
+    ).astype(jnp.float32)
+
+
+def dot_f32(left, right):
+    return jnp.dot(left, right, preferred_element_type=jnp.float32)
+
+
+def dot_t(left, right):
+    return lax.dot_general(
+        left, right, (((0,), (0,)), ((), ())), preferred_element_type=jnp.float32
+    )
+
+
+def per_device(block_input, doc_lens, norm_attn, w_qkv, w_out, norm_mlp, w_gate, w_up, w_down, cot):
+    n = lax.axis_size("blk")
+    tok_rows, width = block_input.shape[1:]
+    seq = tok_rows * n
+    heads = HEADS // n
+    score_scale = HEAD ** (-0.5)
+    gain_one = gather_rows(norm_attn).astype(jnp.float32)
+    gain_two = gather_rows(norm_mlp).astype(jnp.float32)
+    qkv_columns = split_columns(w_qkv, 3)
+    places = jnp.arange(seq, dtype=jnp.int32)
+    lengths = doc_lens[0]
+    starts = jnp.cumsum(lengths) - lengths
+    segment = segment_of(places, starts)
+    cosine, sine_part = angle_tables(places - start_of(places, starts))
+    allowed = (segment[:, None] == segment[None, :]) & (places[None, :] <= places[:, None])
+
+    def normed(values, gain):
+        inv = lax.rsqrt(jnp.mean(values * values, axis=-1, keepdims=True) + EPS)
+        return inv, (values * inv * gain).astype(jnp.bfloat16)
+
+    x_float = block_input[0].astype(jnp.float32)
+    inv_one, normed_own = normed(x_float, gain_one)
+    normed_one = gather_rows(normed_own)
+    gate_columns = split_columns(w_gate, 1)
+    up_columns = split_columns(w_up, 1)
+    seed = gather_rows(cot[0])
+    projected = dot_f32(normed_one, qkv_columns).reshape(seq, 3, heads, HEAD)
+    queries = rotate(projected[:, 0], cosine, sine_part).astype(jnp.bfloat16)
+    keys = rotate(projected[:, 1], cosine, sine_part).astype(jnp.bfloat16)
+    values = projected[:, 2].astype(jnp.bfloat16)
+    scores = (
+        jnp.einsum("qhd,khd->hqk", queries, keys, preferred_element_type=jnp.float32) * score_scale
+    )
+    scores = jnp.where(allowed[None], scores, NEGATIVE)
+    peak = jnp.max(scores, axis=-1)
+    raw = jnp.exp(scores - peak[..., None])
+    total = jnp.sum(raw, axis=-1)
+    attended = jnp.einsum(
+        "hqk,khd->hqd", raw.astype(jnp.bfloat16), values, preferred_element_type=jnp.float32
+    )
+    log_total = peak + jnp.log(total)
+    attended = (attended / total[..., None]).transpose(1, 0, 2)
+    attended_b = attended.reshape(seq, heads * HEAD).astype(jnp.bfloat16)
+    resid = x_float + scatter_rows(dot_f32(attended_b, w_out))
+    inv_two, normed_own = normed(resid, gain_two)
+    normed_two = gather_rows(normed_own)
+    gate_proj = dot_f32(normed_two, gate_columns)
+    up_proj = dot_f32(normed_two, up_columns)
+    sigmoid_gate = jax.nn.sigmoid(gate_proj)
+    swish = gate_proj * sigmoid_gate
+    hidden = (swish * up_proj).astype(jnp.bfloat16)
+    dhidden = contract_rows(seed, w_down)
+    dgate = (dhidden * up_proj * sigmoid_gate * (1.0 + gate_proj * (1.0 - sigmoid_gate))).astype(
+        jnp.bfloat16
+    )
+    dup = (dhidden * swish).astype(jnp.bfloat16)
+    dnormed_two = scatter_rows(contract_rows(dgate, gate_columns) + contract_rows(dup, up_columns))
+    a_two = dnormed_two * gain_two
+    dresid = (
+        cot[0].astype(jnp.float32)
+        + inv_two * a_two
+        - resid * inv_two**3 * jnp.mean(a_two * resid, axis=-1, keepdims=True)
+    )
+    dresid_b = gather_rows(dresid.astype(jnp.bfloat16))
+    block_out = (resid + scatter_rows(dot_f32(hidden, w_down))).astype(jnp.bfloat16)
+    grad_down = lax.psum(dot_t(hidden, seed).astype(jnp.bfloat16), "grp").astype(jnp.float32)
+    grad_gate = lax.psum(
+        merge_columns(dot_t(normed_two, dgate).astype(jnp.bfloat16), 1), "grp"
+    ).astype(jnp.float32)
+    grad_up = lax.psum(
+        merge_columns(dot_t(normed_two, dup).astype(jnp.bfloat16), 1), "grp"
+    ).astype(jnp.float32)
+    dattended = contract_rows(dresid_b, w_out).astype(jnp.bfloat16).reshape(seq, heads, HEAD)
+    grad_out = lax.psum(dot_t(attended_b, dresid_b).astype(jnp.bfloat16), "grp").astype(
+        jnp.float32
+    )
+    delta = jnp.sum(dattended.astype(jnp.float32) * attended, axis=-1).T
+    probs = jnp.exp(scores - log_total[..., None])
+    dprobs = jnp.einsum("qhd,khd->hqk", dattended, values, preferred_element_type=jnp.float32)
+    dscores = (probs * (dprobs - delta[..., None])).astype(jnp.bfloat16)
+    dquery = score_scale * jnp.einsum(
+        "hqk,khd->qhd", dscores, keys, preferred_element_type=jnp.float32
+    )
+    dkey = score_scale * jnp.einsum(
+        "hqk,qhd->khd", dscores, queries, preferred_element_type=jnp.float32
+    )
+    dvalue = jnp.einsum(
+        "hqk,qhd->khd", probs.astype(jnp.bfloat16), dattended, preferred_element_type=jnp.float32
+    )
+    dqkv = (
+        jnp.stack(
+            [unrotate(dquery, cosine, sine_part), unrotate(dkey, cosine, sine_part), dvalue], axis=1
+        )
+        .reshape(seq, 3 * heads * HEAD)
+        .astype(jnp.bfloat16)
+    )
+    dnormed_one = scatter_rows(contract_rows(dqkv, qkv_columns))
+    grad_qkv = lax.psum(
+        merge_columns(dot_t(normed_one, dqkv).astype(jnp.bfloat16), 3), "grp"
+    ).astype(jnp.float32)
+    a_one = dnormed_one * gain_one
+    x_grad = (
+        dresid
+        + inv_one * a_one
+        - x_float * inv_one**3 * jnp.mean(a_one * x_float, axis=-1, keepdims=True)
+    ).astype(jnp.bfloat16)
+    gain_terms = jnp.stack(
+        [
+            jnp.sum(dnormed_one * x_float * inv_one, axis=0),
+            jnp.sum(dnormed_two * resid * inv_two, axis=0),
+        ]
+    )
+    gain_grads = lax.psum(
+        lax.psum_scatter(gain_terms, "blk", scatter_dimension=1, tiled=True), "grp"
+    )
+    return (
+        block_out[None],
+        x_grad[None],
+        gain_grads[0],
+        grad_qkv,
+        grad_out,
+        gain_grads[1],
+        grad_gate,
+        grad_up,
+        grad_down,
+    )
+
+
+def body_for(mesh):
+    return per_device if HEADS % mesh.shape["blk"] == 0 else per_device_gather
+
+
 def solution(mesh):
     return jax.shard_map(
-        per_device,
+        body_for(mesh),
         mesh=mesh,
         in_specs=(
             P("grp", "blk", None),

time: 4400 us -> 1410 us (0.32)
  waiting for transfers between devices: 4020 us -> 1100 us
  matrix products: 207 us -> 105 us
    all_gather x7 -> x4, waiting for transfers between devices: 2000 us -> 72 us  [gather_rows(): return lax.all_gather(block, 'blk', axis=0, tiled=True)]
    reduce_scatter x5 -> x4, waiting for transfers between devices: 1650 us -> 189 us  [scatter_rows(): lax.psum_scatter(partial.astype(jnp.bfloat16), 'blk', scatter_dimension=0...]
    all_to_all x0 -> x6, waiting for transfers between devices: none -> 549 us  [the longest x3 327 us: split_columns(): mixed = lax.all_to_all(cut, 'blk', split_axis=0, concat_axis=0, tiled=True)]
    unnamed x17 -> x11, waiting for transfers between devices: 152 us -> 62.5 us
    dot_general x14, matrix products: 132 us -> 71.2 us  [the longest x5 31.7 us: dot_t(): lax.dot_general(left, right, (((0,), (0,)), ((), ())), preferred_element_...]
  transfers between devices with their start and end apart: 15 -> 16, of which waited for: 15 -> 12; matrix products, arithmetic and copies ran while one was open for 3% -> 8% of each run, Pallas kernels for 0% -> 0%
where the time goes in v1:
time: 1410 us; the launch traced here: 1390 us
  waiting for transfers between devices  1100 us (78%)
  matrix products  105 us (7%)
  local copies, waits for them, and re-layouts  73.4 us (5%)
  blocking collectives  42.4 us (3%)
  starting transfers between devices  31.6 us (2%)
  other arithmetic  30.2 us (2%)
  between operations  15.1 us (1%)
    all_to_all x3, waiting for transfers between devices, split_columns(): mixed = lax.all_to_all(cut, 'blk', split_axis=0, concat_axis=0, tiled=True)  327 us
    psum x1, waiting for transfers between devices, per_device(): lax.psum(merge_columns(dot_t(normed_one, dqkv).astype(jnp.bfloat16), 3),...  222 us
    all_to_all x3, waiting for transfers between devices, merge_columns(): mixed = lax.all_to_all(cut, 'blk', split_axis=0, concat_axis=0, tiled=True)  222 us
    reduce_scatter x4, waiting for transfers between devices, scatter_rows(): lax.psum_scatter(partial.astype(jnp.bfloat16), 'blk', scatter_dimension=0...  189 us
    all_gather x4, waiting for transfers between devices, gather_rows(): return lax.all_gather(block, 'blk', axis=0, tiled=True)  72 us
    unnamed x11, waiting for transfers between devices  62.5 us
    unnamed x79, local copies, waits for them, and re-layouts  51.2 us
    all_gather x2, blocking collectives, gather_rows(): return lax.all_gather(block, 'blk', axis=0, tiled=True)  35.1 us
  transfers between devices with their start and end apart: 16, of which 12 were waited for; matrix products, arithmetic and copies ran while one was open for 8% of the time, Pallas kernels for 0%

profile of v1, /device:TPU:1, one launch (start us, length us, event | category | flops | bytes accessed | tf_op | source)
XLA Modules:
  0.0 1393.3 jit_solution(241510089393555077)
XLA Ops:
  9.8 17.9 %all-gather.1 = bf16[8,1,256]{2,1,0:T(2,128)(2,1)S(1)} all-gather(bf16[1,1,256]{2,1,0:T(2,128)(2,1)S(1)} %reshape.259), channel_id=1, replica_groups=mesh['grp'=4,'blk'=8] {'blk'}, dimensions={0}, use_global_device_ids=true | all-gather | bytes 4608 | tf_op jit(solution)/shard_map/all_gather | solution.py:280
  27.7 2.0 fusion.42
  29.7 4.6 copy.145
  34.4 4.6 copy.146
  39.0 4.6 all-to-all-start
  45.0 1.6 fusion.14
  46.6 111.7 %all-to-all-done = bf16[8,256,3,256]{3,1,2,0:T(8,128)(2,1)} async-done(((bf16[8,256,3,256]{3,1,2,0:T(8,128)(2,1)}), bf16[8,256,3,256]{3,1,2,0:T(8,128)(2,1)}, u32[]{:S(2)}, u32[]{:S(2)}) %all-to-all-start) | async-done | bytes 3145760 | tf_op jit(solution)/shard_map/all_to_all | solution.py:266
  158.3 4.8 copy.147
  163.2 4.6 copy.184
  167.8 6.2 fusion.4
  176.0 2.0 fusion.3
  178.1 2.0 fusion
  181.4 3.6 fusion.65
  185.7 3.3 convolution_convert_fusion.1
  189.7 17.3 %all-gather.2 = bf16[8,1,256]{2,1,0:T(2,128)(2,1)S(1)} all-gather(bf16[1,1,256]{2,1,0:T(2,128)(2,1)S(1)} %reshape.261), channel_id=1, replica_groups=mesh['grp'=4,'blk'=8] {'blk'}, dimensions={0}, use_global_device_ids=true | all-gather | bytes 4608 | tf_op jit(solution)/shard_map/all_gather | solution.py:280
  207.0 71.9 %reduce-scatter.8.cloned.1.call-done = bf16[128,2048]{1,0:T(8,128)(2,1)} async-done(((bf16[1024,2048]{1,0:T(8,128)(2,1)}), bf16[128,2048]{1,0:T(8,128)(2,1)}) %reduce-scatter.8.cloned.1.call-update) | async-done | bytes 524304 | tf_op jit(solution)/shard_map/reduce_scatter | solution.py:284
  280.2 2.0 multiply_convert_fusion.4
  282.2 4.5 copy.151
  286.8 4.5 all-to-all-start.1
  291.8 4.5 copy.154
  296.4 108.0 %all-to-all-done.1 = bf16[8,256,1,704]{1,3,2,0:T(8,128)(2,1)} async-done(((bf16[8,256,1,704]{1,3,2,0:T(8,128)(2,1)}), bf16[8,256,1,704]{1,3,2,0:T(8,128)(2,1)}, u32[]{:S(2)}, u32[]{:S(2)}) %all-to-all-start.1) | async-done | bytes 2883616 | tf_op jit(solution)/shard_map/all_to_all | solution.py:266
  404.4 4.4 all-to-all-start.2
  408.9 3.8 copy.185
  412.7 107.2 %all-to-all-done.2 = bf16[8,256,1,704]{1,3,2,0:T(8,128)(2,1)} async-done(((bf16[8,256,1,704]{1,3,2,0:T(8,128)(2,1)}), bf16[8,256,1,704]{1,3,2,0:T(8,128)(2,1)}, u32[]{:S(2)}, u32[]{:S(2)}) %all-to-all-start.2) | async-done | bytes 2883616 | tf_op jit(solution)/shard_map/all_to_all | solution.py:266
  519.9 3.8 copy.186
  523.7 8.0 fusion.67
  531.7 4.8 fusion.66
  536.5 8.4 multiply_convert_fusion.1
  545.0 3.5 fusion.68
  548.5 5.3 add_convert_fusion
  553.9 90.1 %reduce-scatter.12.cloned.1.call-done = bf16[128,2048]{1,0:T(8,128)(2,1)} async-done(((bf16[1024,2048]{1,0:T(8,128)(2,1)}), bf16[128,2048]{1,0:T(8,128)(2,1)}) %reduce-scatter.12.cloned.1.call-update) | async-done | bytes 524304 | tf_op jit(solution)/shard_map/reduce_scatter | solution.py:284
  644.0 1.6 fusion.39
  645.6 2.6 fusion.63
  648.3 72.0 %all-gather.12.cloned.1.call-done = bf16[1024,2048]{1,0:T(8,128)(2,1)} async-done(((bf16[128,2048]{1,0:T(8,128)(2,1)}), bf16[1024,2048]{1,0:T(8,128)(2,1)}) %all-gather.12.cloned.1.call-update) | async-done | bytes 4194320 | tf_op jit(solution)/shard_map/all_gather | solution.py:280
  720.3 4.2 multiply_reduce_fusion
  724.5 6.1 fusion.24
  730.7 4.5 multiply_convert_fusion
  740.6 5.0 convolution_convert_fusion.2
  745.6 5.8 convolution_convert_fusion.4
  751.4 1.8 copy.191
  753.2 4.4 all-to-all-start.5
  757.6 8.0 convolution_convert_fusion.3
  765.6 4.6 copy.163
  770.2 80.5 %all-to-all-done.5 = bf16[8,256,704]{1,2,0:T(8,128)(2,1)} async-done(((bf16[8,256,704]{1,2,0:T(8,128)(2,1)}), bf16[8,256,704]{1,2,0:T(8,128)(2,1)}, u32[]{:S(2)}, u32[]{:S(2)}) %all-to-all-start.5) | async-done | bytes 2883616 | tf_op jit(solution)/shard_map/all_to_all | solution.py:274
  850.7 4.7 all-to-all-start.3
  855.4 6.4 convolution_convert_fusion
  861.8 5.8 convolution_convert_fusion.5
  867.6 1.8 copy.192
  869.4 72.7 %all-to-all-done.3 = bf16[8,256,768]{1,2,0:T(8,128)(2,1)} async-done(((bf16[8,256,768]{1,2,0:T(8,128)(2,1)}), bf16[8,256,768]{1,2,0:T(8,128)(2,1)}, u32[]{:S(2)}, u32[]{:S(2)}) %all-to-all-start.3) | async-done | bytes 3145760 | tf_op jit(solution)/shard_map/all_to_all | solution.py:274
  942.1 8.3 all-to-all-start.4
  950.4 7.4 fusion.17
  960.7 4.7 convolution_convert_fusion.6
  965.4 3.9 copy.164
  969.3 68.9 %all-to-all-done.4 = bf16[8,256,704]{1,2,0:T(8,128)(2,1)} async-done(((bf16[8,256,704]{1,2,0:T(8,128)(2,1)}), bf16[8,256,704]{1,2,0:T(8,128)(2,1)}, u32[]{:S(2)}, u32[]{:S(2)}) %all-to-all-start.4) | async-done | bytes 2883616 | tf_op jit(solution)/shard_map/all_to_all | solution.py:274
  1038.2 27.5 %reduce-scatter.10.cloned.1.call-done = bf16[128,2048]{1,0:T(8,128)(2,1)} async-done(((bf16[1024,2048]{1,0:T(8,128)(2,1)}), bf16[128,2048]{1,0:T(8,128)(2,1)}) %reduce-scatter.10.cloned.1.call-update) | async-done | bytes 524304 | tf_op jit(solution)/shard_map/reduce_scatter | solution.py:284
  1065.7 3.5 fusion.52
  1069.3 62.2 %reduce-scatter.16.cloned.1.call-done = f32[256,2]{1,0:T(8,128)} async-done(((f32[2048,2]{1,0:T(8,128)}), f32[256,2]{1,0:T(8,128)}) %reduce-scatter.16.cloned.1.call-update) | async-done | bytes 2064
  1132.5 7.3 psum.42
  1140.3 222.2 %all-reduce.3.cloned.1.call-done = (bf16[256,6144]{0,1:T(8,128)(2,1)}, bf16[256,5632]{0,1:T(8,128)(2,1)}, bf16[256,5632]{0,1:T(8,128)(2,1)}, bf16[256,2048]{1,0:T(8,128)(2,1)}, bf16[704,2048]{1,0:T(8,128)(2,1)}) async-done(((bf16[256,6144]{0,1:T(8,128)(2,1)}, bf16[256,5632]{0,1:T(8,128)(2,1)}, bf16[256,5632]{0,1:T(8,128)(2,1)}, bf16[256,2048]{1,0:T(8,128)(2,1)}, bf16[704,2048]{1,0:T(8,128)(2,1)}), ...) | async-done | bytes 12845072 | tf_op jit(solution)/shard_map/psum | solution.py:396
  1362.5 2.8 convert_element_type.179
  1365.3 5.4 copy.167
  1370.7 5.1 copy.168
  1375.8 5.1 copy.169
  1381.0 5.1 convert_element_type.185
  (121 shorter events, 20.6 us)
Async XLA Ops:
  7.2 529.3 %copy-start = (bf16[704,2048]{1,0:T(8,128)(2,1)S(1)}, bf16[704,2048]{1,0:T(8,128)(2,1)}, u32[]{:S(2)}) copy-start(bf16[704,2048]{1,0:T(8,128)(2,1)} %param.18) | copy-start | bytes 8650756
  7.2 160.6 %all-gather.8.cloned.1.call-start = ((), (), s32[]{:S(2)}) async-start(), calls=%async_computation.11 | async-start | bytes 4718592 | tf_op jit(solution)/shard_map/all_gather | solution.py:280
  39.0 4.7 copy-start.27
  39.0 119.3 %all-to-all-start = ((bf16[8,256,3,256]{3,1,2,0:T(8,128)(2,1)}), bf16[8,256,3,256]{3,1,2,0:T(8,128)(2,1)}, u32[]{:S(2)}, u32[]{:S(2)}) async-start(bf16[8,256,3,256]{3,1,2,0:T(8,128)(2,1)} %copy.146), calls=%async_computation | async-start | bytes 6291456 | tf_op jit(solution)/shard_map/all_to_all | solution.py:266
  43.6 235.3 %reduce-scatter.8.cloned.1.call-start = ((), (), s32[]{:S(2)}) async-start(), calls=%async_computation.12 | async-start | bytes 4718592 | tf_op jit(solution)/shard_map/reduce_scatter | solution.py:284
  45.0 129.2 %copy-start.9 = (f32[1024,64]{0,1:T(8,128)}, f32[1024,64]{0,1:T(8,128)S(1)}, u32[]{:S(2)}) copy-start(f32[1024,64]{0,1:T(8,128)S(1)} %get-tuple-element.93) | copy-start | bytes 786436
  45.0 129.2 %copy-start.11 = (f32[1024,64]{0,1:T(8,128)}, f32[1024,64]{0,1:T(8,128)S(1)}, u32[]{:S(2)}) copy-start(f32[1024,64]{0,1:T(8,128)S(1)} %get-tuple-element.94) | copy-start | bytes 786436
  174.0 6.1 copy-start.14
  174.0 2.0 copy-start.3
  174.5 3.5 copy-start.16
  174.6 3.5 copy-start.18
  174.6 3.5 copy-start.20
  174.6 3.5 copy-start.22
  178.1 3.3 copy-start.2
  181.4 4.4 copy-start.24
  184.9 0.8 copy-start.15
  189.1 0.7 copy-start.28
  189.1 89.8 %copy-start.1 = (bf16[1,128,2048]{2,1,0:T(8,128)(2,1)S(1)}, bf16[1,128,2048]{2,1,0:T(8,128)(2,1)}, u32[]{:S(2)}) copy-start(bf16[1,128,2048]{2,1,0:T(8,128)(2,1)} %param.10) | copy-start | bytes 1572868
  189.1 334.6 %all-gather.10.cloned.1.call-start = ((), (), s32[]{:S(2)}) async-start(), calls=%async_computation.13 | async-start | bytes 4718592 | tf_op jit(solution)/shard_map/all_gather | solution.py:280
  286.8 117.6 %all-to-all-start.1 = ((bf16[8,256,1,704]{1,3,2,0:T(8,128)(2,1)}), bf16[8,256,1,704]{1,3,2,0:T(8,128)(2,1)}, u32[]{:S(2)}, u32[]{:S(2)}) async-start(bf16[8,256,1,704]{1,3,2,0:T(8,128)(2,1)} %bitcast.176), calls=%async_computation.2 | async-start | bytes 5767168 | tf_op jit(solution)/shard_map/all_to_all | solution.py:266
  291.3 245.2 %all-gather.14.cloned.1.call-start = ((), (), s32[]{:S(2)}) async-start(), calls=%async_computation.18 | async-start | bytes 4718592 | tf_op jit(solution)/shard_map/all_gather | solution.py:280
  404.4 115.5 %all-to-all-start.2 = ((bf16[8,256,1,704]{1,3,2,0:T(8,128)(2,1)}), bf16[8,256,1,704]{1,3,2,0:T(8,128)(2,1)}, u32[]{:S(2)}, u32[]{:S(2)}) async-start(bf16[8,256,1,704]{1,3,2,0:T(8,128)(2,1)} %bitcast.177), calls=%async_computation.3 | async-start | bytes 5767168 | tf_op jit(solution)/shard_map/all_to_all | solution.py:266
  408.8 235.2 %reduce-scatter.12.cloned.1.call-start = ((), (), s32[]{:S(2)}) async-start(), calls=%async_computation.15 | async-start | bytes 4718592 | tf_op jit(solution)/shard_map/reduce_scatter | solution.py:284
  523.7 8.0 copy-start.6
  523.7 8.0 copy-start.26
  536.5 8.4 copy-start.7
  544.9 3.6 copy-start.29
  544.9 3.6 copy-start.30
  544.9 3.6 copy-start.8
  553.9 166.4 %all-gather.12.cloned.1.call-start = ((), (), s32[]{:S(2)}) async-start(), calls=%async_computation.16 | async-start | bytes 4718592 | tf_op jit(solution)/shard_map/all_gather | solution.py:280
  648.2 309.6 %reduce-scatter.14.cloned.1.call-start = ((), (), s32[]{:S(2)}) async-start(), calls=%async_computation.17 | async-start | bytes 4718592 | tf_op jit(solution)/shard_map/reduce_scatter | solution.py:284
  720.3 4.2 copy-start.4
  720.3 10.4 slice-start
  724.5 6.1 slice-start.1
  730.6 4.5 copy-start.21
  730.7 4.5 copy-start.23
  735.1 1.6 copy-start.17
  735.2 1.6 copy-start.19
  736.7 1.0 copy-start.10
  736.7 1.0 copy-start.12
  738.1 2.5 copy-start.5
  738.4 1.1 copy-start.13
  753.2 97.5 %all-to-all-start.5 = ((bf16[8,256,704]{1,2,0:T(8,128)(2,1)}), bf16[8,256,704]{1,2,0:T(8,128)(2,1)}, u32[]{:S(2)}, u32[]{:S(2)}) async-start(bf16[8,256,704]{1,2,0:T(8,128)(2,1)} %bitcast.178), calls=%async_computation.9 | async-start | bytes 5767168 | tf_op jit(solution)/shard_map/all_to_all | solution.py:274
  850.7 91.4 %all-to-all-start.3 = ((bf16[8,256,768]{1,2,0:T(8,128)(2,1)}), bf16[8,256,768]{1,2,0:T(8,128)(2,1)}, u32[]{:S(2)}, u32[]{:S(2)}) async-start(bf16[8,256,768]{1,2,0:T(8,128)(2,1)} %copy.163), calls=%async_computation.7 | async-start | bytes 6291456 | tf_op jit(solution)/shard_map/all_to_all | solution.py:274
  855.4 210.4 %reduce-scatter.10.cloned.1.call-start = ((), (), s32[]{:S(2)}) async-start(), calls=%async_computation.14 | async-start | bytes 4718592 | tf_op jit(solution)/shard_map/reduce_scatter | solution.py:284
  942.1 96.1 %all-to-all-start.4 = ((bf16[8,256,704]{1,2,0:T(8,128)(2,1)}), bf16[8,256,704]{1,2,0:T(8,128)(2,1)}, u32[]{:S(2)}, u32[]{:S(2)}) async-start(bf16[8,256,704]{1,2,0:T(8,128)(2,1)} %bitcast.175), calls=%async_computation.8 | async-start | bytes 5767168 | tf_op jit(solution)/shard_map/all_to_all | solution.py:274
  950.3 181.1 %reduce-scatter.16.cloned.1.call-start = ((), (), s32[]{:S(2)}) async-start(), calls=%async_computation.19 | async-start | bytes 1179648
  960.6 401.9 %all-reduce.3.cloned.1.call-start = ((), (), s32[]{:S(2)}) async-start(), calls=%async_computation.20 | async-start | bytes 25690112 | tf_op jit(solution)/shard_map/psum | solution.py:396
  1038.2 27.5 %copy-start.25 = (f32[128]{0:T(128)S(1)}, f32[128]{0:T(128)}, u32[]{:S(2)}) copy-start(f32[128]{0:T(128)} %get-tuple-element.97) | copy-start | bytes 1540
Sparse Core Ops, SparseCore 0:
  29.9 131.9 all-gather.7
  189.2 89.6 reduce-scatter.7
  282.4 126.4 all-gather.9
  411.0 117.2 all-gather.13
  554.0 89.9 reduce-scatter.11
  648.3 71.8 all-gather.11
  745.7 156.7 reduce-scatter.13
  907.2 158.4 reduce-scatter.9
  1069.7 61.7 reduce-scatter.15
  1135.8 226.7 all-reduce.2

commit v2 on v1

--- a/solution.py
+++ b/solution.py
@@ -1,8 +1,11 @@
+import functools
 import math
 
 import jax
 import jax.numpy as jnp
 from jax import lax
+from jax.experimental import pallas as pl
+from jax.experimental.pallas import tpu as pltpu
 from jax.sharding import PartitionSpec as P
 
 HEADS = 16
@@ -259,31 +262,366 @@
     )
 
 
-def split_columns(shard, parts):
-    rows, columns = shard.shape
+MESH = pl.DeviceIdType.MESH
+VMEM_BYTES = 56 * 2**20
+
+
+def ring_place(block, n):
+    up, row = block // 2, block % 2
+    return (1 - row) * up + row * (n - 1 - up)
+
+
+def ring_block(place, n):
+    back = place // (n // 2)
+    return (1 - back) * 2 * place + back * (2 * (n - 1 - place) + 1)
+
+
+def at_offset(place, offset, n):
+    return ring_block((place + offset + n) % n, n)
+
+
+def greet(devices):
+    barrier = pltpu.get_barrier_semaphore()
+    for device in devices:
+        pl.semaphore_signal(barrier, inc=1, device_id=device, device_id_type=MESH)
+    pl.semaphore_wait(barrier, len(devices))
+
+
+def push(src, dst, send_sem, recv_sem, device):
+    return pltpu.make_async_remote_copy(
+        src_ref=src,
+        dst_ref=dst,
+        send_sem=send_sem,
+        recv_sem=recv_sem,
+        device_id=device,
+        device_id_type=MESH,
+    )
+
+
+def kernel_params(collective_id):
+    return pltpu.CompilerParams(
+        collective_id=collective_id, has_side_effects=True, vmem_limit_bytes=VMEM_BYTES
+    )
+
+
+def gather_kernel(n, x_ref, o_ref, local_sem, send, recv):
+    grp, me = lax.axis_index("grp"), lax.axis_index("blk")
+    place = ring_place(me, n)
+    ends = ((grp, at_offset(place, 1, n)), (grp, at_offset(place, -1, n)))
+    greet(ends)
+    rows = x_ref.shape[0]
+    half = rows // 2
+    own = pltpu.make_async_copy(x_ref, o_ref.at[me], local_sem)
+    own.start()
+    copies = {}
+    for step in range(n // 2):
+        for chunk in range(2):
+            for way in range(2):
+                if step == n // 2 - 1 and chunk != way:
+                    continue
+                block = at_offset(place, step if way else -step, n)
+                part = pl.ds(chunk * half, half)
+                if step:
+                    copies[step - 1, chunk, way].wait_recv()
+                copy = push(
+                    x_ref.at[part] if step == 0 else o_ref.at[block, part],
+                    o_ref.at[block, part],
+                    send.at[step, chunk, way],
+                    recv.at[step, chunk, way],
+                    ends[way],
+                )
+                copy.start()
+                copies[step, chunk, way] = copy
+    for (step, chunk, way), copy in copies.items():
+        if (step + 1, chunk, way) not in copies:
+            copy.wait_recv()
+    for copy in copies.values():
+        copy.wait_send()
+    own.wait()
+
+
+def ring_gather(block):
     n = lax.axis_size("blk")
-    cut = shard.reshape(rows, parts, n, columns // (parts * n)).transpose(2, 0, 1, 3)
-    mixed = lax.all_to_all(cut, "blk", split_axis=0, concat_axis=0, tiled=True)
-    return mixed.reshape(n * rows, columns // n)
-
-
-def merge_columns(grad, parts):
-    rows, columns = grad.shape
+    rows, columns = block.shape
+    return pl.pallas_call(
+        functools.partial(gather_kernel, n),
+        out_shape=jax.ShapeDtypeStruct((n, rows, columns), block.dtype),
+        in_specs=[pl.BlockSpec(memory_space=pl.ANY)],
+        out_specs=pl.BlockSpec(memory_space=pl.ANY),
+        scratch_shapes=[pltpu.SemaphoreType.DMA]
+        + [pltpu.SemaphoreType.DMA((n // 2, 2, 2))] * 2,
+        compiler_params=kernel_params(0),
+        name="ring_gather",
+    )(block).reshape(n * rows, columns)
+
+
+def scatter_kernel(n, p_ref, o_ref, held, send, recv):
+    grp, me = lax.axis_index("grp"), lax.axis_index("blk")
+    place = ring_place(me, n)
+    ends = ((grp, at_offset(place, 1, n)), (grp, at_offset(place, -1, n)))
+    greet(ends)
+    rows, columns = o_ref.shape
+    half, wide = rows // 2, columns // 2
+    copies = {}
+    for step in range(n):
+        for chunk in range(2):
+            for way in range(2):
+                part = pl.ds(chunk * half, half)
+                lanes = pl.ds(way * wide, wide)
+                offset = (step + 1) if way else -(step + 1)
+                block = at_offset(place, offset, n)
+                if step:
+                    copies[step - 1, chunk, way].wait_recv()
+                    total = held[way, step - 1, part].astype(jnp.float32) + p_ref[
+                        block, part, lanes
+                    ].astype(jnp.float32)
+                    if step == n - 1:
+                        o_ref[part, lanes] = total
+                        continue
+                    held[way, step - 1, part] = total.astype(jnp.bfloat16)
+                copy = push(
+                    held.at[way, step - 1, part] if step else p_ref.at[block, part, lanes],
+                    held.at[way, step, part],
+                    send.at[step, chunk, way],
+                    recv.at[step, chunk, way],
+                    ends[way],
+                )
+                copy.start()
+                copies[step, chunk, way] = copy
+    for copy in copies.values():
+        copy.wait_send()
+
+
+def ring_scatter(partial):
     n = lax.axis_size("blk")
-    cut = grad.reshape(n, rows // n, columns)
-    mixed = lax.all_to_all(cut, "blk", split_axis=0, concat_axis=0, tiled=True)
-    mixed = mixed.reshape(n, rows // n, parts, columns // parts).transpose(1, 2, 0, 3)
-    return mixed.reshape(rows // n, columns * n)
-
-
-def gather_rows(block):
-    return lax.all_gather(block, "blk", axis=0, tiled=True)
-
-
-def scatter_rows(partial):
-    return lax.psum_scatter(
-        partial.astype(jnp.bfloat16), "blk", scatter_dimension=0, tiled=True
-    ).astype(jnp.float32)
+    rows, columns = partial.shape
+    rows //= n
+    return pl.pallas_call(
+        functools.partial(scatter_kernel, n),
+        out_shape=jax.ShapeDtypeStruct((rows, columns), jnp.float32),
+        in_specs=[pl.BlockSpec(memory_space=pltpu.VMEM)],
+        out_specs=pl.BlockSpec(memory_space=pltpu.VMEM),
+        scratch_shapes=[pltpu.VMEM((2, n - 1, rows, columns // 2), jnp.bfloat16)]
+        + [pltpu.SemaphoreType.DMA((n - 1, 2, 2))] * 2,
+        compiler_params=kernel_params(1),
+        name="ring_scatter",
+    )(partial.astype(jnp.bfloat16).reshape(n, rows, columns))
+
+
+def team(grp):
+    over, core = grp // 2, grp % 2
+    return over, core, (1 - over) * 2 + core, over * 2 + 1 - core
+
+
+def spread_pieces(n, slab_of, out, near, sems):
+    s_blk, r_blk, s_x, r_x, s_c, r_c = sems
+    grp, me = lax.axis_index("grp"), lax.axis_index("blk")
+    over, core, grp_x, grp_c = team(grp)
+    sent = []
+    arriving = {}
+    for k in range(1, n):
+        to = (me + k) % n
+        copy = push(slab_of(to), out.at[core, over, me], s_blk.at[k], r_blk.at[k], (grp, to))
+        copy.start()
+        sent.append(copy)
+        arriving[k] = copy
+    near.wait()
+    from_x, from_c, far = {}, {}, {}
+    for k in range(n):
+        source = (me - k + n) % n
+        if k:
+            arriving[k].wait_recv()
+        piece = out.at[core, over, source]
+        from_x[k] = push(piece, piece, s_x.at[k], r_x.at[k], (grp_x, me))
+        from_c[k] = push(piece, piece, s_c.at[0, k], r_c.at[0, k], (grp_c, me))
+        from_x[k].start()
+        from_c[k].start()
+    for k in range(n):
+        source = (me - k + n) % n
+        from_x[k].wait_recv()
+        piece = out.at[core, 1 - over, source]
+        far[k] = push(piece, piece, s_c.at[1, k], r_c.at[1, k], (grp_c, me))
+        far[k].start()
+    for k in range(n):
+        from_c[k].wait_recv()
+        far[k].wait_recv()
+    for copy in sent + list(from_x.values()) + list(from_c.values()) + list(far.values()):
+        copy.wait_send()
+
+
+def spread_sems(n):
+    dma = pltpu.SemaphoreType.DMA
+    return [dma((n,)), dma((n,)), dma((n,)), dma((n,)), dma((2, n)), dma((2, n))]
+
+
+def team_and_ring(n):
+    grp, me = lax.axis_index("grp"), lax.axis_index("blk")
+    _, _, grp_x, grp_c = team(grp)
+    return [(grp, (me + k) % n) for k in range(1, n)] + [(grp_x, me), (grp_c, me)]
+
+
+def weights_kernel(n, slab, gains, out, gains_out, local_sem, gain_sem, s_gain, r_gain, *sems):
+    grp, me = lax.axis_index("grp"), lax.axis_index("blk")
+    over, core, _, _ = team(grp)
+    greet(team_and_ring(n))
+    near = pltpu.make_async_copy(slab.at[me], out.at[core, over, me], local_sem)
+    near.start()
+    own_gain = pltpu.make_async_copy(gains, gains_out.at[me], gain_sem)
+    own_gain.start()
+    gain_copies = []
+    for k in range(1, n):
+        copy = push(gains, gains_out.at[me], s_gain.at[k], r_gain.at[k], (grp, (me + k) % n))
+        copy.start()
+        gain_copies.append(copy)
+    spread_pieces(n, lambda to: slab.at[to], out, near, sems)
+    own_gain.wait()
+    for copy in gain_copies:
+        copy.wait()
+
+
+def spread_weights(slab, gains):
+    n = lax.axis_size("blk")
+    dma = pltpu.SemaphoreType.DMA
+    return pl.pallas_call(
+        functools.partial(weights_kernel, n),
+        out_shape=(
+            jax.ShapeDtypeStruct((2, 2) + slab.shape, slab.dtype),
+            jax.ShapeDtypeStruct((n,) + gains.shape, gains.dtype),
+        ),
+        in_specs=[pl.BlockSpec(memory_space=pl.ANY)] * 2,
+        out_specs=[pl.BlockSpec(memory_space=pl.ANY)] * 2,
+        scratch_shapes=[dma, dma, dma((n,)), dma((n,))] + spread_sems(n),
+        compiler_params=kernel_params(2),
+        name="spread_weights",
+    )(slab, gains)
+
+
+def grads_kernel(n, wide, tall, out, out_tall, near_c, near_x, mine, tall_c, tall_x, *all_sems):
+    s_rc, r_rc, s_rx, r_rx, s_tc, r_tc, s_tx, r_tx, s_t, r_t, local_sem, tall_sem = all_sems[:12]
+    sems = all_sems[12:]
+    grp, me = lax.axis_index("grp"), lax.axis_index("blk")
+    over, core, grp_x, grp_c = team(grp)
+    greet(team_and_ring(n))
+    first, second = [], []
+    for k in range(n):
+        to = (me + k) % n
+        copy = push(wide.at[to, 1 - core], near_c.at[to], s_rc.at[k], r_rc.at[k], (grp_c, me))
+        copy.start()
+        first.append(copy)
+    tall_first = push(tall.at[1 - core], tall_c, s_tc, r_tc, (grp_c, me))
+    tall_first.start()
+    f32 = jnp.float32
+    for k in range(n):
+        to = (me + k) % n
+        first[k].wait_recv()
+        near_c[to, 1 - over] = (
+            wide[to, core, 1 - over].astype(f32) + near_c[to, 1 - over].astype(f32)
+        ).astype(jnp.bfloat16)
+        copy = push(near_c.at[to, 1 - over], near_x.at[to], s_rx.at[k], r_rx.at[k], (grp_x, me))
+        copy.start()
+        second.append(copy)
+    tall_first.wait_recv()
+    tall_c[1 - over] = (tall[core, 1 - over].astype(f32) + tall_c[1 - over].astype(f32)).astype(
+        jnp.bfloat16
+    )
+    tall_second = push(tall_c.at[1 - over], tall_x, s_tx, r_tx, (grp_x, me))
+    tall_second.start()
+    for k in range(n):
+        to = (me + k) % n
+        second[k].wait_recv()
+        mine[to] = (
+            wide[to, core, over].astype(f32)
+            + near_c[to, over].astype(f32)
+            + near_x[to].astype(f32)
+        ).astype(jnp.bfloat16)
+    near = pltpu.make_async_copy(mine.at[me], out.at[core, over, me], local_sem)
+    near.start()
+    tall_second.wait_recv()
+    tall_x[...] = (
+        tall[core, over].astype(f32) + tall_c[over].astype(f32) + tall_x[...].astype(f32)
+    ).astype(jnp.bfloat16)
+    tall_own = pltpu.make_async_copy(tall_x, out_tall.at[core, over], tall_sem)
+    tall_own.start()
+    tall_to_x = push(tall_x, out_tall.at[core, over], s_t.at[0], r_t.at[0], (grp_x, me))
+    tall_to_c = push(tall_x, out_tall.at[core, over], s_t.at[1], r_t.at[1], (grp_c, me))
+    tall_to_x.start()
+    tall_to_c.start()
+    spread_pieces(n, lambda to: mine.at[to], out, near, sems)
+    tall_to_x.wait_recv()
+    piece = out_tall.at[core, 1 - over]
+    tall_far = push(piece, piece, s_t.at[2], r_t.at[2], (grp_c, me))
+    tall_far.start()
+    tall_to_c.wait_recv()
+    tall_far.wait_recv()
+    tall_own.wait()
+    for copy in first + second + [tall_first, tall_second, tall_to_x, tall_to_c, tall_far]:
+        copy.wait_send()
+
+
+def sum_grads(wide, tall):
+    n = lax.axis_size("blk")
+    dma = pltpu.SemaphoreType.DMA
+    rows, columns = wide.shape
+    rows //= 4 * n
+    tall_rows, tall_columns = tall.shape
+    tall_rows //= 4
+    bf16 = jnp.bfloat16
+    return pl.pallas_call(
+        functools.partial(grads_kernel, n),
+        out_shape=(
+            jax.ShapeDtypeStruct((2, 2, n, rows, columns), bf16),
+            jax.ShapeDtypeStruct((2, 2, tall_rows, tall_columns), bf16),
+        ),
+        in_specs=[pl.BlockSpec(memory_space=pltpu.VMEM)] * 2,
+        out_specs=[pl.BlockSpec(memory_space=pl.ANY)] * 2,
+        scratch_shapes=[
+            pltpu.VMEM((n, 2, rows, columns), bf16),
+            pltpu.VMEM((n, rows, columns), bf16),
+            pltpu.VMEM((n, rows, columns), bf16),
+            pltpu.VMEM((2, tall_rows, tall_columns), bf16),
+            pltpu.VMEM((tall_rows, tall_columns), bf16),
+        ]
+        + [dma((n,))] * 4
+        + [dma] * 4
+        + [dma((3,))] * 2
+        + [dma] * 2
+        + spread_sems(n),
+        compiler_params=kernel_params(3),
+        name="sum_grads",
+    )(wide.reshape(n, 2, 2, rows, columns), tall.reshape(2, 2, tall_rows, tall_columns))
+
+
+def gains_kernel(n, teams, terms, out, heard, send, recv):
+    grp, me = lax.axis_index("grp"), lax.axis_index("blk")
+    others = [(i, k) for i in range(teams) for k in range(n) if i or k]
+    greet([((grp + i) % teams, (me + k) % n) for i, k in others])
+    copies = []
+    for i, k in others:
+        to = (me + k) % n
+        copy = push(
+            terms.at[to], heard.at[i, k], send.at[i, k], recv.at[i, k], ((grp + i) % teams, to)
+        )
+        copy.start()
+        copies.append(copy)
+    heard[0, 0] = terms[me]
+    for copy in copies:
+        copy.wait()
+    out[...] = jnp.sum(heard[...].reshape((teams * n,) + out.shape), axis=0)
+
+
+def sum_gains(terms):
+    n, teams = lax.axis_size("blk"), lax.axis_size("grp")
+    dma = pltpu.SemaphoreType.DMA
+    return pl.pallas_call(
+        functools.partial(gains_kernel, n, teams),
+        out_shape=jax.ShapeDtypeStruct(terms.shape[1:], jnp.float32),
+        in_specs=[pl.BlockSpec(memory_space=pltpu.VMEM)],
+        out_specs=pl.BlockSpec(memory_space=pltpu.VMEM),
+        scratch_shapes=[pltpu.VMEM((teams,) + terms.shape, jnp.float32)]
+        + [dma((teams, n))] * 2,
+        compiler_params=kernel_params(4),
+        name="sum_gains",
+    )(terms)
 
 
 def dot_f32(left, right):
@@ -294,6 +632,12 @@
     return lax.dot_general(
         left, right, (((0,), (0,)), ((), ())), preferred_element_type=jnp.float32
     )
+
+
+def pad_to(array, axis, size):
+    widths = [(0, 0)] * array.ndim
+    widths[axis] = (0, size - array.shape[axis])
+    return jnp.pad(array, widths)
 
 
 def per_device(block_input, doc_lens, norm_attn, w_qkv, w_out, norm_mlp, w_gate, w_up, w_down, cot):
@@ -301,10 +645,42 @@
     tok_rows, width = block_input.shape[1:]
     seq = tok_rows * n
     heads = HEADS // n
+    head_lanes = heads * HEAD
     score_scale = HEAD ** (-0.5)
-    gain_one = gather_rows(norm_attn).astype(jnp.float32)
-    gain_two = gather_rows(norm_mlp).astype(jnp.float32)
-    qkv_columns = split_columns(w_qkv, 3)
+    units = w_down.shape[0]
+    lanes = -(-units // 128) * 128
+    bf16 = jnp.bfloat16
+
+    over, core, _, _ = team(lax.axis_index("grp"))
+    quarter = w_qkv.shape[0] // 4
+    first_row = (2 * core + over) * quarter
+
+    def quarter_of(weight):
+        return lax.dynamic_slice_in_dim(weight, first_row, quarter, 0)
+
+    slab = jnp.concatenate(
+        [
+            quarter_of(w_qkv)
+            .reshape(quarter, 3, n, head_lanes)
+            .transpose(2, 0, 1, 3)
+            .reshape(n, quarter, 3 * head_lanes)
+        ]
+        + [
+            pad_to(quarter_of(w).reshape(quarter, n, units).transpose(1, 0, 2), 2, lanes)
+            for w in (w_gate, w_up)
+        ],
+        axis=2,
+    )
+    gains = pad_to(jnp.stack([norm_attn, norm_mlp]).astype(jnp.float32), 0, 8)
+    columns_all, gains_all = spread_weights(slab, gains)
+    columns_all = columns_all.transpose(2, 0, 1, 3, 4).reshape(width, slab.shape[2])
+    qkv_columns = columns_all[:, : 3 * head_lanes]
+    gate_columns = columns_all[:, 3 * head_lanes : 3 * head_lanes + lanes]
+    up_columns = columns_all[:, 3 * head_lanes + lanes :]
+    gain_one = gains_all[:, 0].reshape(width)
+    gain_two = gains_all[:, 1].reshape(width)
+    down_rows = pad_to(w_down, 0, lanes)
+
     places = jnp.arange(seq, dtype=jnp.int32)
     lengths = doc_lens[0]
     starts = jnp.cumsum(lengths) - lengths
@@ -314,18 +690,16 @@
 
     def normed(values, gain):
         inv = lax.rsqrt(jnp.mean(values * values, axis=-1, keepdims=True) + EPS)
-        return inv, (values * inv * gain).astype(jnp.bfloat16)
+        return inv, (values * inv * gain).astype(bf16)
 
     x_float = block_input[0].astype(jnp.float32)
     inv_one, normed_own = normed(x_float, gain_one)
-    normed_one = gather_rows(normed_own)
-    gate_columns = split_columns(w_gate, 1)
-    up_columns = split_columns(w_up, 1)
-    seed = gather_rows(cot[0])
+    normed_one = ring_gather(normed_own)
+    seed = ring_gather(cot[0])
     projected = dot_f32(normed_one, qkv_columns).reshape(seq, 3, heads, HEAD)
-    queries = rotate(projected[:, 0], cosine, sine_part).astype(jnp.bfloat16)
-    keys = rotate(projected[:, 1], cosine, sine_part).astype(jnp.bfloat16)
-    values = projected[:, 2].astype(jnp.bfloat16)
+    queries = rotate(projected[:, 0], cosine, sine_part).astype(bf16)
+    keys = rotate(projected[:, 1], cosine, sine_part).astype(bf16)
+    values = projected[:, 2].astype(bf16)
     scores = (
         jnp.einsum("qhd,khd->hqk", queries, keys, preferred_element_type=jnp.float32) * score_scale
     )
@@ -334,48 +708,38 @@
     raw = jnp.exp(scores - peak[..., None])
     total = jnp.sum(raw, axis=-1)
     attended = jnp.einsum(
-        "hqk,khd->hqd", raw.astype(jnp.bfloat16), values, preferred_element_type=jnp.float32
+        "hqk,khd->hqd", raw.astype(bf16), values, preferred_element_type=jnp.float32
     )
     log_total = peak + jnp.log(total)
     attended = (attended / total[..., None]).transpose(1, 0, 2)
-    attended_b = attended.reshape(seq, heads * HEAD).astype(jnp.bfloat16)
-    resid = x_float + scatter_rows(dot_f32(attended_b, w_out))
+    attended_b = attended.reshape(seq, head_lanes).astype(bf16)
+    resid = x_float + ring_scatter(dot_f32(attended_b, w_out))
     inv_two, normed_own = normed(resid, gain_two)
-    normed_two = gather_rows(normed_own)
+    normed_two = ring_gather(normed_own)
     gate_proj = dot_f32(normed_two, gate_columns)
     up_proj = dot_f32(normed_two, up_columns)
     sigmoid_gate = jax.nn.sigmoid(gate_proj)
     swish = gate_proj * sigmoid_gate
-    hidden = (swish * up_proj).astype(jnp.bfloat16)
-    dhidden = contract_rows(seed, w_down)
+    hidden = (swish * up_proj).astype(bf16)
+    dhidden = contract_rows(seed, down_rows)
     dgate = (dhidden * up_proj * sigmoid_gate * (1.0 + gate_proj * (1.0 - sigmoid_gate))).astype(
-        jnp.bfloat16
-    )
-    dup = (dhidden * swish).astype(jnp.bfloat16)
-    dnormed_two = scatter_rows(contract_rows(dgate, gate_columns) + contract_rows(dup, up_columns))
+        bf16
+    )
+    dup = (dhidden * swish).astype(bf16)
+    dnormed_two = ring_scatter(contract_rows(dgate, gate_columns) + contract_rows(dup, up_columns))
     a_two = dnormed_two * gain_two
     dresid = (
         cot[0].astype(jnp.float32)
         + inv_two * a_two
         - resid * inv_two**3 * jnp.mean(a_two * resid, axis=-1, keepdims=True)
     )
-    dresid_b = gather_rows(dresid.astype(jnp.bfloat16))
-    block_out = (resid + scatter_rows(dot_f32(hidden, w_down))).astype(jnp.bfloat16)
-    grad_down = lax.psum(dot_t(hidden, seed).astype(jnp.bfloat16), "grp").astype(jnp.float32)
-    grad_gate = lax.psum(
-        merge_columns(dot_t(normed_two, dgate).astype(jnp.bfloat16), 1), "grp"
-    ).astype(jnp.float32)
-    grad_up = lax.psum(
-        merge_columns(dot_t(normed_two, dup).astype(jnp.bfloat16), 1), "grp"
-    ).astype(jnp.float32)
-    dattended = contract_rows(dresid_b, w_out).astype(jnp.bfloat16).reshape(seq, heads, HEAD)
-    grad_out = lax.psum(dot_t(attended_b, dresid_b).astype(jnp.bfloat16), "grp").astype(
-        jnp.float32
-    )
+    dresid_b = ring_gather(dresid.astype(bf16))
+    block_out = (resid + ring_scatter(dot_f32(hidden, down_rows))).astype(bf16)
+    dattended = contract_rows(dresid_b, w_out).astype(bf16).reshape(seq, heads, HEAD)
     delta = jnp.sum(dattended.astype(jnp.float32) * attended, axis=-1).T
     probs = jnp.exp(scores - log_total[..., None])
     dprobs = jnp.einsum("qhd,khd->hqk", dattended, values, preferred_element_type=jnp.float32)
-    dscores = (probs * (dprobs - delta[..., None])).astype(jnp.bfloat16)
+    dscores = (probs * (dprobs - delta[..., None])).astype(bf16)
     dquery = score_scale * jnp.einsum(
         "hqk,khd->qhd", dscores, keys, preferred_element_type=jnp.float32
     )
@@ -383,34 +747,58 @@
         "hqk,qhd->khd", dscores, queries, preferred_element_type=jnp.float32
     )
     dvalue = jnp.einsum(
-        "hqk,qhd->khd", probs.astype(jnp.bfloat16), dattended, preferred_element_type=jnp.float32
+        "hqk,qhd->khd", probs.astype(bf16), dattended, preferred_element_type=jnp.float32
     )
     dqkv = (
         jnp.stack(
             [unrotate(dquery, cosine, sine_part), unrotate(dkey, cosine, sine_part), dvalue], axis=1
         )
-        .reshape(seq, 3 * heads * HEAD)
-        .astype(jnp.bfloat16)
-    )
-    dnormed_one = scatter_rows(contract_rows(dqkv, qkv_columns))
-    grad_qkv = lax.psum(
-        merge_columns(dot_t(normed_one, dqkv).astype(jnp.bfloat16), 3), "grp"
-    ).astype(jnp.float32)
+        .reshape(seq, 3 * head_lanes)
+        .astype(bf16)
+    )
+    dnormed_one = ring_scatter(contract_rows(dqkv, qkv_columns))
     a_one = dnormed_one * gain_one
     x_grad = (
         dresid
         + inv_one * a_one
         - x_float * inv_one**3 * jnp.mean(a_one * x_float, axis=-1, keepdims=True)
-    ).astype(jnp.bfloat16)
+    ).astype(bf16)
+    wide = jnp.concatenate(
+        [
+            dot_t(normed_one, dqkv).astype(bf16),
+            dot_t(normed_two, dgate).astype(bf16),
+            dot_t(normed_two, dup).astype(bf16),
+        ],
+        axis=1,
+    )
+    tall = jnp.concatenate(
+        [dot_t(attended_b, dresid_b).astype(bf16), dot_t(hidden, seed).astype(bf16)], axis=0
+    )
+    wide_sum, tall_sum = sum_grads(wide, tall)
+    wide_sum = wide_sum.astype(jnp.float32)
+    tall_sum = tall_sum.reshape(tall.shape).astype(jnp.float32)
+    shard_rows = 4 * quarter
+
+    def merged(part):
+        return part.transpose(0, 1, 3, 2, 4).reshape(shard_rows, n * part.shape[-1])
+
+    grad_qkv = (
+        wide_sum[..., : 3 * head_lanes]
+        .reshape(2, 2, n, quarter, 3, head_lanes)
+        .transpose(0, 1, 3, 4, 2, 5)
+        .reshape(shard_rows, 3 * width)
+    )
+    grad_gate = merged(wide_sum[..., 3 * head_lanes : 3 * head_lanes + units])
+    grad_up = merged(wide_sum[..., 3 * head_lanes + lanes : 3 * head_lanes + lanes + units])
+    grad_out = tall_sum[:head_lanes]
+    grad_down = tall_sum[head_lanes : head_lanes + units]
     gain_terms = jnp.stack(
         [
             jnp.sum(dnormed_one * x_float * inv_one, axis=0),
             jnp.sum(dnormed_two * resid * inv_two, axis=0),
         ]
     )
-    gain_grads = lax.psum(
-        lax.psum_scatter(gain_terms, "blk", scatter_dimension=1, tiled=True), "grp"
-    )
+    gain_grads = sum_gains(pad_to(gain_terms, 0, 8).reshape(8, n, -1).transpose(1, 0, 2))
     return (
         block_out[None],
         x_grad[None],

time: 1410 us -> 876 us (0.62)
  waiting for transfers between devices: 1100 us -> 0 us
  Pallas kernels: 0 us -> 605 us
  local copies, waits for them, and re-layouts: 73.4 us -> 128 us
  blocking collectives: 42.4 us -> 0 us
  starting transfers between devices: 31.6 us -> 0 us
  matrix products: 105 us -> 88.7 us
    pallas_call x0 -> x11, Pallas kernels: none -> 605 us  [the longest x1 180 us: sum_grads(): pl.pallas_call(functools.partial(grads_kernel, n), out_shape=(jax.ShapeDt...]
    all_to_all x6 -> x0, waiting for transfers between devices: 549 us -> none  [the longest x3 327 us: split_columns(): mixed = lax.all_to_all(cut, 'blk', split_axis=0, concat_axis=0, tiled=True)]
    psum x1 -> x0, waiting for transfers between devices: 222 us -> none  [per_device(): lax.psum(merge_columns(dot_t(normed_one, dqkv).astype(jnp.bfloat16), 3),...]
    reduce_scatter x4 -> x0, waiting for transfers between devices: 189 us -> none  [scatter_rows(): lax.psum_scatter(partial.astype(jnp.bfloat16), 'blk', scatter_dimension=0...]
    all_gather x4 -> x0, waiting for transfers between devices: 72 us -> none  [gather_rows(): return lax.all_gather(block, 'blk', axis=0, tiled=True)]
    unnamed x11 -> x0, waiting for transfers between devices: 62.5 us -> none
    unnamed x79, local copies, waits for them, and re-layouts: 51.2 us -> 3.98 us
    transpose x2 -> x6, local copies, waits for them, and re-layouts: 8.51 us -> 47.4 us  [the longest x3 28.9 us: merged(): return part.transpose(0, 1, 3, 2, 4).reshape(shard_rows, n * part.shape[-1])]
  transfers between devices with their start and end apart: 16 -> 0, of which waited for: 12 -> 0; matrix products, arithmetic and copies ran while one was open for 8% -> 0% of each run, Pallas kernels for 0% -> 0%
where the time goes in v2:
time: 876 us; the launch traced here: 866 us
  Pallas kernels  605 us (69%)
  local copies, waits for them, and re-layouts  128 us (15%)
  matrix products  88.7 us (10%)
  other arithmetic  41.8 us (5%)
    pallas_call x1, Pallas kernels, sum_grads(): pl.pallas_call(functools.partial(grads_kernel, n), out_shape=(jax.ShapeDt...  180 us
    pallas_call x4, Pallas kernels, ring_gather(): pl.pallas_call(functools.partial(gather_kernel, n), out_shape=jax.ShapeDt...  175 us
    pallas_call x4, Pallas kernels, ring_scatter(): pl.pallas_call(functools.partial(scatter_kernel, n), out_shape=jax.ShapeD...  158 us
    pallas_call x1, Pallas kernels, spread_weights(): pl.pallas_call(functools.partial(weights_kernel, n), out_shape=(jax.Shape...  74 us
    dot_general x5, matrix products, contract_rows(): lax.dot_general(left, right, (((1,), (1,)), ((), ())), preferred_element_...  29.7 us
    transpose x3, local copies, waits for them, and re-layouts, merged(): return part.transpose(0, 1, 3, 2, 4).reshape(shard_rows, n * part.shape[-1])  28.9 us
    dot_general x5, matrix products, dot_f32(): return jnp.dot(left, right, preferred_element_type=jnp.float32)  25.2 us
    dot_general x5, matrix products, dot_t(): lax.dot_general(left, right, (((0,), (0,)), ((), ())), preferred_element_...  19 us

profile of v2, /device:TPU:1, one launch (start us, length us, event | category | flops | bytes accessed | tf_op | source)
XLA Modules:
  0.0 865.6 jit_solution(18398453936894813738)
XLA Ops:
  2.3 1.2 fusion.40
  6.1 1.8 multiply_cosine_fusion
  10.1 2.7 constant_dynamic-slice_fusion
  12.8 1.5 reshape.262
  14.3 1.3 copy.101
  15.6 2.5 reshape.261
  18.1 1.3 copy.102
  19.4 1.5 fusion.31.slab
  20.9 44.6 %ring_gather.6 = bf16[8,128,2048]{2,1,0:T(8,128)(2,1)} custom-call(bf16[128,2048]{1,0:T(8,128)(2,1)} %bitcast.176), custom_call_target="tpu_custom_call" | custom-call | tf_op jit(solution)/shard_map/ring_gather/pallas_call | solution.py:346
  65.5 74.0 %spread_weights.1 = (bf16[2,2,8,64,2304]{4,3,2,1,0:T(8,128)(2,1)}, f32[8,8,256]{2,1,0:T(8,128)}) custom-call(bf16[8,64,2304]{2,1,0:T(8,128)(2,1)} %fusion.31.slab, f32[8,256]{1,0:T(8,128)} %fusion.61.gains), custom_call_target="tpu_custom_call" | custom-call | tf_op jit(solution)/shard_map/spread_weights/pallas_call | solution.py:485
  140.4 8.4 copy.71
  149.8 3.8 slice_bitcast_fusion.2
  153.5 4.6 copy.72
  158.2 55.2 %ring_gather.4 = bf16[8,128,2048]{2,1,0:T(8,128)(2,1)} custom-call(bf16[128,2048]{1,0:T(8,128)(2,1)} %fusion.42.x_ref), custom_call_target="tpu_custom_call" | custom-call | tf_op jit(solution)/shard_map/ring_gather/pallas_call | solution.py:346
  213.4 5.3 fusion.75
  220.2 2.0 fusion.6
  222.2 2.2 fusion
  225.5 3.6 fusion.74
  229.2 3.3 convolution_convert_fusion
  232.5 43.8 %ring_scatter.4 = f32[128,2048]{1,0:T(8,128)} custom-call(bf16[8,128,2048]{2,1,0:T(8,128)(2,1)} %bitcast.147), custom_call_target="tpu_custom_call" | custom-call | tf_op jit(solution)/shard_map/ring_scatter/pallas_call | solution.py:399
  276.3 1.4 multiply_reduce_fusion.3
  278.7 40.3 %ring_gather.5 = bf16[8,128,2048]{2,1,0:T(8,128)(2,1)} custom-call(bf16[128,2048]{1,0:T(8,128)(2,1)} %multiply_convert_fusion.2.x_ref), custom_call_target="tpu_custom_call" | custom-call | tf_op jit(solution)/shard_map/ring_gather/pallas_call | solution.py:346
  319.1 6.3 fusion.23
  325.4 5.5 fusion.27
  330.9 5.7 fusion.17
  336.6 5.0 convolution_convert_fusion.4
  341.6 3.8 convolution_convert_fusion.5
  345.5 5.0 convolution_convert_fusion.6
  350.5 4.9 convolution_convert_fusion.2
  355.4 40.2 %ring_scatter.5 = f32[128,2048]{1,0:T(8,128)} custom-call(bf16[8,128,2048]{2,1,0:T(8,128)(2,1)} %bitcast.160), custom_call_target="tpu_custom_call" | custom-call | tf_op jit(solution)/shard_map/ring_scatter/pallas_call | solution.py:399
  395.7 5.9 fusion.25
  401.6 7.3 add_convert_fusion
  409.0 38.7 %ring_scatter.6 = f32[128,2048]{1,0:T(8,128)} custom-call(bf16[8,128,2048]{2,1,0:T(8,128)(2,1)} %bitcast.159), custom_call_target="tpu_custom_call" | custom-call | tf_op jit(solution)/shard_map/ring_scatter/pallas_call | solution.py:399
  447.7 1.5 multiply_reduce_fusion
  449.2 2.9 fusion.71
  452.1 34.8 %ring_gather.7 = bf16[8,128,2048]{2,1,0:T(8,128)(2,1)} custom-call(bf16[128,2048]{1,0:T(8,128)(2,1)} %get-tuple-element.23.x_ref), custom_call_target="tpu_custom_call" | custom-call | tf_op jit(solution)/shard_map/ring_gather/pallas_call | solution.py:346
  487.0 3.6 multiply_reduce_fusion.1
  490.6 1.3 convolution_convert_fusion.7
  492.0 2.5 pad_maximum_fusion.1
  494.5 1.4 slice-done.4
  496.1 2.6 fusion.35
  498.7 4.3 multiply_convert_fusion
  503.1 1.5 fusion.38
  506.0 7.1 convolution_convert_fusion.1
  513.1 3.8 convolution_convert_fusion.3
  516.9 4.5 pad_maximum_fusion
  521.4 12.4 %copy.83 = bf16[2048,2304]{1,0:T(8,128)(2,1)} copy(bf16[2048,2304]{0,1:T(8,128)(2,1)} %pad_maximum_fusion) | data formatting | bytes 18874368 | tf_op jit(solution)/shard_map/concatenate | solution.py:766
  533.8 34.8 %ring_scatter.7 = f32[128,2048]{1,0:T(8,128)} custom-call(bf16[8,128,2048]{2,1,0:T(8,128)(2,1)} %bitcast.158), custom_call_target="tpu_custom_call" | custom-call | tf_op jit(solution)/shard_map/ring_scatter/pallas_call | solution.py:399
  568.6 179.9 %sum_grads.1 = (bf16[2,2,8,64,2304]{4,3,2,1,0:T(8,128)(2,1)}, bf16[2,2,256,2048]{3,2,1,0:T(8,128)(2,1)}) custom-call(bf16[8,2,2,64,2304]{4,3,2,1,0:T(8,128)(2,1)} %bitcast.143, bf16[2,2,256,2048]{3,2,1,0:T(8,128)(2,1)} %bitcast.154), custom_call_target="tpu_custom_call" | custom-call | tf_op jit(solution)/shard_map/sum_grads/pallas_call | solution.py:569
  750.7 18.7 %sum_gains.1 = f32[8,256]{1,0:T(8,128)} custom-call(f32[8,8,256]{2,1,0:T(8,128)} %bitcast.181), custom_call_target="tpu_custom_call" | custom-call | tf_op jit(solution)/shard_map/sum_gains/pallas_call | solution.py:615
  769.4 1.3 fusion.73
  770.8 1.3 bitcast_convert_fusion
  772.1 1.5 slice.108
  773.6 2.9 slice.111
  776.5 3.5 slice.107
  780.0 10.9 %reshape.276 = f32[2,2,8,64,3,256]{5,4,3,2,1,0:T(4,128)} reshape(f32[2,2,8,64,768]{4,3,2,1,0:T(8,128)} %slice.107) | data formatting | bytes 12582912 | tf_op jit(solution)/shard_map/reshape | solution.py:787
  791.0 9.7 %copy.84 = f32[2,2,64,3,8,256]{5,4,3,2,1,0:T(8,128)} copy(f32[2,2,64,3,8,256]{5,3,2,4,1,0:T(4,128)} %bitcast.144) | data formatting | bytes 12582912 | tf_op jit(solution)/shard_map/transpose | solution.py:788
  800.7 7.3 reshape.277
  808.0 12.5 %convert_element_type.162 = f32[2,2,8,64,2304]{4,3,2,1,0:T(8,128)} convert(bf16[2,2,8,64,2304]{4,3,2,1,0:T(8,128)(2,1)} %get-tuple-element.15) | non-fusion elementwise | flops 4718592 | bytes 28311552 | tf_op jit(solution)/shard_map/convert_element_type | solution.py:778
  820.5 10.6 %slice_bitcast_fusion = (f32[2,2,64,8,704]{4,2,3,1,0:T(8,128)}, f32[2,2,64,8,704]{4,2,3,1,0:T(8,128)}) fusion(f32[2,2,8,64,2304]{4,3,2,1,0:T(8,128)} %convert_element_type.162), kind=kLoop, calls=%fused_computation.11 | loop fusion | bytes 23068672 | tf_op jit(solution)/shard_map/transpose | solution.py:783
  831.1 9.1 %copy.86 = f32[2,2,64,8,704]{4,3,2,1,0:T(8,128)} copy(f32[2,2,64,8,704]{4,2,3,1,0:T(8,128)} %get-tuple-element.27) | data formatting | bytes 11534336 | tf_op jit(solution)/shard_map/transpose | solution.py:783
  840.2 8.0 reshape.279
  848.2 9.2 %copy.85 = f32[2,2,64,8,704]{4,3,2,1,0:T(8,128)} copy(f32[2,2,64,8,704]{4,2,3,1,0:T(8,128)} %get-tuple-element.28) | data formatting | bytes 11534336 | tf_op jit(solution)/shard_map/transpose | solution.py:783
  857.4 7.8 reshape.278
  (110 shorter events, 15.6 us)
Async XLA Ops:
  0.6 7.3 copy-start
  4.1 144.7 %copy-start.26 = (f32[128]{0:T(128)}, f32[128]{0:T(128)S(1)}, u32[]{:S(2)}) copy-start(f32[128]{0:T(128)S(1)} %get-tuple-element.54) | copy-start | bytes 1540
  10.1 214.3 %copy-start.7 = (pred[1024,1024]{0,1:T(8,128)(4,1)}, pred[1024,1024]{0,1:T(8,128)(4,1)S(1)}, u32[]{:S(2)}) copy-start(pred[1024,1024]{0,1:T(8,128)(4,1)S(1)} %fusion.11) | copy-start | bytes 3145732
  140.4 8.4 copy-start.24
  140.4 8.4 copy-start.2
  158.2 55.2 %copy-start.15 = (bf16[768,2048]{1,0:T(8,128)(2,1)S(1)}, bf16[768,2048]{1,0:T(8,128)(2,1)}, u32[]{:S(2)}) copy-start(bf16[768,2048]{1,0:T(8,128)(2,1)} %copy.72) | copy-start | bytes 9437188
  218.7 5.8 copy-start.19
  218.7 1.1 copy-start.17
  220.2 2.0 copy-start.20
  222.2 3.3 copy-start.4
  225.5 3.6 copy-start.22
  319.1 6.3 copy-start.12
  325.4 5.5 copy-start.11
  325.4 5.5 copy-start.29
  336.6 8.9 %copy-start.31 = (bf16[1024,768]{1,0:T(8,128)(2,1)}, bf16[1024,768]{1,0:T(8,128)(2,1)S(1)}, u32[]{:S(2)}) copy-start(bf16[1024,768]{1,0:T(8,128)(2,1)S(1)} %get-tuple-element.30) | copy-start | bytes 4718596
  336.6 5.0 copy-start.32
  395.7 5.9 copy-start.33
  408.9 40.3 %copy-start.6 = (f32[128,2048]{1,0:T(8,128)S(1)}, f32[128,2048]{1,0:T(8,128)}, u32[]{:S(2)}) copy-start(f32[128,2048]{1,0:T(8,128)} %ring_scatter.5) | copy-start | bytes 3145732
  408.9 40.3 %copy-start.18 = (bf16[1,128,2048]{2,1,0:T(8,128)(2,1)S(1)}, bf16[1,128,2048]{2,1,0:T(8,128)(2,1)}, u32[]{:S(2)}) copy-start(bf16[1,128,2048]{2,1,0:T(8,128)(2,1)} %param.19) | copy-start | bytes 1572868
  452.1 34.8 %copy-start.23 = (bf16[256,2048]{1,0:T(8,128)(2,1)S(1)}, bf16[256,2048]{1,0:T(8,128)(2,1)}, u32[]{:S(2)}) copy-start(bf16[256,2048]{1,0:T(8,128)(2,1)} %param.14) | copy-start | bytes 3145732
  452.1 34.8 %copy-start.30 = (f32[1024,2,128]{0,2,1:T(8,128)S(1)}, f32[1024,2,128]{0,2,1:T(8,128)}, u32[]{:S(2)}) copy-start(f32[1024,2,128]{0,2,1:T(8,128)} %get-tuple-element.60) | copy-start | bytes 3145732
  486.9 3.7 copy-start.13
  487.0 5.0 copy-start.16
  490.6 3.9 slice-start.3
  491.9 4.0 slice-start.4
  491.9 4.2 copy-start.8
  498.7 4.3 copy-start.21
  506.0 7.1 copy-start.10
  513.1 3.8 copy-start.14
  568.6 180.0 %copy-start.3 = (f32[128,2048]{1,0:T(8,128)S(1)}, f32[128,2048]{1,0:T(8,128)}, u32[]{:S(2)}) copy-start(f32[128,2048]{1,0:T(8,128)} %ring_scatter.7) | copy-start | bytes 3145732
  568.6 180.0 %copy-start.25 = (f32[8,1,256]{2,1,0:T(1,128)S(1)}, f32[8,1,256]{2,1,0:T(1,128)}, u32[]{:S(2)}) copy-start(f32[8,1,256]{2,1,0:T(1,128)} %copy-done.24) | copy-start | bytes 24580
  568.6 180.0 %copy-start.27 = (f32[128]{0:T(128)S(1)}, f32[128]{0:T(128)}, u32[]{:S(2)}) copy-start(f32[128]{0:T(128)} %copy-done.26) | copy-start | bytes 1540
  568.6 180.3 %copy-start.9 = (f32[128,2048]{1,0:T(8,128)S(1)}, f32[128,2048]{1,0:T(8,128)}, u32[]{:S(2)}) copy-start(f32[128,2048]{1,0:T(8,128)} %get-tuple-element.24) | copy-start | bytes 3145732
  568.6 180.3 %copy-start.28 = (f32[128]{0:T(128)S(1)}, f32[128]{0:T(128)}, u32[]{:S(2)}) copy-start(f32[128]{0:T(128)} %get-tuple-element.53) | copy-start | bytes 1540
  748.6 22.2 %copy-start.5 = (bf16[2,2,256,2048]{3,2,1,0:T(8,128)(2,1)S(1)}, bf16[2,2,256,2048]{3,2,1,0:T(8,128)(2,1)}, u32[]{:S(2)}) copy-start(bf16[2,2,256,2048]{3,2,1,0:T(8,128)(2,1)} %get-tuple-element.16) | copy-start | bytes 12582916
  770.8 5.8 slice-start
  770.8 5.8 slice-start.1
  773.6 2.9 slice-start.2
  848.2 17.0 %copy-start.1 = (bf16[256,6144]{1,0:T(8,128)(2,1)S(1)}, bf16[256,6144]{1,0:T(8,128)(2,1)}, u32[]{:S(2)}) copy-start(bf16[256,6144]{1,0:T(8,128)(2,1)} %param.13) | copy-start | bytes 9437188

commit v3 on v0

--- a/solution.py
+++ b/solution.py
@@ -1,8 +1,11 @@
+import functools
 import math
 
 import jax
 import jax.numpy as jnp
 from jax import lax
+from jax.experimental import pallas as pl
+from jax.experimental.pallas import tpu as pltpu
 from jax.sharding import PartitionSpec as P
 
 HEADS = 16
@@ -80,7 +83,7 @@
     return lax.psum(shared, "grp").astype(jnp.float32)
 
 
-def per_device(block_input, doc_lens, norm_attn, w_qkv, w_out, norm_mlp, w_gate, w_up, w_down, cot):
+def per_device_gather(block_input, doc_lens, norm_attn, w_qkv, w_out, norm_mlp, w_gate, w_up, w_down, cot):
     tok_rows = block_input.shape[1]
     width = block_input.shape[2]
     score_scale = HEAD ** (-0.5)
@@ -259,9 +262,1238 @@
     )
 
 
+MESH = pl.DeviceIdType.MESH
+VMEM_BYTES = 62 * 2**20
+
+
+def ring_place(block, n):
+    up, row = block // 2, block % 2
+    return (1 - row) * up + row * (n - 1 - up)
+
+
+def ring_block(place, n):
+    back = place // (n // 2)
+    return (1 - back) * 2 * place + back * (2 * (n - 1 - place) + 1)
+
+
+def at_offset(place, offset, n):
+    return ring_block((place + offset + n) % n, n)
+
+
+def greet(devices):
+    barrier = pltpu.get_barrier_semaphore()
+    for device in devices:
+        pl.semaphore_signal(barrier, inc=1, device_id=device, device_id_type=MESH)
+    pl.semaphore_wait(barrier, len(devices))
+
+
+def push(src, dst, send_sem, recv_sem, device):
+    return pltpu.make_async_remote_copy(
+        src_ref=src,
+        dst_ref=dst,
+        send_sem=send_sem,
+        recv_sem=recv_sem,
+        device_id=device,
+        device_id_type=MESH,
+    )
+
+
+def kernel_params(collective_id):
+    return pltpu.CompilerParams(
+        collective_id=collective_id, has_side_effects=True, vmem_limit_bytes=VMEM_BYTES
+    )
+
+
+def dot_f32(left, right):
+    return jnp.dot(left, right, preferred_element_type=jnp.float32)
+
+
+def dot_t(left, right):
+    return lax.dot_general(
+        left, right, (((0,), (0,)), ((), ())), preferred_element_type=jnp.float32
+    )
+
+
+def nt_dot(left, right):
+    return lax.dot_general(
+        left, right, (((1,), (1,)), ((), ())), preferred_element_type=jnp.float32
+    )
+
+
+def ring_ends(n):
+    grp, me = lax.axis_index("grp"), lax.axis_index("blk")
+    place = ring_place(me, n)
+    return place, ((grp, at_offset(place, 1, n)), (grp, at_offset(place, -1, n)))
+
+
+class Gather:
+    def __init__(self, n, buf, send, recv, ends, own=None):
+        self.n, self.buf, self.send, self.recv, self.ends = n, buf, send, recv, ends
+        self.own = buf.at[0] if own is None else own
+        self.half = buf.shape[1] // 2
+
+    def copy(self, step, chunk, way):
+        part = pl.ds(chunk * self.half, self.half)
+        if isinstance(step, int):
+            target = min(2 * step + 1 + way, self.n - 1)
+        else:
+            target = jnp.minimum(2 * step + 1 + way, self.n - 1)
+        first = isinstance(step, int) and step == 0
+        return push(
+            self.own.at[part] if first else self.buf.at[2 * step - 1 + way, part],
+            self.buf.at[target, part],
+            self.send.at[step, chunk, way],
+            self.recv.at[step, chunk, way],
+            self.ends[way],
+        )
+
+    def landed(self, step, chunk, way):
+        target = jnp.minimum(2 * step + 1 + way, self.n - 1)
+        place = self.buf.at[target, pl.ds(chunk * self.half, self.half)]
+        sems = (self.send.at[step, chunk, way], self.recv.at[step, chunk, way])
+        return push(place, place, *sems, self.ends[way])
+
+    def used(self, step, chunk, way):
+        return step < self.n // 2 - 1 or chunk == way
+
+    def start(self):
+        for chunk in range(2):
+            for way in range(2):
+                self.copy(0, chunk, way).start()
+
+    def advance(self, step):
+        for chunk in range(2):
+            for way in range(2):
+                if isinstance(step, int):
+                    if self.used(step, chunk, way):
+                        self.copy(step, chunk, way).wait_recv()
+                        if step + 1 < self.n // 2 and self.used(step + 1, chunk, way):
+                            self.copy(step + 1, chunk, way).start()
+                elif chunk == way:
+                    self.landed(step, chunk, way).wait_recv()
+                    pl.when(step + 1 < self.n // 2)(self.copy(step + 1, chunk, way).start)
+                else:
+                    pl.when(step < self.n // 2 - 1)(self.landed(step, chunk, way).wait_recv)
+                    pl.when(step + 1 < self.n // 2 - 1)(self.copy(step + 1, chunk, way).start)
+
+    def finish(self):
+        for step in range(self.n // 2):
+            for chunk in range(2):
+                for way in range(2):
+                    if self.used(step, chunk, way):
+                        self.copy(step, chunk, way).wait_send()
+
+
+class Scatter:
+    def __init__(self, n, held, terms, send, recv, ends, term):
+        self.n, self.held, self.terms, self.send, self.recv = n, held, terms, send, recv
+        self.ends, self.term = ends, term
+        self.half = held.shape[2] // 2
+
+    def copy(self, step, chunk, way):
+        part = pl.ds(chunk * self.half, self.half)
+        return push(
+            self.held.at[way, step, part],
+            self.held.at[way, step + 1, part],
+            self.send.at[step, chunk, way],
+            self.recv.at[step, chunk, way],
+            self.ends[way],
+        )
+
+    def step(self, step):
+        for way in range(2):
+            self.terms[way] = self.term(step, way)
+        for chunk in range(2):
+            for way in range(2):
+                part = pl.ds(chunk * self.half, self.half)
+
+                def first(way=way, part=part):
+                    self.held[way, step, part] = self.terms[way, part].astype(jnp.bfloat16)
+
+                def later(chunk=chunk, way=way, part=part):
+                    self.copy(step - 1, chunk, way).wait_recv()
+                    self.held[way, step, part] = (
+                        self.terms[way, part] + self.held[way, step, part].astype(jnp.float32)
+                    ).astype(jnp.bfloat16)
+
+                if isinstance(step, int):
+                    (later if step else first)()
+                else:
+                    pl.when(step == 0)(first)
+                    pl.when(step > 0)(later)
+                self.copy(step, chunk, way).start()
+
+    def result(self, way):
+        for chunk in range(2):
+            self.copy(self.n - 2, chunk, way).wait_recv()
+        return self.term(self.n - 1, way) + self.held[way, self.n - 1].astype(jnp.float32)
+
+    def finish(self):
+        def body(step, _):
+            for chunk in range(2):
+                for way in range(2):
+                    self.copy(step, chunk, way).wait_send()
+            return 0
+
+        lax.fori_loop(0, self.n - 1, body, 0)
+
+
+def behind(step, way, n):
+    near = 2 * step + 1 + way
+    far = 2 * (n - 1 - step) - way
+    if isinstance(step, int):
+        return 0 if step == n - 1 else min(near, far, n - 1)
+    return jnp.where(step == n - 1, 0, jnp.minimum(jnp.minimum(near, far), n - 1))
+
+
+def team(grp):
+    over, core = grp // 2, grp % 2
+    return over, core, (1 - over) * 2 + core, over * 2 + 1 - core
+
+
+def mlp_kernel(
+    n,
+    lanes,
+    ob,
+    w_out,
+    x_ref,
+    gain,
+    weights,
+    w_down,
+    seed_hbm,
+    seed_own,
+    block_out,
+    dresid_out,
+    dattended,
+    gain_terms,
+    wide_sum,
+    down_sum,
+    dresid,
+    normed,
+    seed,
+    gate_up,
+    down,
+    hidden,
+    dgate_up,
+    held_one,
+    held_two,
+    terms,
+    resid,
+    wide,
+    wide_c,
+    tall,
+    tall_c,
+    load_sem,
+    s_one,
+    r_one,
+    s_two,
+    r_two,
+    s_three,
+    r_three,
+    s_norm,
+    r_norm,
+    s_dres,
+    r_dres,
+    s_wc,
+    r_wc,
+    s_wx,
+    r_wx,
+    s_tall,
+    r_tall,
+):
+    f32, bf16 = jnp.float32, jnp.bfloat16
+    grp, me = lax.axis_index("grp"), lax.axis_index("blk")
+    over, core, grp_x, grp_c = team(grp)
+    _, ends = ring_ends(n)
+    units = w_down.shape[0]
+    loads = [
+        pltpu.make_async_copy(weights, gate_up, load_sem.at[0]),
+        pltpu.make_async_copy(w_down, down.at[pl.ds(0, units)], load_sem.at[1]),
+        pltpu.make_async_copy(
+            seed_hbm.at[pl.ds(1, n - 1)], seed.at[pl.ds(1, n - 1)], load_sem.at[2]
+        ),
+        pltpu.make_async_copy(seed_own, seed.at[0], load_sem.at[3]),
+    ]
+    for load in loads:
+        load.start()
+    if units < lanes:
+        down[pl.ds(units, lanes - units)] = jnp.zeros((lanes - units, down.shape[1]), bf16)
+    greet(list(ends) + [(grp_x, me), (grp_c, me)])
+    columns = x_ref.shape[1]
+    half = columns // 2
+
+    def out_term(step, way):
+        return dot_f32(ob[behind(step, way, n)], w_out[:, way * half : (way + 1) * half])
+
+    one = Scatter(n, held_one, terms, s_one, r_one, ends, out_term)
+    one.step(0)
+    lax.fori_loop(1, n - 1, lambda step, _: (one.step(step), 0)[1], 0)
+    for way in range(2):
+        part = slice(way * half, (way + 1) * half)
+        resid[:, part] = x_ref[:, part].astype(f32) + one.result(way)
+    value = resid[...]
+    inv = lax.rsqrt(jnp.mean(value * value, axis=-1, keepdims=True) + EPS)
+    normed[0] = (value * inv * gain[...]).astype(bf16)
+    gather = Gather(n, normed, s_norm, r_norm, ends)
+    gather.start()
+    one.finish()
+    for load in loads:
+        load.wait()
+
+    def mlp(slot, _):
+        both = dot_f32(normed[slot], gate_up[...])
+        grad = nt_dot(seed[slot], down[...])
+        gate, up = both[:, :lanes], both[:, lanes:]
+        sig = jax.nn.sigmoid(gate)
+        swish = gate * sig
+        hidden[slot] = (swish * up).astype(bf16)
+        dgate_up[slot, :, :lanes] = (grad * up * sig * (1.0 + gate * (1.0 - sig))).astype(bf16)
+        dgate_up[slot, :, lanes:] = (grad * swish).astype(bf16)
+        return 0
+
+    def norm_term(step, way):
+        return nt_dot(dgate_up[behind(step, way, n)], gate_up[way * half : (way + 1) * half, :])
+
+    two = Scatter(n, held_two, terms, s_two, r_two, ends, norm_term)
+
+    def turn(t, _):
+        pl.when(t > 0)(lambda: gather.advance(t - 1))
+        low = jnp.maximum(2 * t - 1, 0)
+        lax.fori_loop(low, jnp.minimum(2 * t + 1, n), mlp, 0)
+        pl.when(t > 0)(lambda: two.step(t - 1))
+        return 0
+
+    lax.fori_loop(0, n // 2 + 1, turn, 0)
+
+    tall_rows = lanes // 4
+
+    def tall_at(first, count):
+        return pl.ds(pl.multiple_of(first * tall_rows, tall_rows), count * tall_rows)
+
+    tall_tile = 256 if lanes % 256 == 0 else 128
+    tiles = lanes // tall_tile
+
+    def tall_grad(tile):
+        at = pl.multiple_of(tile * tall_tile, tall_tile)
+        left = hidden[:, :, pl.ds(at, tall_tile)].reshape(-1, tall_tile)
+        grad_rows = dot_t(left, seed[...].reshape(-1, columns)).astype(bf16)
+        tall[pl.ds(at, tall_tile)] = grad_rows
+
+    def rest(step, _):
+        two.step(step)
+        pl.when(step - n // 2 < tiles)(lambda: tall_grad(step - n // 2))
+        return 0
+
+    lax.fori_loop(n // 2, n - 1, rest, 0)
+    for tile in range(n // 2 - 1, tiles):
+        tall_grad(tile)
+    tall_one = push(tall.at[tall_at(2 - 2 * core, 2)], tall_c, s_tall.at[0], r_tall.at[0], (grp_c, me))
+    tall_one.start()
+
+    value = resid[...]
+    inv = lax.rsqrt(jnp.mean(value * value, axis=-1, keepdims=True) + EPS)
+    for way in range(2):
+        part = slice(way * half, (way + 1) * half)
+        dresid_out[:, part] = two.result(way)
+    dnormed = dresid_out[...]
+    gain_terms[...] = jnp.sum(dnormed * value * inv, axis=0, keepdims=True)
+    a_two = dnormed * gain[...]
+    total = (
+        seed[0].astype(f32)
+        + inv * a_two
+        - value * inv**3 * jnp.mean(a_two * value, axis=-1, keepdims=True)
+    )
+    dresid_out[...] = total
+    dresid[0] = total.astype(bf16)
+    back = Gather(n, dresid, s_dres, r_dres, ends)
+    back.start()
+    two.finish()
+
+    def down_term(step, way):
+        return dot_f32(hidden[behind(step, way, n)], down[:, way * half : (way + 1) * half])
+
+    three = Scatter(n, held_one, terms, s_three, r_three, ends, down_term)
+
+    def dob(slot, _):
+        dattended[slot] = nt_dot(dresid[slot], w_out[...]).astype(bf16)
+        return 0
+
+    def wide_copy_c(tile):
+        return push(
+            wide.at[tile, 1 - core], wide_c.at[tile], s_wc.at[tile], r_wc.at[tile], (grp_c, me)
+        )
+
+    def wide_copy_x(tile):
+        return push(
+            wide_c.at[tile, 1 - over], wide_sum.at[tile], s_wx.at[tile], r_wx.at[tile], (grp_x, me)
+        )
+
+    quarter = wide.shape[3]
+
+    def wide_grad(tile):
+        at = pl.multiple_of(tile * 4 * quarter, 4 * quarter)
+        left = normed[:, :, pl.ds(at, 4 * quarter)].reshape(-1, 4 * quarter)
+        grad = dot_t(left, dgate_up[...].reshape(-1, 2 * lanes)).astype(bf16)
+        wide[tile] = grad.reshape(2, 2, quarter, 2 * lanes)
+        wide_copy_c(tile).start()
+
+    def wide_pass(tile):
+        wide_copy_c(tile).wait_recv()
+        wide_c[tile, 1 - over] = (
+            wide[tile, core, 1 - over].astype(f32) + wide_c[tile, 1 - over].astype(f32)
+        ).astype(bf16)
+        wide_copy_x(tile).start()
+
+    tall_two = push(tall_c.at[tall_at(1 - over, 1)], down_sum, s_tall.at[1], r_tall.at[1], (grp_x, me))
+
+    def again(t, _):
+        pl.when(t > 0)(lambda: back.advance(t - 1))
+        low = jnp.maximum(2 * t - 1, 0)
+        lax.fori_loop(low, jnp.minimum(2 * t + 1, n), dob, 0)
+
+        def inner(step, _):
+            pl.when(step < n - 1)(lambda: three.step(step))
+            pl.when(step > 0)(lambda: wide_pass(step - 1))
+            wide_grad(step)
+            return 0
+
+        lax.fori_loop(2 * t, jnp.minimum(2 * t + 2, n), inner, 0)
+        return 0
+
+    lax.fori_loop(0, n // 2 + 1, again, 0)
+    wide_pass(n - 1)
+    tall_one.wait_recv()
+    tall_c[tall_at(1 - over, 1)] = (
+        tall[tall_at(2 * core + 1 - over, 1)].astype(f32)
+        + tall_c[tall_at(1 - over, 1)].astype(f32)
+    ).astype(bf16)
+    tall_two.start()
+    for way in range(2):
+        part = slice(way * half, (way + 1) * half)
+        block_out[:, part] = (resid[:, part] + three.result(way)).astype(bf16)
+
+    def wide_take(tile, _):
+        wide_copy_x(tile).wait_recv()
+        wide_sum[tile] = (
+            wide[tile, core, over].astype(f32)
+            + wide_c[tile, over].astype(f32)
+            + wide_sum[tile].astype(f32)
+        ).astype(bf16)
+        return 0
+
+    lax.fori_loop(0, n, wide_take, 0)
+    tall_two.wait_recv()
+    down_sum[...] = (
+        tall[tall_at(2 * core + over, 1)].astype(f32)
+        + tall_c[tall_at(over, 1)].astype(f32)
+        + down_sum[...].astype(f32)
+    ).astype(bf16)
+    gather.finish()
+    back.finish()
+    three.finish()
+    tall_one.wait_send()
+    tall_two.wait_send()
+
+    def sent(tile, _):
+        wide_copy_c(tile).wait_send()
+        wide_copy_x(tile).wait_send()
+        return 0
+
+    lax.fori_loop(0, n, sent, 0)
+
+
+def mlp_and_back(ob, w_out, x_own, gain, weights, lanes, w_down, seed, seed_own):
+    n = lax.axis_size("blk")
+    _, rows, columns = seed.shape
+    head_lanes = ob.shape[2]
+    quarter = columns // (4 * n)
+    f32, bf16 = jnp.float32, jnp.bfloat16
+    vmem, dma = pltpu.VMEM, pltpu.SemaphoreType.DMA
+    in_vmem, anywhere = pl.BlockSpec(memory_space=vmem), pl.BlockSpec(memory_space=pl.ANY)
+    ring = [dma((n - 1, 2, 2))] * 6 + [dma((n // 2, 2, 2))] * 4
+    return pl.pallas_call(
+        functools.partial(mlp_kernel, n, lanes),
+        out_shape=(
+            jax.ShapeDtypeStruct((rows, columns), bf16),
+            jax.ShapeDtypeStruct((rows, columns), f32),
+            jax.ShapeDtypeStruct((n, rows, head_lanes), bf16),
+            jax.ShapeDtypeStruct((1, columns), f32),
+            jax.ShapeDtypeStruct((n, quarter, 2 * lanes), bf16),
+            jax.ShapeDtypeStruct((lanes // 4, columns), bf16),
+            jax.ShapeDtypeStruct((n, rows, columns), bf16),
+        ),
+        in_specs=[in_vmem] * 4 + [anywhere] * 4,
+        out_specs=[in_vmem] * 7,
+        scratch_shapes=[
+            vmem((n, rows, columns), bf16),
+            vmem((n, rows, columns), bf16),
+            vmem((columns, 2 * lanes), bf16),
+            vmem((lanes, columns), bf16),
+            vmem((n, rows, lanes), bf16),
+            vmem((n, rows, 2 * lanes), bf16),
+            vmem((2, n, rows, columns // 2), bf16),
+            vmem((2, n, rows, columns // 2), bf16),
+            vmem((2, rows, columns // 2), f32),
+            vmem((rows, columns), f32),
+            vmem((n, 2, 2, quarter, 2 * lanes), bf16),
+            vmem((n, 2, quarter, 2 * lanes), bf16),
+            vmem((lanes, columns), bf16),
+            vmem((lanes // 2, columns), bf16),
+            dma((4,)),
+        ]
+        + ring
+        + [dma((n,))] * 4
+        + [dma((2,))] * 2,
+        compiler_params=kernel_params(5),
+        name="mlp_and_back",
+    )(ob, w_out, x_own, gain, weights, w_down, seed, seed_own)
+
+
+class Spread:
+    def __init__(self, n, pieces, out, sems):
+        self.n, self.pieces, self.out = n, pieces, out
+        self.s_blk, self.r_blk, self.s_x, self.r_x, self.s_c, self.r_c = sems
+        self.grp, self.me = lax.axis_index("grp"), lax.axis_index("blk")
+        self.over, self.core, self.grp_x, self.grp_c = team(self.grp)
+
+    def first(self, k):
+        to = (self.me + k) % self.n
+        place = self.out.at[self.me, 2 * self.core + self.over]
+        return push(
+            self.pieces.at[to], place, self.s_blk.at[k], self.r_blk.at[k], (self.grp, to)
+        )
+
+    def own(self, sem):
+        place = self.out.at[self.me, 2 * self.core + self.over]
+        return pltpu.make_async_copy(self.pieces.at[self.me], place, sem)
+
+    def to_x(self, k):
+        piece = self.out.at[(self.me - k + self.n) % self.n, 2 * self.core + self.over]
+        return push(piece, piece, self.s_x.at[k], self.r_x.at[k], (self.grp_x, self.me))
+
+    def to_core(self, k, far):
+        over = 1 - self.over if far else self.over
+        piece = self.out.at[(self.me - k + self.n) % self.n, 2 * self.core + over]
+        sems = (self.s_c.at[int(far), k], self.r_c.at[int(far), k])
+        return push(piece, piece, *sems, (self.grp_c, self.me))
+
+    def pass_on(self, k):
+        pl.when(k > 0)(self.first(k).wait_recv)
+        self.to_x(k).start()
+        self.to_core(k, False).start()
+
+    def pass_far(self, k):
+        self.to_x(k).wait_recv()
+        self.to_core(k, True).start()
+
+    def arrived(self, k):
+        for far in (False, True):
+            self.to_core(k, far).wait_recv()
+
+    def finish(self):
+        def body(k, _):
+            pl.when(k > 0)(self.first(k).wait_send)
+            self.to_x(k).wait_send()
+            for far in (False, True):
+                self.to_core(k, far).wait_send()
+            return 0
+
+        lax.fori_loop(0, self.n, body, 0)
+
+
+def each(count, body, low=0):
+    lax.fori_loop(low, count, lambda k, _: (body(k), 0)[1], 0)
+
+
+def spread_sems(n):
+    dma = pltpu.SemaphoreType.DMA
+    return [dma((n,)), dma((n,)), dma((n,)), dma((n,)), dma((2, n)), dma((2, n))]
+
+
+def team_and_ring(n):
+    grp, me = lax.axis_index("grp"), lax.axis_index("blk")
+    _, _, grp_x, grp_c = team(grp)
+    return [(grp, (me + k) % n) for k in range(1, n)] + [(grp_x, me), (grp_c, me)]
+
+
+def fill_row(row, gains_all, which, share):
+    for block in range(gains_all.shape[0]):
+        row[:, block * share : (block + 1) * share] = gains_all[block, which : which + 1, :]
+
+
+def turned(value, cosine, sine_part):
+    half_size = HEAD // 2
+    swapped = jnp.concatenate([value[:, half_size:], value[:, :half_size]], axis=1)
+    return value * cosine + swapped * sine_part
+
+
+def attend_kernel(
+    n,
+    heads,
+    x_own,
+    cosine,
+    sine_part,
+    first_key,
+    query_place,
+    key_place,
+    slab_qkv,
+    slab_gate_up,
+    gains,
+    seed_own,
+    gains_all,
+    columns_qkv,
+    normed,
+    qkv,
+    attended,
+    attended_b,
+    log_total,
+    gate_up,
+    seed,
+    x_all,
+    gain_row,
+    local,
+    s_gain,
+    r_gain,
+    s_x,
+    r_x,
+    s_seed,
+    r_seed,
+    *spread_all,
+):
+    f32, bf16 = jnp.float32, jnp.bfloat16
+    grp, me = lax.axis_index("grp"), lax.axis_index("blk")
+    _, ends = ring_ends(n)
+    rows, columns = x_own.shape
+    spread_qkv = Spread(n, slab_qkv, columns_qkv, spread_all[:6])
+    spread_gu = Spread(n, slab_gate_up, gate_up, spread_all[6:])
+    near_gain = pltpu.make_async_copy(gains, gains_all.at[me], local.at[0])
+    near_gain.start()
+    near_qkv = spread_qkv.own(local.at[1])
+    near_qkv.start()
+    x_all[0] = x_own[...]
+    greet(team_and_ring(n))
+
+    def gain(k):
+        return push(gains, gains_all.at[me], s_gain.at[k], r_gain.at[k], (grp, (me + k) % n))
+
+    each(n, lambda k: gain(k).start(), 1)
+    x_ring = Gather(n, x_all, s_x, r_x, ends)
+    x_ring.start()
+    each(n, lambda k: spread_qkv.first(k).start(), 1)
+    near_gu = spread_gu.own(local.at[2])
+    near_gu.start()
+
+    def norm(slot):
+        value = x_all[slot].astype(f32)
+        inv = lax.rsqrt(jnp.mean(value * value, axis=-1, keepdims=True) + EPS)
+        normed[slot] = (value * inv * gain_row[...]).astype(bf16)
+
+    near_gain.wait()
+    each(n, lambda k: gain(k).wait_recv(), 1)
+    fill_row(gain_row, gains_all, 0, columns // n)
+
+    def arrive(t):
+        pl.when(t > 0)(lambda: x_ring.advance(t - 1))
+        low = jnp.maximum(2 * t - 1, 0)
+        each(jnp.minimum(2 * t + 1, n), norm, low)
+        pl.when(t == 1)(near_qkv.wait)
+        pl.when(t == 2)(lambda: each(n, spread_qkv.pass_on))
+        pl.when(t == 3)(lambda: each(n, spread_qkv.pass_far))
+
+    each(n // 2 + 1, arrive)
+    seed_ring = Gather(n, seed, s_seed, r_seed, ends, seed_own)
+    seed_ring.start()
+    each(n, lambda k: spread_gu.first(k).start(), 1)
+    each(n, spread_qkv.arrived)
+
+    head_lanes = heads * HEAD
+    pair = 2 * rows
+
+    def project(i):
+        both = normed[pl.ds(2 * i, 2)].reshape(pair, columns)
+        result = dot_f32(both, columns_qkv[...].reshape(columns, 3 * head_lanes))
+        at = pl.ds(pl.multiple_of(i * pair, pair), pair)
+        table_c, table_s = cosine[at, :], sine_part[at, :]
+        for piece in range(3 * heads):
+            lane = slice(piece * HEAD, (piece + 1) * HEAD)
+            value = result[:, lane]
+            if piece < 2 * heads:
+                value = turned(value, table_c, table_s)
+            qkv[at, lane] = value.astype(bf16)
+
+    each(n // 2, project)
+    near_gu.wait()
+
+    def tile(i):
+        for head in range(heads):
+            lane = slice(head * HEAD, (head + 1) * HEAD)
+            at = pl.ds(pl.multiple_of(i * pair, pair), pair)
+            keys = qkv[:, head_lanes + head * HEAD : head_lanes + (head + 1) * HEAD]
+            values = qkv[:, 2 * head_lanes + head * HEAD : 2 * head_lanes + (head + 1) * HEAD]
+            scores = nt_dot(qkv[at, lane], keys) * HEAD ** (-0.5)
+            allowed = (key_place[...] >= first_key[at, :]) & (key_place[...] <= query_place[at, :])
+            scores = jnp.where(allowed, scores, NEGATIVE)
+            peak = jnp.max(scores, axis=-1, keepdims=True)
+            raw = jnp.exp(scores - peak)
+            total = jnp.sum(raw, axis=-1, keepdims=True)
+            out = dot_f32(raw.astype(bf16), values) / total
+            attended[at, lane] = out
+            attended_b[at, lane] = out.astype(bf16)
+            log_total[head, at, :] = peak + jnp.log(total)
+        seed_ring.advance(i)
+        each(2 * i + 2, spread_gu.pass_on, 2 * i)
+
+    each(n // 2, tile)
+    each(n, spread_gu.pass_far)
+    each(n, spread_gu.arrived)
+    near_qkv_sent = [spread_qkv, spread_gu]
+    for spread in near_qkv_sent:
+        spread.finish()
+    each(n, lambda k: gain(k).wait_send(), 1)
+    x_ring.finish()
+    seed_ring.finish()
+
+
+def attend(slab_qkv, slab_gate_up, gains, x_own, seed_own, cosine, sine_part, first_key, places):
+    n = lax.axis_size("blk")
+    rows, columns = x_own.shape
+    seq = n * rows
+    lanes = slab_qkv.shape[2]
+    head_lanes = lanes // 3
+    heads = head_lanes // HEAD
+    f32, bf16 = jnp.float32, jnp.bfloat16
+    vmem, dma = pltpu.VMEM, pltpu.SemaphoreType.DMA
+    in_vmem, anywhere = pl.BlockSpec(memory_space=vmem), pl.BlockSpec(memory_space=pl.ANY)
+    return pl.pallas_call(
+        functools.partial(attend_kernel, n, heads),
+        out_shape=(
+            jax.ShapeDtypeStruct((n,) + gains.shape, f32),
+            jax.ShapeDtypeStruct((n, 4) + slab_qkv.shape[1:], bf16),
+            jax.ShapeDtypeStruct((n, rows, columns), bf16),
+            jax.ShapeDtypeStruct((seq, lanes), bf16),
+            jax.ShapeDtypeStruct((seq, head_lanes), f32),
+            jax.ShapeDtypeStruct((seq, head_lanes), bf16),
+            jax.ShapeDtypeStruct((heads, seq, 1), f32),
+            jax.ShapeDtypeStruct((n, 4) + slab_gate_up.shape[1:], bf16),
+            jax.ShapeDtypeStruct((n, rows, columns), bf16),
+        ),
+        in_specs=[in_vmem] * 6 + [anywhere] * 4,
+        out_specs=[in_vmem] * 7 + [anywhere] * 2,
+        scratch_shapes=[
+            vmem((n, rows, columns), bf16),
+            vmem((1, columns), f32),
+            dma((3,)),
+            dma((n,)),
+            dma((n,)),
+        ]
+        + [dma((n // 2, 2, 2))] * 4
+        + spread_sems(n) * 2,
+        compiler_params=kernel_params(0),
+        name="attend",
+    )(
+        x_own,
+        cosine,
+        sine_part,
+        first_key,
+        places.reshape(seq, 1),
+        places.reshape(1, seq),
+        slab_qkv,
+        slab_gate_up,
+        gains,
+        seed_own,
+    )
+
+
+def finish_kernel(
+    n,
+    dqkv,
+    x_own,
+    gain,
+    dresid,
+    terms_two,
+    out_grad,
+    weights,
+    normed_hbm,
+    gate_up_sum,
+    down_sum,
+    x_grad,
+    gain_grads,
+    wide_gate_up,
+    wide_qkv,
+    tall_down,
+    tall_out,
+    normed,
+    columns_qkv,
+    held,
+    terms,
+    wide,
+    wide_c,
+    wide_x,
+    out_c,
+    out_x,
+    gain_slabs,
+    gain_heard,
+    gain_team,
+    load_sem,
+    s_ring,
+    r_ring,
+    s_wc,
+    r_wc,
+    s_wx,
+    r_wx,
+    s_tall,
+    r_tall,
+    s_gain,
+    r_gain,
+    *spread_all,
+):
+    f32, bf16 = jnp.float32, jnp.bfloat16
+    grp, me = lax.axis_index("grp"), lax.axis_index("blk")
+    over, core, grp_x, grp_c = team(grp)
+    _, ends = ring_ends(n)
+    columns = x_own.shape[1]
+    half = columns // 2
+    lanes = wide.shape[4]
+    quarter = wide.shape[3]
+    load_normed = pltpu.make_async_copy(normed_hbm, normed, load_sem.at[0])
+    load_qkv = pltpu.make_async_copy(weights, columns_qkv, load_sem.at[1])
+    load_normed.start()
+    load_qkv.start()
+    spread_gu = Spread(n, gate_up_sum, wide_gate_up, spread_all[:6])
+    spread_qkv = Spread(n, wide_x, wide_qkv, spread_all[6:])
+    near_gu = spread_gu.own(load_sem.at[2])
+    near_gu.start()
+    greet(team_and_ring(n))
+
+    down_own = pltpu.make_async_copy(down_sum, tall_down.at[2 * core + over], load_sem.at[3])
+    down_own.start()
+    down_place = tall_down.at[2 * core + over]
+    down_x = push(down_sum, down_place, s_tall.at[0], r_tall.at[0], (grp_x, me))
+    down_c = push(down_sum, down_place, s_tall.at[1], r_tall.at[1], (grp_c, me))
+    far_place = tall_down.at[2 * core + 1 - over]
+    down_far = push(far_place, far_place, s_tall.at[2], r_tall.at[2], (grp_c, me))
+    out_one = push(out_grad.at[1 - core], out_c, s_tall.at[3], r_tall.at[3], (grp_c, me))
+    out_two = push(out_c.at[1 - over], out_x, s_tall.at[4], r_tall.at[4], (grp_x, me))
+    out_place = tall_out.at[2 * core + over]
+    out_own = pltpu.make_async_copy(out_x, out_place, load_sem.at[4])
+    out_to_x = push(out_x, out_place, s_tall.at[5], r_tall.at[5], (grp_x, me))
+    out_to_c = push(out_x, out_place, s_tall.at[6], r_tall.at[6], (grp_c, me))
+    out_far_place = tall_out.at[2 * core + 1 - over]
+    out_far = push(out_far_place, out_far_place, s_tall.at[7], r_tall.at[7], (grp_c, me))
+    out_one.start()
+
+    load_qkv.wait()
+
+    def term(step, way):
+        return nt_dot(dqkv[behind(step, way, n)], columns_qkv[way * half : (way + 1) * half, :])
+
+    ring = Scatter(n, held, terms, s_ring, r_ring, ends, term)
+
+    def copy_c(k):
+        tile = (me + k) % n
+        return push(wide.at[tile, 1 - core], wide_c.at[tile], s_wc.at[k], r_wc.at[k], (grp_c, me))
+
+    def copy_x(k):
+        tile = (me + k) % n
+        return push(
+            wide_c.at[tile, 1 - over], wide_x.at[tile], s_wx.at[k], r_wx.at[k], (grp_x, me)
+        )
+
+    def grad(k):
+        tile = (me + k) % n
+        at = pl.multiple_of(tile * 4 * quarter, 4 * quarter)
+        left = normed[:, :, pl.ds(at, 4 * quarter)].reshape(-1, 4 * quarter)
+        rows = dot_t(left, dqkv[...].reshape(-1, lanes)).astype(bf16)
+        wide[tile] = rows.reshape(2, 2, quarter, lanes)
+        copy_c(k).start()
+
+    def pass_x(k):
+        tile = (me + k) % n
+        copy_c(k).wait_recv()
+        wide_c[tile, 1 - over] = (
+            wide[tile, core, 1 - over].astype(f32) + wide_c[tile, 1 - over].astype(f32)
+        ).astype(bf16)
+        copy_x(k).start()
+
+    ring.step(0)
+    each(n, lambda k: spread_gu.first(k).start(), 1)
+    out_one.wait_recv()
+    out_c[1 - over] = (
+        out_grad[core, 1 - over].astype(f32) + out_c[1 - over].astype(f32)
+    ).astype(bf16)
+    out_two.start()
+    down_x.start()
+    down_c.start()
+    load_normed.wait()
+    near_gu.wait()
+
+    def turn(k):
+        grad(k)
+        pl.when(k > 0)(lambda: pass_x(k - 1))
+        pl.when(k < n - 2)(lambda: ring.step(k + 1))
+
+    each(n, turn)
+    pass_x(n - 1)
+
+    x_float = x_own[...].astype(f32)
+    inv = lax.rsqrt(jnp.mean(x_float * x_float, axis=-1, keepdims=True) + EPS)
+    for way in range(2):
+        terms[way] = ring.result(way)
+    dnormed = jnp.concatenate([terms[0], terms[1]], axis=1)
+    terms_one = jnp.sum(dnormed * x_float * inv, axis=0, keepdims=True)
+    share = columns // n
+    for block in range(n):
+        gain_slabs[block] = jnp.zeros_like(gain_slabs[block])
+        lane = slice(block * share, (block + 1) * share)
+        gain_slabs[block, 0:1, :] = terms_one[:, lane]
+        gain_slabs[block, 1:2, :] = terms_two[:, lane]
+
+    def gain_blk(k):
+        to = (me + k) % n
+        return push(gain_slabs.at[to], gain_heard.at[k], s_gain.at[k], r_gain.at[k], (grp, to))
+
+    each(n, lambda k: gain_blk(k).start(), 1)
+    a_one = dnormed * gain[...]
+    x_grad[...] = (
+        dresid[...]
+        + inv * a_one
+        - x_float * inv**3 * jnp.mean(a_one * x_float, axis=-1, keepdims=True)
+    ).astype(bf16)
+    each(n, spread_gu.pass_on)
+
+    def take(k):
+        tile = (me + k) % n
+        copy_x(k).wait_recv()
+        wide_x[tile] = (
+            wide[tile, core, over].astype(f32)
+            + wide_c[tile, over].astype(f32)
+            + wide_x[tile].astype(f32)
+        ).astype(bf16)
+
+    def take_and_push(k):
+        take(k)
+        spread_qkv.first(k).start()
+
+    each(n, take_and_push, 1)
+    take(0)
+    near_qkv = spread_qkv.own(load_sem.at[5])
+    near_qkv.start()
+    gain_heard[0] = gain_slabs[me]
+    each(n, lambda k: gain_blk(k).wait_recv(), 1)
+    gain_team[0] = jnp.sum(gain_heard[...], axis=0)
+    gain_c = push(gain_team.at[0], gain_team.at[1], s_gain.at[n], r_gain.at[n], (grp_c, me))
+    gain_c.start()
+    out_two.wait_recv()
+    out_x[...] = (
+        out_grad[core, over].astype(f32) + out_c[over].astype(f32) + out_x[...].astype(f32)
+    ).astype(bf16)
+    out_own.start()
+    out_to_x.start()
+    out_to_c.start()
+    each(n, spread_gu.pass_far)
+    down_x.wait_recv()
+    down_far.start()
+    gain_c.wait_recv()
+    gain_team[2] = gain_team[0] + gain_team[1]
+    gain_x = push(
+        gain_team.at[2], gain_team.at[3], s_gain.at[n + 1], r_gain.at[n + 1], (grp_x, me)
+    )
+    gain_x.start()
+    near_qkv.wait()
+    each(n, spread_qkv.pass_on)
+    out_to_x.wait_recv()
+    out_far.start()
+    each(n, spread_qkv.pass_far)
+    gain_x.wait_recv()
+    gain_grads[...] = gain_team[2] + gain_team[3]
+    each(n, spread_gu.arrived)
+    each(n, spread_qkv.arrived)
+    spread_gu.finish()
+    spread_qkv.finish()
+    ring.finish()
+    down_own.wait()
+    out_own.wait()
+    for copy in (down_c, down_far, out_to_c, out_far):
+        copy.wait()
+    for copy in (down_x, out_one, out_two, out_to_x, gain_c, gain_x):
+        copy.wait_send()
+
+    def sent(k):
+        copy_c(k).wait_send()
+        copy_x(k).wait_send()
+        pl.when(k > 0)(gain_blk(k).wait_send)
+
+    each(n, sent)
+
+
+def finish(
+    dqkv, x_own, gain, dresid, terms_two, out_grad, weights, normed, gate_up_sum, down_sum
+):
+    n, rows, columns = normed.shape
+    lanes = dqkv.shape[2]
+    quarter = columns // (4 * n)
+    share = columns // n
+    f32, bf16 = jnp.float32, jnp.bfloat16
+    vmem, dma = pltpu.VMEM, pltpu.SemaphoreType.DMA
+    in_vmem, anywhere = pl.BlockSpec(memory_space=vmem), pl.BlockSpec(memory_space=pl.ANY)
+    out_rows = out_grad.shape[0] // 4
+    return pl.pallas_call(
+        functools.partial(finish_kernel, n),
+        out_shape=(
+            jax.ShapeDtypeStruct((rows, columns), bf16),
+            jax.ShapeDtypeStruct((8, share), f32),
+            jax.ShapeDtypeStruct((n, 4) + gate_up_sum.shape[1:], bf16),
+            jax.ShapeDtypeStruct((n, 4, quarter, lanes), bf16),
+            jax.ShapeDtypeStruct((4,) + down_sum.shape, bf16),
+            jax.ShapeDtypeStruct((4, out_rows, columns), bf16),
+        ),
+        in_specs=[in_vmem] * 6 + [anywhere] * 4,
+        out_specs=[in_vmem] * 2 + [anywhere] * 4,
+        scratch_shapes=[
+            vmem((n, rows, columns), bf16),
+            vmem((columns, lanes), bf16),
+            vmem((2, n, rows, columns // 2), bf16),
+            vmem((2, rows, columns // 2), f32),
+            vmem((n, 2, 2, quarter, lanes), bf16),
+            vmem((n, 2, quarter, lanes), bf16),
+            vmem((n, quarter, lanes), bf16),
+            vmem((2, out_rows, columns), bf16),
+            vmem((out_rows, columns), bf16),
+            vmem((n, 8, share), f32),
+            vmem((n, 8, share), f32),
+            vmem((4, 8, share), f32),
+            dma((6,)),
+        ]
+        + [dma((n - 1, 2, 2))] * 2
+        + [dma((n,))] * 4
+        + [dma((8,))] * 2
+        + [dma((n + 2,))] * 2
+        + spread_sems(n) * 2,
+        compiler_params=kernel_params(6),
+        name="finish",
+    )(
+        dqkv,
+        x_own,
+        gain,
+        dresid,
+        terms_two,
+        out_grad.reshape(2, 2, out_rows, columns),
+        weights,
+        normed,
+        gate_up_sum,
+        down_sum,
+    )
+
+
+def assemble_kernel(n, units, lanes, head_lanes, qkv, gate_up, down, out, *grads):
+    grad_qkv, grad_out, grad_gate, grad_up, grad_down = grads
+    f32 = jnp.float32
+    for source in range(n):
+        for part in range(3):
+            first = (part * n + source) * head_lanes
+            grad_qkv[:, first : first + head_lanes] = qkv[
+                source, :, part * head_lanes : (part + 1) * head_lanes
+            ].astype(f32)
+        first = source * units
+        grad_gate[:, first : first + units] = gate_up[source, :, :units].astype(f32)
+        grad_up[:, first : first + units] = gate_up[source, :, lanes : lanes + units].astype(f32)
+    grad_out[...] = out[...].astype(f32)
+    grad_down[...] = down[...].astype(f32)
+
+
+def assemble(qkv, gate_up, down, out, units, steps=4):
+    n, rows, qkv_lanes = qkv.shape
+    columns = down.shape[1]
+    lanes = gate_up.shape[2] // 2
+    head_lanes = qkv_lanes // 3
+    step = rows // steps
+    down_step = units // steps
+    f32 = jnp.float32
+
+    def wide(width):
+        return pl.BlockSpec((n, step, width), lambda i: (0, i, 0))
+
+    def flat(height, width):
+        return pl.BlockSpec((height, width), lambda i: (i, 0))
+
+    return pl.pallas_call(
+        functools.partial(assemble_kernel, n, units, lanes, head_lanes),
+        grid=(steps,),
+        out_shape=(
+            jax.ShapeDtypeStruct((rows, n * qkv_lanes), f32),
+            jax.ShapeDtypeStruct((rows, columns), f32),
+            jax.ShapeDtypeStruct((rows, n * units), f32),
+            jax.ShapeDtypeStruct((rows, n * units), f32),
+            jax.ShapeDtypeStruct((units, columns), f32),
+        ),
+        in_specs=[
+            wide(qkv_lanes),
+            wide(2 * lanes),
+            flat(down_step, columns),
+            flat(out.shape[0] // steps, columns),
+        ],
+        out_specs=[
+            flat(step, n * qkv_lanes),
+            flat(step, columns),
+            flat(step, n * units),
+            flat(step, n * units),
+            flat(down_step, columns),
+        ],
+        compiler_params=pltpu.CompilerParams(vmem_limit_bytes=VMEM_BYTES),
+        name="assemble",
+    )(qkv, gate_up, down, out)
+
+
+def pad_to(array, axis, size):
+    widths = [(0, 0)] * array.ndim
+    widths[axis] = (0, size - array.shape[axis])
+    return jnp.pad(array, widths)
+
+
+def per_device(block_input, doc_lens, norm_attn, w_qkv, w_out, norm_mlp, w_gate, w_up, w_down, cot):
+    n = lax.axis_size("blk")
+    tok_rows, width = block_input.shape[1:]
+    seq = tok_rows * n
+    heads = HEADS // n
+    head_lanes = heads * HEAD
+    qkv_lanes = 3 * head_lanes
+    score_scale = HEAD ** (-0.5)
+    units = w_down.shape[0]
+    lanes = -(-units // 128) * 128
+    bf16 = jnp.bfloat16
+
+    over, core, _, _ = team(lax.axis_index("grp"))
+    quarter = w_qkv.shape[0] // 4
+    first_row = (2 * core + over) * quarter
+
+    def quarter_of(weight):
+        return lax.dynamic_slice_in_dim(weight, first_row, quarter, 0)
+
+    slab_qkv = (
+        quarter_of(w_qkv)
+        .reshape(quarter, 3, n, head_lanes)
+        .transpose(2, 0, 1, 3)
+        .reshape(n, quarter, qkv_lanes)
+    )
+    slab_gate_up = jnp.concatenate(
+        [
+            pad_to(quarter_of(w).reshape(quarter, n, units).transpose(1, 0, 2), 2, lanes)
+            for w in (w_gate, w_up)
+        ],
+        axis=2,
+    )
+    gains = pad_to(jnp.stack([norm_attn, norm_mlp]).astype(jnp.float32), 0, 8)
+    place = ring_place(lax.axis_index("blk"), n)
+    offsets = [0] + [k * sign for k in range(1, n // 2) for sign in (-1, 1)] + [n // 2]
+    blocks = jnp.stack([at_offset(place, offset, n) for offset in offsets])
+    places = (blocks[:, None] * tok_rows + jnp.arange(tok_rows, dtype=jnp.int32)).reshape(seq)
+    lengths = doc_lens[0]
+    starts = jnp.cumsum(lengths) - lengths
+    first_key = start_of(places, starts)
+    half_cosine, half_sine = angle_tables(places - first_key)
+    half_cosine, half_sine = half_cosine[:, 0], half_sine[:, 0]
+    cosine = jnp.concatenate([half_cosine, half_cosine], axis=1)
+    sine_part = jnp.concatenate([-half_sine, half_sine], axis=1)
+    gains_all, qkv_columns, normed_one, qkv, attended, attended_b, log_total, gate_up, seed = attend(
+        slab_qkv,
+        slab_gate_up,
+        gains,
+        block_input[0],
+        cot[0],
+        cosine,
+        sine_part,
+        first_key.reshape(seq, 1),
+        places,
+    )
+    gain_one = gains_all[:, 0].reshape(1, width)
+    gain_two = gains_all[:, 1].reshape(1, width)
+    qkv_columns = qkv_columns.reshape(width, qkv_lanes)
+    gate_up = gate_up.reshape(width, 2 * lanes)
+    block_out, dresid, dattended, terms_two, gate_up_sum, down_sum, dresid_b = mlp_and_back(
+        attended_b.reshape(n, tok_rows, head_lanes),
+        w_out,
+        block_input[0],
+        gain_two,
+        gate_up,
+        lanes,
+        w_down,
+        seed,
+        cot[0],
+    )
+    dattended = dattended.reshape(seq, heads, HEAD)
+    out_grad = dot_t(attended_b, dresid_b.reshape(seq, width)).astype(bf16)
+    delta = jnp.sum(
+        dattended.astype(jnp.float32) * attended.reshape(seq, heads, HEAD), axis=-1
+    ).T
+    queries, keys, values = qkv.reshape(seq, 3, heads, HEAD).transpose(1, 0, 2, 3)
+    allowed = (places[None, :] >= first_key[:, None]) & (places[None, :] <= places[:, None])
+    scores = (
+        jnp.einsum("qhd,khd->hqk", queries, keys, preferred_element_type=jnp.float32) * score_scale
+    )
+    probs = jnp.where(allowed[None], jnp.exp(scores - log_total), 0.0)
+    dprobs = jnp.einsum("qhd,khd->hqk", dattended, values, preferred_element_type=jnp.float32)
+    dscores = (probs * (dprobs - delta[..., None])).astype(bf16)
+    dquery = score_scale * jnp.einsum(
+        "hqk,khd->qhd", dscores, keys, preferred_element_type=jnp.float32
+    )
+    dkey = score_scale * jnp.einsum(
+        "hqk,qhd->khd", dscores, queries, preferred_element_type=jnp.float32
+    )
+    dvalue = jnp.einsum(
+        "hqk,qhd->khd", probs.astype(bf16), dattended, preferred_element_type=jnp.float32
+    )
+    dqkv = (
+        jnp.stack(
+            [
+                unrotate(dquery, half_cosine[:, None], half_sine[:, None]),
+                unrotate(dkey, half_cosine[:, None], half_sine[:, None]),
+                dvalue,
+            ],
+            axis=1,
+        )
+        .reshape(n, tok_rows, qkv_lanes)
+        .astype(bf16)
+    )
+    x_grad, gain_grads, wide_gate_up, wide_qkv, tall_down, tall_out = finish(
+        dqkv,
+        block_input[0],
+        gain_one,
+        dresid,
+        terms_two,
+        out_grad,
+        qkv_columns,
+        normed_one,
+        gate_up_sum,
+        down_sum,
+    )
+    shard_rows = 4 * quarter
+    grad_qkv, grad_out, grad_gate, grad_up, grad_down = assemble(
+        wide_qkv.reshape(n, shard_rows, qkv_lanes),
+        wide_gate_up.reshape(n, shard_rows, 2 * lanes),
+        tall_down.reshape(lanes, width),
+        tall_out.reshape(head_lanes, width),
+        units,
+    )
+    return (
+        block_out[None],
+        x_grad[None],
+        gain_grads[0],
+        grad_qkv,
+        grad_out,
+        gain_grads[1],
+        grad_gate,
+        grad_up,
+        grad_down,
+    )
+
+
+def body_for(mesh):
+    return per_device if HEADS % mesh.shape["blk"] == 0 else per_device_gather
+
+
 def solution(mesh):
     return jax.shard_map(
-        per_device,
+        body_for(mesh),
         mesh=mesh,
         in_specs=(
             P("grp", "blk", None),

time: 4400 us -> 614 us (0.14)
  waiting for transfers between devices: 4020 us -> 0 us
  Pallas kernels: 0 us -> 553 us
  matrix products: 207 us -> 14.2 us
    all_gather x7 -> x0, waiting for transfers between devices: 2000 us -> none  [the longest x1 461 us: per_device(): lax.all_gather(shards[1], 'blk', axis=0, tiled=True)]
    reduce_scatter x5 -> x0, waiting for transfers between devices: 1650 us -> none  [shard_grad(): lax.psum_scatter(term_fn(jnp.int32(0), shard_rows * lax.axis_size('blk'))...]
    pallas_call x0 -> x4, Pallas kernels: none -> 553 us  [the longest x1 238 us: mlp_and_back(): pl.pallas_call(functools.partial(mlp_kernel, n, lanes), out_shape=(jax.Sh...]
    psum x1 -> x0, waiting for transfers between devices: 221 us -> none  [shard_grad(): return lax.psum(shared, 'grp').astype(jnp.float32)]
    dot_general x20 -> x5, matrix products: 204 us -> 13.4 us  [the longest x1 4.43 us: dot_t(): lax.dot_general(left, right, (((0,), (0,)), ((), ())), preferred_element_...]
    unnamed x17 -> x0, waiting for transfers between devices: 152 us -> none
  transfers between devices with their start and end apart: 15 -> 0, of which waited for: 15 -> 0; matrix products, arithmetic and copies ran while one was open for 3% -> 0% of each run, Pallas kernels for 0% -> 0%
where the time goes in v3:
time: 614 us; the launch traced here: 605 us
  Pallas kernels  553 us (90%)
  local copies, waits for them, and re-layouts  24.3 us (4%)
  matrix products  14.2 us (2%)
  other arithmetic  12.1 us (2%)
    pallas_call x1, Pallas kernels, mlp_and_back(): pl.pallas_call(functools.partial(mlp_kernel, n, lanes), out_shape=(jax.Sh...  238 us
    pallas_call x1, Pallas kernels, attend(): pl.pallas_call(functools.partial(attend_kernel, n, heads), out_shape=(jax...  158 us
    pallas_call x1, Pallas kernels, finish(): pl.pallas_call(functools.partial(finish_kernel, n), out_shape=(jax.ShapeD...  145 us
    pallas_call x1, Pallas kernels, assemble(): pl.pallas_call(functools.partial(assemble_kernel, n, units, lanes, head_l...  13.1 us

profile of v3, /device:TPU:1, one launch (start us, length us, event | category | flops | bytes accessed | tf_op | source)
XLA Modules:
  0.0 605.4 jit_solution(9718932803529978452)
XLA Ops:
  1.0 0.1 stack.60
  1.1 0.8 reduce-window_clone.1
  1.9 0.7 subtract_bitcast_fusion
  2.6 0.7 stack.61
  3.3 0.7 stack.62
  3.9 0.6 fusion.20.gains
  4.5 0.1 iota_add_fusion
  4.6 0.0 copy-start.4
  4.6 0.1 select_reduce_fusion
  4.7 0.1 subtract_convert_fusion.2
  4.8 1.0 copy.72.first_key
  5.8 1.0 copy.73.query_place
  6.8 1.2 constant_dynamic-slice_fusion.2
  8.0 0.2 copy.86
  8.2 0.4 copy.69
  8.6 1.7 reshape.311.slab_qkv
  10.3 1.9 compare_and_fusion
  12.2 0.0 copy-done.4
  12.2 1.4 constant_dynamic-slice_fusion
  13.6 0.7 reshape.313
  14.3 0.1 copy.92
  14.4 0.7 reshape.312
  15.1 0.1 copy.93
  15.2 1.3 fusion.6.slab_gate_up
  16.5 1.9 fusion.16
  18.4 0.2 copy.79
  18.6 1.3 pad_maximum_fusion.1
  19.9 0.2 copy.78
  20.1 157.8 %attend.1 = (f32[8,8,256]{2,1,0:T(8,128)}, bf16[8,4,64,768]{3,2,1,0:T(8,128)(2,1)}, bf16[8,128,2048]{2,1,0:T(8,128)(2,1)}, bf16[1024,768]{1,0:T(8,128)(2,1)}, f3...) custom-call(bf16[128,2048]{1,0:T(8,128)(2,1)} %bitcast.92, ...), custom_call_target="tpu_custom_call" | custom-call | tf_op jit(solution)/shard_map/attend/pallas_call | solution.py:967
  177.9 1.5 fusion.24
  179.5 0.0 copy-start.1
  179.5 237.6 %mlp_and_back.1 = (bf16[128,2048]{1,0:T(8,128)(2,1)}, f32[128,2048]{1,0:T(8,128)}, bf16[8,128,256]{2,1,0:T(8,128)(2,1)}, f32[1,2048]{1,0:T(1,128)}, bf16[8,64,15...) custom-call(bf16[8,128,256]{2,1,0:T(8,128)(2,1)} %bitcast.107, ...), custom_call_target="tpu_custom_call" | custom-call | tf_op jit(solution)/shard_map/mlp_and_back/pallas_call | solution.py:714
  417.1 1.6 reduce
  418.7 1.2 reshape.317
  419.8 0.6 copy.81
  420.5 0.0 copy-done.1
  420.5 4.4 convolution_convert_fusion
  424.9 1.7 reshape.318
  426.7 1.2 multiply_reduce_fusion
  427.8 0.2 copy.76
  428.0 3.4 reshape.316
  431.4 0.2 copy.91
  431.6 0.0 copy-start
  431.6 1.3 fusion.15
  432.9 0.0 copy-done
  432.9 2.4 fusion.12
  435.3 3.8 multiply_convert_fusion
  439.1 0.8 fusion.7
  439.9 1.5 fusion.8
  441.4 0.4 add_convert_fusion.1
  441.9 0.2 pad_maximum_fusion
  442.1 0.4 copy.87
  442.5 1.8 copy.85.dqkv
  444.4 144.6 %finish.1 = (bf16[128,2048]{1,0:T(8,128)(2,1)}, f32[8,256]{1,0:T(8,128)}, bf16[8,4,64,1536]{3,2,1,0:T(8,128)(2,1)}, bf16[8,4,64,768]{3,2,1,0:T(8,128)(2,1)}, bf1...) custom-call(bf16[8,128,768]{2,1,0:T(8,128)(2,1)} %copy.85.dqkv, bf16[128,2048]{1,0:T(8,128)(2,1)} %bitcast.94, ...), custom_call_target="tpu_custom_call" | custom-call | tf_op jit(solution)/shard_map/finish/pallas_call | solution.py:1240
  588.9 1.3 fusion.25
  590.3 0.0 copy-start.2
  590.3 0.0 copy-start.3
  590.3 13.1 %assemble.1 = (f32[256,6144]{1,0:T(8,128)}, f32[256,2048]{1,0:T(8,128)}, f32[256,5632]{1,0:T(8,128)}, f32[256,5632]{1,0:T(8,128)}, f32[704,2048]{1,0:T(8,128)}) custom-call(bf16[8,256,768]{2,1,0:T(8,128)(2,1)} %bitcast.100, bf16[8,256,1536]{2,1,0:T(8,128)(2,1)} %bitcast.91, bf16[768,2048]{1,0:T(8,128)(2,1)} %bitcast.101, bf16[256,2048]{1,0:T(8,128)(2,1)} %bitcast.106), custom_call_target="tpu_custom_call" | custom-call | tf_op jit(solution)/shard_map/assemble/pallas_call | solution.py:1319
  603.4 0.0 copy-done.2
  603.4 0.8 copy.96
  604.2 0.0 copy-done.3
  604.2 0.8 copy.97
  (4 shorter events, 0.1 us)
Async XLA Ops:
  4.6 7.6 %copy-start.4 = (s32[8,128]{1,0:T(8,128)}, s32[8,128]{1,0:T(8,128)S(1)}, u32[]{:S(2)}) copy-start(s32[8,128]{1,0:T(8,128)S(1)} %get-tuple-element.76) | copy-start | bytes 12292
  179.5 241.0 %copy-start.1 = (bf16[1024,256]{1,0:T(8,128)(2,1)S(1)}, bf16[1024,256]{1,0:T(8,128)(2,1)}, u32[]{:S(2)}) copy-start(bf16[1024,256]{1,0:T(8,128)(2,1)} %get-tuple-element.36) | copy-start | bytes 1572868
  431.6 1.3 copy-start
  590.3 13.1 %copy-start.2 = (bf16[128,2048]{1,0:T(8,128)(2,1)S(1)}, bf16[128,2048]{1,0:T(8,128)(2,1)}, u32[]{:S(2)}) copy-start(bf16[128,2048]{1,0:T(8,128)(2,1)} %get-tuple-element.40) | copy-start | bytes 1572868
  590.3 13.9 %copy-start.3 = (bf16[128,2048]{1,0:T(8,128)(2,1)S(1)}, bf16[128,2048]{1,0:T(8,128)(2,1)}, u32[]{:S(2)}) copy-start(bf16[128,2048]{1,0:T(8,128)(2,1)} %get-tuple-element.52) | copy-start | bytes 1572868

commit v4 on v3

--- a/solution.py
+++ b/solution.py
@@ -468,6 +468,7 @@
     gain_terms,
     wide_sum,
     down_sum,
+    out_grad,
     dresid,
     normed,
     seed,
@@ -668,6 +669,9 @@
         + tall_c[tall_at(1 - over, 1)].astype(f32)
     ).astype(bf16)
     tall_two.start()
+    out_grad[...] = dot_t(
+        ob[...].reshape(-1, ob.shape[2]), dresid[...].reshape(-1, columns)
+    ).astype(bf16)
     for way in range(2):
         part = slice(way * half, (way + 1) * half)
         block_out[:, part] = (resid[:, part] + three.result(way)).astype(bf16)
@@ -720,11 +724,12 @@
             jax.ShapeDtypeStruct((1, columns), f32),
             jax.ShapeDtypeStruct((n, quarter, 2 * lanes), bf16),
             jax.ShapeDtypeStruct((lanes // 4, columns), bf16),
-            jax.ShapeDtypeStruct((n, rows, columns), bf16),
+            jax.ShapeDtypeStruct((head_lanes, columns), bf16),
         ),
         in_specs=[in_vmem] * 4 + [anywhere] * 4,
         out_specs=[in_vmem] * 7,
         scratch_shapes=[
+            vmem((n, rows, columns), bf16),
             vmem((n, rows, columns), bf16),
             vmem((n, rows, columns), bf16),
             vmem((columns, 2 * lanes), bf16),
@@ -1006,7 +1011,16 @@
 
 def finish_kernel(
     n,
-    dqkv,
+    heads,
+    qkv,
+    attended,
+    dattended,
+    log_total,
+    cosine,
+    sine_part,
+    first_key,
+    query_place,
+    key_place,
     x_own,
     gain,
     dresid,
@@ -1024,6 +1038,9 @@
     tall_out,
     normed,
     columns_qkv,
+    dqkv,
+    dkeys,
+    dvalues,
     held,
     terms,
     wide,
@@ -1051,7 +1068,7 @@
     grp, me = lax.axis_index("grp"), lax.axis_index("blk")
     over, core, grp_x, grp_c = team(grp)
     _, ends = ring_ends(n)
-    columns = x_own.shape[1]
+    rows, columns = x_own.shape
     half = columns // 2
     lanes = wide.shape[4]
     quarter = wide.shape[3]
@@ -1081,7 +1098,49 @@
     out_far_place = tall_out.at[2 * core + 1 - over]
     out_far = push(out_far_place, out_far_place, s_tall.at[7], r_tall.at[7], (grp_c, me))
     out_one.start()
-
+    each(n, lambda k: spread_gu.first(k).start(), 1)
+    down_x.start()
+    down_c.start()
+
+    pair = 2 * rows
+    head_lanes = heads * HEAD
+    scale = HEAD ** (-0.5)
+
+    def unturned(value, at):
+        return turned(value, cosine[at, :], -sine_part[at, :]).astype(bf16)
+
+    def tile(i, head):
+        at = pl.ds(pl.multiple_of(i * pair, pair), pair)
+        lane = slice(head * HEAD, (head + 1) * HEAD)
+        query = qkv[at, lane]
+        keys = qkv[:, head_lanes + head * HEAD : head_lanes + (head + 1) * HEAD]
+        values = qkv[:, 2 * head_lanes + head * HEAD : 2 * head_lanes + (head + 1) * HEAD]
+        grad = dattended[at, lane]
+        delta = jnp.sum(grad.astype(f32) * attended[at, lane], axis=-1, keepdims=True)
+        scores = nt_dot(query, keys) * scale
+        allowed = (key_place[...] >= first_key[at, :]) & (key_place[...] <= query_place[at, :])
+        probs = jnp.where(allowed, jnp.exp(scores - log_total[head, at, :]), 0.0)
+        dscores = (probs * (nt_dot(grad, values) - delta)).astype(bf16)
+        dqkv[2 * i : 2 * i + 2, :, lane] = unturned(dot_f32(dscores, keys) * scale, at).reshape(
+            2, rows, HEAD
+        )
+        more_keys = dot_t(dscores, query)
+        more_values = dot_t(probs.astype(bf16), grad)
+        if i == 0:
+            dkeys[...] = more_keys
+            dvalues[...] = more_values
+        else:
+            dkeys[...] += more_keys
+            dvalues[...] += more_values
+
+    for head in range(heads):
+        for i in range(n // 2):
+            tile(i, head)
+        everything = slice(0, n * rows)
+        lane = slice(head_lanes + head * HEAD, head_lanes + (head + 1) * HEAD)
+        dqkv[:, :, lane] = unturned(dkeys[...] * scale, everything).reshape(n, rows, HEAD)
+        lane = slice(2 * head_lanes + head * HEAD, 2 * head_lanes + (head + 1) * HEAD)
+        dqkv[:, :, lane] = dvalues[...].astype(bf16).reshape(n, rows, HEAD)
     load_qkv.wait()
 
     def term(step, way):
@@ -1103,8 +1162,8 @@
         tile = (me + k) % n
         at = pl.multiple_of(tile * 4 * quarter, 4 * quarter)
         left = normed[:, :, pl.ds(at, 4 * quarter)].reshape(-1, 4 * quarter)
-        rows = dot_t(left, dqkv[...].reshape(-1, lanes)).astype(bf16)
-        wide[tile] = rows.reshape(2, 2, quarter, lanes)
+        grad_rows = dot_t(left, dqkv[...].reshape(-1, lanes)).astype(bf16)
+        wide[tile] = grad_rows.reshape(2, 2, quarter, lanes)
         copy_c(k).start()
 
     def pass_x(k):
@@ -1116,14 +1175,11 @@
         copy_x(k).start()
 
     ring.step(0)
-    each(n, lambda k: spread_gu.first(k).start(), 1)
     out_one.wait_recv()
     out_c[1 - over] = (
         out_grad[core, 1 - over].astype(f32) + out_c[1 - over].astype(f32)
     ).astype(bf16)
     out_two.start()
-    down_x.start()
-    down_c.start()
     load_normed.wait()
     near_gu.wait()
 
@@ -1131,6 +1187,7 @@
         grad(k)
         pl.when(k > 0)(lambda: pass_x(k - 1))
         pl.when(k < n - 2)(lambda: ring.step(k + 1))
+        spread_gu.pass_on(k)
 
     each(n, turn)
     pass_x(n - 1)
@@ -1159,8 +1216,6 @@
         + inv * a_one
         - x_float * inv**3 * jnp.mean(a_one * x_float, axis=-1, keepdims=True)
     ).astype(bf16)
-    each(n, spread_gu.pass_on)
-
     def take(k):
         tile = (me + k) % n
         copy_x(k).wait_recv()
@@ -1227,10 +1282,11 @@
 
 
 def finish(
-    dqkv, x_own, gain, dresid, terms_two, out_grad, weights, normed, gate_up_sum, down_sum
+    attention, x_own, gain, dresid, terms_two, out_grad, weights, normed, gate_up_sum, down_sum
 ):
     n, rows, columns = normed.shape
-    lanes = dqkv.shape[2]
+    seq, lanes = attention[0].shape
+    heads = lanes // (3 * HEAD)
     quarter = columns // (4 * n)
     share = columns // n
     f32, bf16 = jnp.float32, jnp.bfloat16
@@ -1238,7 +1294,7 @@
     in_vmem, anywhere = pl.BlockSpec(memory_space=vmem), pl.BlockSpec(memory_space=pl.ANY)
     out_rows = out_grad.shape[0] // 4
     return pl.pallas_call(
-        functools.partial(finish_kernel, n),
+        functools.partial(finish_kernel, n, heads),
         out_shape=(
             jax.ShapeDtypeStruct((rows, columns), bf16),
             jax.ShapeDtypeStruct((8, share), f32),
@@ -1247,11 +1303,14 @@
             jax.ShapeDtypeStruct((4,) + down_sum.shape, bf16),
             jax.ShapeDtypeStruct((4, out_rows, columns), bf16),
         ),
-        in_specs=[in_vmem] * 6 + [anywhere] * 4,
+        in_specs=[in_vmem] * 14 + [anywhere] * 4,
         out_specs=[in_vmem] * 2 + [anywhere] * 4,
         scratch_shapes=[
             vmem((n, rows, columns), bf16),
             vmem((columns, lanes), bf16),
+            vmem((n, rows, lanes), bf16),
+            vmem((seq, HEAD), f32),
+            vmem((seq, HEAD), f32),
             vmem((2, n, rows, columns // 2), bf16),
             vmem((2, rows, columns // 2), f32),
             vmem((n, 2, 2, quarter, lanes), bf16),
@@ -1272,7 +1331,7 @@
         compiler_params=kernel_params(6),
         name="finish",
     )(
-        dqkv,
+        *attention,
         x_own,
         gain,
         dresid,
@@ -1357,7 +1416,6 @@
     heads = HEADS // n
     head_lanes = heads * HEAD
     qkv_lanes = 3 * head_lanes
-    score_scale = HEAD ** (-0.5)
     units = w_down.shape[0]
     lanes = -(-units // 128) * 128
     bf16 = jnp.bfloat16
@@ -1391,6 +1449,7 @@
     starts = jnp.cumsum(lengths) - lengths
     first_key = start_of(places, starts)
     half_cosine, half_sine = angle_tables(places - first_key)
+    first_key = first_key.reshape(seq, 1)
     half_cosine, half_sine = half_cosine[:, 0], half_sine[:, 0]
     cosine = jnp.concatenate([half_cosine, half_cosine], axis=1)
     sine_part = jnp.concatenate([-half_sine, half_sine], axis=1)
@@ -1402,14 +1461,14 @@
         cot[0],
         cosine,
         sine_part,
-        first_key.reshape(seq, 1),
+        first_key,
         places,
     )
     gain_one = gains_all[:, 0].reshape(1, width)
     gain_two = gains_all[:, 1].reshape(1, width)
     qkv_columns = qkv_columns.reshape(width, qkv_lanes)
     gate_up = gate_up.reshape(width, 2 * lanes)
-    block_out, dresid, dattended, terms_two, gate_up_sum, down_sum, dresid_b = mlp_and_back(
+    block_out, dresid, dattended, terms_two, gate_up_sum, down_sum, out_grad = mlp_and_back(
         attended_b.reshape(n, tok_rows, head_lanes),
         w_out,
         block_input[0],
@@ -1420,42 +1479,18 @@
         seed,
         cot[0],
     )
-    dattended = dattended.reshape(seq, heads, HEAD)
-    out_grad = dot_t(attended_b, dresid_b.reshape(seq, width)).astype(bf16)
-    delta = jnp.sum(
-        dattended.astype(jnp.float32) * attended.reshape(seq, heads, HEAD), axis=-1
-    ).T
-    queries, keys, values = qkv.reshape(seq, 3, heads, HEAD).transpose(1, 0, 2, 3)
-    allowed = (places[None, :] >= first_key[:, None]) & (places[None, :] <= places[:, None])
-    scores = (
-        jnp.einsum("qhd,khd->hqk", queries, keys, preferred_element_type=jnp.float32) * score_scale
-    )
-    probs = jnp.where(allowed[None], jnp.exp(scores - log_total), 0.0)
-    dprobs = jnp.einsum("qhd,khd->hqk", dattended, values, preferred_element_type=jnp.float32)
-    dscores = (probs * (dprobs - delta[..., None])).astype(bf16)
-    dquery = score_scale * jnp.einsum(
-        "hqk,khd->qhd", dscores, keys, preferred_element_type=jnp.float32
-    )
-    dkey = score_scale * jnp.einsum(
-        "hqk,qhd->khd", dscores, queries, preferred_element_type=jnp.float32
-    )
-    dvalue = jnp.einsum(
-        "hqk,qhd->khd", probs.astype(bf16), dattended, preferred_element_type=jnp.float32
-    )
-    dqkv = (
-        jnp.stack(
-            [
-                unrotate(dquery, half_cosine[:, None], half_sine[:, None]),
-                unrotate(dkey, half_cosine[:, None], half_sine[:, None]),
-                dvalue,
-            ],
-            axis=1,
-        )
-        .reshape(n, tok_rows, qkv_lanes)
-        .astype(bf16)
-    )
     x_grad, gain_grads, wide_gate_up, wide_qkv, tall_down, tall_out = finish(
-        dqkv,
+        (
+            qkv,
+            attended,
+            dattended.reshape(seq, head_lanes),
+            log_total,
+            cosine,
+            sine_part,
+            first_key,
+            places.reshape(seq, 1),
+            places.reshape(1, seq),
+        ),
         block_input[0],
         gain_one,
         dresid,

time: 614 us -> 556 us (0.906); the launches traced: 605 us -> 555 us
  Pallas kernels: 553 us -> 532 us
  matrix products: 14.2 us -> 0 us
  local copies, waits for them, and re-layouts: 24.3 us -> 14.4 us
    pallas_call x1, Pallas kernels: 145 us -> 125 us  [finish(): pl.pallas_call(functools.partial(finish_kernel, n, heads), out_shape=(jax...]
    dot_general x6 -> x0, matrix products: 14.2 us -> none  [the longest x1 4.43 us: dot_t(): lax.dot_general(left, right, (((0,), (0,)), ((), ())), preferred_element_...]
    reshape x5 -> x0, local copies, waits for them, and re-layouts: 7.1 us -> none  [the longest x2 3.56 us: per_device(): qkv.reshape(seq, 3, heads, HEAD).transpose(1, 0, 2, 3)]
where the time goes in v4:
time: 556 us; the launch traced here: 555 us
  Pallas kernels  532 us (96%)
  local copies, waits for them, and re-layouts  14.4 us (3%)
  other arithmetic  6.84 us (1%)
    pallas_call x1, Pallas kernels, mlp_and_back(): pl.pallas_call(functools.partial(mlp_kernel, n, lanes), out_shape=(jax.Sh...  237 us
    pallas_call x1, Pallas kernels, attend(): pl.pallas_call(functools.partial(attend_kernel, n, heads), out_shape=(jax...  158 us
    pallas_call x1, Pallas kernels, finish(): pl.pallas_call(functools.partial(finish_kernel, n, heads), out_shape=(jax...  125 us
    pallas_call x1, Pallas kernels, assemble(): pl.pallas_call(functools.partial(assemble_kernel, n, units, lanes, head_l...  13.1 us

profile of v4, /device:TPU:1, one launch (start us, length us, event | category | flops | bytes accessed | tf_op | source)
XLA Modules:
  0.0 554.6 jit_solution(10581284184042441581)
XLA Ops:
  1.0 0.1 stack.44
  1.1 0.8 reduce-window_clone.1
  1.9 0.7 subtract_bitcast_fusion
  2.6 0.7 stack.45
  3.3 0.7 stack.46
  3.9 0.6 fusion.7.gains
  4.5 0.1 iota_add_fusion
  4.6 0.0 copy-start.2
  4.6 0.1 select_reduce_fusion
  4.7 0.1 subtract_convert_fusion
  4.8 1.0 copy.30.query_place
  5.8 1.0 copy.29.first_key
  6.8 1.2 constant_dynamic-slice_fusion.2
  8.0 0.2 copy.33
  8.2 0.4 copy.26
  8.6 1.7 reshape.196.slab_qkv
  10.3 0.0 copy-done.2
  10.3 1.4 constant_dynamic-slice_fusion
  11.7 0.7 reshape.198
  12.4 0.1 copy.36
  12.5 0.7 reshape.197
  13.2 0.1 copy.37
  13.3 1.3 fusion.2.slab_gate_up
  14.6 1.9 fusion.3
  16.5 1.3 pad_maximum_fusion
  17.8 157.8 %attend.1 = (f32[8,8,256]{2,1,0:T(8,128)}, bf16[8,4,64,768]{3,2,1,0:T(8,128)(2,1)}, bf16[8,128,2048]{2,1,0:T(8,128)(2,1)}, bf16[1024,768]{1,0:T(8,128)(2,1)}, f3...) custom-call(bf16[128,2048]{1,0:T(8,128)(2,1)} %bitcast.47, ...), custom_call_target="tpu_custom_call" | custom-call | tf_op jit(solution)/shard_map/attend/pallas_call | solution.py:972
  175.6 1.5 fusion.9
  177.1 236.7 %mlp_and_back.1 = (bf16[128,2048]{1,0:T(8,128)(2,1)}, f32[128,2048]{1,0:T(8,128)}, bf16[8,128,256]{2,1,0:T(8,128)(2,1)}, f32[1,2048]{1,0:T(1,128)}, bf16[8,64,15...) custom-call(bf16[8,128,256]{2,1,0:T(8,128)(2,1)} %bitcast.62, bf16[256,2048]{1,0:T(8,128)(2,1)} %w_out.1, ...), custom_call_target="tpu_custom_call" | custom-call | tf_op jit(solution)/shard_map/mlp_and_back/pallas_call | solution.py:718
  413.9 124.6 %finish.1 = (bf16[128,2048]{1,0:T(8,128)(2,1)}, f32[8,256]{1,0:T(8,128)}, bf16[8,4,64,1536]{3,2,1,0:T(8,128)(2,1)}, bf16[8,4,64,768]{3,2,1,0:T(8,128)(2,1)}, bf1...) custom-call(bf16[1024,768]{1,0:T(8,128)(2,1)} %get-tuple-element.41.qkv, ...), custom_call_target="tpu_custom_call" | custom-call | tf_op jit(solution)/shard_map/finish/pallas_call | solution.py:1296
  538.5 1.3 fusion.10
  539.8 0.0 copy-start
  539.8 0.0 copy-start.1
  539.8 13.1 %assemble.1 = (f32[256,6144]{1,0:T(8,128)}, f32[256,2048]{1,0:T(8,128)}, f32[256,5632]{1,0:T(8,128)}, f32[256,5632]{1,0:T(8,128)}, f32[704,2048]{1,0:T(8,128)}) custom-call(bf16[8,256,768]{2,1,0:T(8,128)(2,1)} %bitcast.55, bf16[8,256,1536]{2,1,0:T(8,128)(2,1)} %bitcast.46, bf16[768,2048]{1,0:T(8,128)(2,1)} %bitcast.56, bf16[256,2048]{1,0:T(8,128)(2,1)} %bitcast.60), custom_call_target="tpu_custom_call" | custom-call | tf_op jit(solution)/shard_map/assemble/pallas_call | solution.py:1378
  553.0 0.0 copy-done
  553.0 0.8 copy.40
  553.8 0.0 copy-done.1
  553.8 0.8 copy.41
  (2 shorter events, 0.0 us)
Async XLA Ops:
  4.6 5.7 %copy-start.2 = (s32[8,128]{1,0:T(8,128)}, s32[8,128]{1,0:T(8,128)S(1)}, u32[]{:S(2)}) copy-start(s32[8,128]{1,0:T(8,128)S(1)} %get-tuple-element.70) | copy-start | bytes 12292
  539.8 13.1 %copy-start = (bf16[128,2048]{1,0:T(8,128)(2,1)S(1)}, bf16[128,2048]{1,0:T(8,128)(2,1)}, u32[]{:S(2)}) copy-start(bf16[128,2048]{1,0:T(8,128)(2,1)} %get-tuple-element.40) | copy-start | bytes 1572868
  539.8 13.9 %copy-start.1 = (bf16[128,2048]{1,0:T(8,128)(2,1)S(1)}, bf16[128,2048]{1,0:T(8,128)(2,1)}, u32[]{:S(2)}) copy-start(bf16[128,2048]{1,0:T(8,128)(2,1)} %get-tuple-element.52) | copy-start | bytes 1572868

commit v5 on v4

--- a/solution.py
+++ b/solution.py
@@ -263,7 +263,7 @@
 
 
 MESH = pl.DeviceIdType.MESH
-VMEM_BYTES = 62 * 2**20
+VMEM_BYTES = 60 * 2**20
 
 
 def ring_place(block, n):
@@ -469,7 +469,6 @@
     wide_sum,
     down_sum,
     out_grad,
-    dresid,
     normed,
     seed,
     gate_up,
@@ -506,10 +505,9 @@
     grp, me = lax.axis_index("grp"), lax.axis_index("blk")
     over, core, grp_x, grp_c = team(grp)
     _, ends = ring_ends(n)
-    units = w_down.shape[0]
     loads = [
         pltpu.make_async_copy(weights, gate_up, load_sem.at[0]),
-        pltpu.make_async_copy(w_down, down.at[pl.ds(0, units)], load_sem.at[1]),
+        pltpu.make_async_copy(w_down, down, load_sem.at[1]),
         pltpu.make_async_copy(
             seed_hbm.at[pl.ds(1, n - 1)], seed.at[pl.ds(1, n - 1)], load_sem.at[2]
         ),
@@ -517,8 +515,6 @@
     ]
     for load in loads:
         load.start()
-    if units < lanes:
-        down[pl.ds(units, lanes - units)] = jnp.zeros((lanes - units, down.shape[1]), bf16)
     greet(list(ends) + [(grp_x, me), (grp_c, me)])
     columns = x_ref.shape[1]
     half = columns // 2
@@ -571,23 +567,16 @@
     def tall_at(first, count):
         return pl.ds(pl.multiple_of(first * tall_rows, tall_rows), count * tall_rows)
 
-    tall_tile = 256 if lanes % 256 == 0 else 128
-    tiles = lanes // tall_tile
+    tiles = [slice(at, min(at + 256, lanes)) for at in range(0, lanes, 256)]
 
     def tall_grad(tile):
-        at = pl.multiple_of(tile * tall_tile, tall_tile)
-        left = hidden[:, :, pl.ds(at, tall_tile)].reshape(-1, tall_tile)
-        grad_rows = dot_t(left, seed[...].reshape(-1, columns)).astype(bf16)
-        tall[pl.ds(at, tall_tile)] = grad_rows
-
-    def rest(step, _):
+        left = hidden[:, :, tile].reshape(-1, tile.stop - tile.start)
+        tall[tile] = dot_t(left, seed[...].reshape(-1, columns)).astype(bf16)
+
+    for index, step in enumerate(range(n // 2, n - 1)):
+        for tile in tiles[index :: n // 2 - 1]:
+            tall_grad(tile)
         two.step(step)
-        pl.when(step - n // 2 < tiles)(lambda: tall_grad(step - n // 2))
-        return 0
-
-    lax.fori_loop(n // 2, n - 1, rest, 0)
-    for tile in range(n // 2 - 1, tiles):
-        tall_grad(tile)
     tall_one = push(tall.at[tall_at(2 - 2 * core, 2)], tall_c, s_tall.at[0], r_tall.at[0], (grp_c, me))
     tall_one.start()
 
@@ -605,6 +594,7 @@
         - value * inv**3 * jnp.mean(a_two * value, axis=-1, keepdims=True)
     )
     dresid_out[...] = total
+    dresid = seed
     dresid[0] = total.astype(bf16)
     back = Gather(n, dresid, s_dres, r_dres, ends)
     back.start()
@@ -647,6 +637,22 @@
 
     tall_two = push(tall_c.at[tall_at(1 - over, 1)], down_sum, s_tall.at[1], r_tall.at[1], (grp_x, me))
 
+    def tall_pass():
+        tall_one.wait_recv()
+        tall_c[tall_at(1 - over, 1)] = (
+            tall[tall_at(2 * core + 1 - over, 1)].astype(f32)
+            + tall_c[tall_at(1 - over, 1)].astype(f32)
+        ).astype(bf16)
+        tall_two.start()
+
+    def wide_take(tile):
+        wide_copy_x(tile).wait_recv()
+        wide_sum[tile] = (
+            wide[tile, core, over].astype(f32)
+            + wide_c[tile, over].astype(f32)
+            + wide_sum[tile].astype(f32)
+        ).astype(bf16)
+
     def again(t, _):
         pl.when(t > 0)(lambda: back.advance(t - 1))
         low = jnp.maximum(2 * t - 1, 0)
@@ -654,21 +660,29 @@
 
         def inner(step, _):
             pl.when(step < n - 1)(lambda: three.step(step))
-            pl.when(step > 0)(lambda: wide_pass(step - 1))
-            wide_grad(step)
+
+            @pl.when(step < n // 2)
+            def _():
+                wide_grad(2 * step)
+                pl.when(step == 0)(tall_pass)
+                pl.when(step > 0)(lambda: wide_pass(2 * step - 1))
+                wide_grad(2 * step + 1)
+                wide_pass(2 * step)
+
+            pl.when(step == n // 2)(lambda: wide_pass(n - 1))
+
+            @pl.when(step >= n // 2)
+            def _():
+                wide_take(2 * step - n)
+                pl.when(step < n - 1)(lambda: wide_take(2 * step - n + 1))
+
             return 0
 
         lax.fori_loop(2 * t, jnp.minimum(2 * t + 2, n), inner, 0)
         return 0
 
     lax.fori_loop(0, n // 2 + 1, again, 0)
-    wide_pass(n - 1)
-    tall_one.wait_recv()
-    tall_c[tall_at(1 - over, 1)] = (
-        tall[tall_at(2 * core + 1 - over, 1)].astype(f32)
-        + tall_c[tall_at(1 - over, 1)].astype(f32)
-    ).astype(bf16)
-    tall_two.start()
+    wide_take(n - 1)
     out_grad[...] = dot_t(
         ob[...].reshape(-1, ob.shape[2]), dresid[...].reshape(-1, columns)
     ).astype(bf16)
@@ -676,16 +690,6 @@
         part = slice(way * half, (way + 1) * half)
         block_out[:, part] = (resid[:, part] + three.result(way)).astype(bf16)
 
-    def wide_take(tile, _):
-        wide_copy_x(tile).wait_recv()
-        wide_sum[tile] = (
-            wide[tile, core, over].astype(f32)
-            + wide_c[tile, over].astype(f32)
-            + wide_sum[tile].astype(f32)
-        ).astype(bf16)
-        return 0
-
-    lax.fori_loop(0, n, wide_take, 0)
     tall_two.wait_recv()
     down_sum[...] = (
         tall[tall_at(2 * core + over, 1)].astype(f32)
@@ -731,7 +735,6 @@
         scratch_shapes=[
             vmem((n, rows, columns), bf16),
             vmem((n, rows, columns), bf16),
-            vmem((n, rows, columns), bf16),
             vmem((columns, 2 * lanes), bf16),
             vmem((lanes, columns), bf16),
             vmem((n, rows, lanes), bf16),
@@ -772,18 +775,24 @@
         place = self.out.at[self.me, 2 * self.core + self.over]
         return pltpu.make_async_copy(self.pieces.at[self.me], place, sem)
 
-    def to_x(self, k):
+    def to_x(self, k, own=False):
         piece = self.out.at[(self.me - k + self.n) % self.n, 2 * self.core + self.over]
-        return push(piece, piece, self.s_x.at[k], self.r_x.at[k], (self.grp_x, self.me))
-
-    def to_core(self, k, far):
+        source = self.pieces.at[self.me] if own else piece
+        return push(source, piece, self.s_x.at[k], self.r_x.at[k], (self.grp_x, self.me))
+
+    def to_core(self, k, far, own=False):
         over = 1 - self.over if far else self.over
         piece = self.out.at[(self.me - k + self.n) % self.n, 2 * self.core + over]
+        source = self.pieces.at[self.me] if own else piece
         sems = (self.s_c.at[int(far), k], self.r_c.at[int(far), k])
-        return push(piece, piece, *sems, (self.grp_c, self.me))
+        return push(source, piece, *sems, (self.grp_c, self.me))
+
+    def pass_own(self):
+        self.to_x(0, True).start()
+        self.to_core(0, False, True).start()
 
     def pass_on(self, k):
-        pl.when(k > 0)(self.first(k).wait_recv)
+        self.first(k).wait_recv()
         self.to_x(k).start()
         self.to_core(k, False).start()
 
@@ -885,8 +894,10 @@
     x_ring = Gather(n, x_all, s_x, r_x, ends)
     x_ring.start()
     each(n, lambda k: spread_qkv.first(k).start(), 1)
+    spread_qkv.pass_own()
     near_gu = spread_gu.own(local.at[2])
     near_gu.start()
+
 
     def norm(slot):
         value = x_all[slot].astype(f32)
@@ -901,15 +912,22 @@
         pl.when(t > 0)(lambda: x_ring.advance(t - 1))
         low = jnp.maximum(2 * t - 1, 0)
         each(jnp.minimum(2 * t + 1, n), norm, low)
-        pl.when(t == 1)(near_qkv.wait)
-        pl.when(t == 2)(lambda: each(n, spread_qkv.pass_on))
+        pl.when(t == 2)(lambda: each(n, spread_qkv.pass_on, 1))
         pl.when(t == 3)(lambda: each(n, spread_qkv.pass_far))
+
+        @pl.when(t == 2)
+        def _():
+            each(n, lambda k: spread_gu.first(k).start(), 1)
+            spread_gu.pass_own()
+
 
     each(n // 2 + 1, arrive)
     seed_ring = Gather(n, seed, s_seed, r_seed, ends, seed_own)
+    each(n, spread_gu.pass_on, 1)
     seed_ring.start()
-    each(n, lambda k: spread_gu.first(k).start(), 1)
     each(n, spread_qkv.arrived)
+    near_qkv.wait()
+
 
     head_lanes = heads * HEAD
     pair = 2 * rows
@@ -927,7 +945,7 @@
             qkv[at, lane] = value.astype(bf16)
 
     each(n // 2, project)
-    near_gu.wait()
+
 
     def tile(i):
         for head in range(heads):
@@ -946,13 +964,12 @@
             attended_b[at, lane] = out.astype(bf16)
             log_total[head, at, :] = peak + jnp.log(total)
         seed_ring.advance(i)
-        each(2 * i + 2, spread_gu.pass_on, 2 * i)
 
     each(n // 2, tile)
     each(n, spread_gu.pass_far)
     each(n, spread_gu.arrived)
-    near_qkv_sent = [spread_qkv, spread_gu]
-    for spread in near_qkv_sent:
+    near_gu.wait()
+    for spread in (spread_qkv, spread_gu):
         spread.finish()
     each(n, lambda k: gain(k).wait_send(), 1)
     x_ring.finish()
@@ -1099,6 +1116,7 @@
     out_far = push(out_far_place, out_far_place, s_tall.at[7], r_tall.at[7], (grp_c, me))
     out_one.start()
     each(n, lambda k: spread_gu.first(k).start(), 1)
+    spread_gu.pass_own()
     down_x.start()
     down_c.start()
 
@@ -1174,23 +1192,48 @@
         ).astype(bf16)
         copy_x(k).start()
 
+    def take(k):
+        tile = (me + k) % n
+        copy_x(k).wait_recv()
+        wide_x[tile] = (
+            wide[tile, core, over].astype(f32)
+            + wide_c[tile, over].astype(f32)
+            + wide_x[tile].astype(f32)
+        ).astype(bf16)
+
+    def take_and_push(k):
+        take(k)
+        spread_qkv.first(k).start()
+
     ring.step(0)
+    load_normed.wait()
+
+    def grads(i):
+        k = (i + 1) % n
+        grad(k)
+        pl.when(i > 0)(lambda: pass_x(i))
+
+    each(n, grads)
+    pass_x(0)
     out_one.wait_recv()
     out_c[1 - over] = (
         out_grad[core, 1 - over].astype(f32) + out_c[1 - over].astype(f32)
     ).astype(bf16)
     out_two.start()
-    load_normed.wait()
-    near_gu.wait()
 
     def turn(k):
-        grad(k)
-        pl.when(k > 0)(lambda: pass_x(k - 1))
         pl.when(k < n - 2)(lambda: ring.step(k + 1))
-        spread_gu.pass_on(k)
-
-    each(n, turn)
-    pass_x(n - 1)
+        each(jnp.minimum(2 * k + 3, n), spread_gu.pass_on, jnp.minimum(2 * k + 1, n))
+        pl.when(k < n - 1)(lambda: take_and_push(k + 1))
+
+        @pl.when(k == n - 2)
+        def _():
+            take(0)
+            spread_qkv.pass_own()
+
+    each(n - 1, turn)
+    near_qkv = spread_qkv.own(load_sem.at[5])
+    near_qkv.start()
 
     x_float = x_own[...].astype(f32)
     inv = lax.rsqrt(jnp.mean(x_float * x_float, axis=-1, keepdims=True) + EPS)
@@ -1216,23 +1259,6 @@
         + inv * a_one
         - x_float * inv**3 * jnp.mean(a_one * x_float, axis=-1, keepdims=True)
     ).astype(bf16)
-    def take(k):
-        tile = (me + k) % n
-        copy_x(k).wait_recv()
-        wide_x[tile] = (
-            wide[tile, core, over].astype(f32)
-            + wide_c[tile, over].astype(f32)
-            + wide_x[tile].astype(f32)
-        ).astype(bf16)
-
-    def take_and_push(k):
-        take(k)
-        spread_qkv.first(k).start()
-
-    each(n, take_and_push, 1)
-    take(0)
-    near_qkv = spread_qkv.own(load_sem.at[5])
-    near_qkv.start()
     gain_heard[0] = gain_slabs[me]
     each(n, lambda k: gain_blk(k).wait_recv(), 1)
     gain_team[0] = jnp.sum(gain_heard[...], axis=0)
@@ -1245,6 +1271,7 @@
     out_own.start()
     out_to_x.start()
     out_to_c.start()
+    each(n, spread_qkv.pass_on, 1)
     each(n, spread_gu.pass_far)
     down_x.wait_recv()
     down_far.start()
@@ -1254,13 +1281,13 @@
         gain_team.at[2], gain_team.at[3], s_gain.at[n + 1], r_gain.at[n + 1], (grp_x, me)
     )
     gain_x.start()
-    near_qkv.wait()
-    each(n, spread_qkv.pass_on)
     out_to_x.wait_recv()
     out_far.start()
     each(n, spread_qkv.pass_far)
     gain_x.wait_recv()
     gain_grads[...] = gain_team[2] + gain_team[3]
+    near_gu.wait()
+    near_qkv.wait()
     each(n, spread_gu.arrived)
     each(n, spread_qkv.arrived)
     spread_gu.finish()
@@ -1417,7 +1444,7 @@
     head_lanes = heads * HEAD
     qkv_lanes = 3 * head_lanes
     units = w_down.shape[0]
-    lanes = -(-units // 128) * 128
+    lanes = units
     bf16 = jnp.bfloat16
 
     over, core, _, _ = team(lax.axis_index("grp"))
@@ -1435,7 +1462,7 @@
     )
     slab_gate_up = jnp.concatenate(
         [
-            pad_to(quarter_of(w).reshape(quarter, n, units).transpose(1, 0, 2), 2, lanes)
+            quarter_of(w).reshape(quarter, n, units).transpose(1, 0, 2)
             for w in (w_gate, w_up)
         ],
         axis=2,

time: 556 us -> 535 us (0.962); the launches traced: 555 us -> 526 us
  Pallas kernels: 532 us -> 503 us
    pallas_call x1, Pallas kernels: 237 us -> 214 us  [mlp_and_back(): pl.pallas_call(functools.partial(mlp_kernel, n, lanes), out_shape=(jax.Sh...]
    pallas_call x1, Pallas kernels: 158 us -> 149 us  [attend(): pl.pallas_call(functools.partial(attend_kernel, n, heads), out_shape=(jax...]
where the time goes in v5:
time: 535 us; the launch traced here: 526 us
  Pallas kernels  503 us (94%)
  local copies, waits for them, and re-layouts  14.3 us (3%)
  other arithmetic  7.33 us (1%)
    pallas_call x1, Pallas kernels, mlp_and_back(): pl.pallas_call(functools.partial(mlp_kernel, n, lanes), out_shape=(jax.Sh...  214 us
    pallas_call x1, Pallas kernels, attend(): pl.pallas_call(functools.partial(attend_kernel, n, heads), out_shape=(jax...  149 us
    pallas_call x1, Pallas kernels, finish(): pl.pallas_call(functools.partial(finish_kernel, n, heads), out_shape=(jax...  126 us
    pallas_call x1, Pallas kernels, assemble(): pl.pallas_call(functools.partial(assemble_kernel, n, units, lanes, head_l...  14 us

profile of v5, /device:TPU:1, one launch (start us, length us, event | category | flops | bytes accessed | tf_op | source)
XLA Modules:
  0.0 525.6 jit_solution(9395357491036564261)
XLA Ops:
  0.6 0.0 copy-start
  1.0 0.1 stack.44
  1.1 1.1 reduce-window_clone.1
  2.2 0.7 subtract_bitcast_fusion
  2.9 0.7 stack.45
  3.5 0.7 stack.46
  4.2 0.6 fusion.4.gains
  4.8 0.1 iota_add_fusion
  4.9 0.0 copy-start.3
  4.9 0.1 select_reduce_fusion
  4.9 0.1 subtract_convert_fusion
  5.0 1.0 copy.30.query_place
  6.0 1.0 copy.29.first_key
  7.1 0.0 copy-done
  7.1 0.1 constant_dynamic-slice_fusion.2
  7.1 0.2 copy.33
  7.3 0.4 copy.26
  7.7 0.0 copy-done.3
  7.7 1.7 reshape.196.slab_qkv
  9.4 1.4 constant_dynamic-slice_fusion
  10.8 0.7 reshape.198
  11.5 0.1 copy.36
  11.6 0.7 reshape.197
  12.3 0.1 copy.37
  12.5 1.5 pad_maximum_fusion.slab_gate_up
  14.0 1.9 fusion
  15.9 1.3 pad_maximum_fusion.1
  17.2 148.7 %attend.1 = (f32[8,8,256]{2,1,0:T(8,128)}, bf16[8,4,64,768]{3,2,1,0:T(8,128)(2,1)}, bf16[8,128,2048]{2,1,0:T(8,128)(2,1)}, bf16[1024,768]{1,0:T(8,128)(2,1)}, f3...) custom-call(bf16[128,2048]{1,0:T(8,128)(2,1)} %bitcast.47, ...), custom_call_target="tpu_custom_call" | custom-call | tf_op jit(solution)/shard_map/attend/pallas_call | solution.py:989
  165.9 1.5 fusion.6
  167.4 214.4 %mlp_and_back.1 = (bf16[128,2048]{1,0:T(8,128)(2,1)}, f32[128,2048]{1,0:T(8,128)}, bf16[8,128,256]{2,1,0:T(8,128)(2,1)}, f32[1,2048]{1,0:T(1,128)}, bf16[8,64,14...) custom-call(bf16[8,128,256]{2,1,0:T(8,128)(2,1)} %bitcast.62, bf16[256,2048]{1,0:T(8,128)(2,1)} %w_out.1, ...), custom_call_target="tpu_custom_call" | custom-call | tf_op jit(solution)/shard_map/mlp_and_back/pallas_call | solution.py:722
  381.9 125.6 %finish.1 = (bf16[128,2048]{1,0:T(8,128)(2,1)}, f32[8,256]{1,0:T(8,128)}, bf16[8,4,64,1408]{3,2,1,0:T(8,128)(2,1)}, bf16[8,4,64,768]{3,2,1,0:T(8,128)(2,1)}, bf1...) custom-call(bf16[1024,768]{1,0:T(8,128)(2,1)} %get-tuple-element.41.qkv, ...), custom_call_target="tpu_custom_call" | custom-call | tf_op jit(solution)/shard_map/finish/pallas_call | solution.py:1323
  507.5 1.3 fusion.7
  508.8 0.0 copy-start.2
  508.8 0.0 copy-start.1
  508.8 14.0 %assemble.1 = (f32[256,6144]{1,0:T(8,128)}, f32[256,2048]{1,0:T(8,128)}, f32[256,5632]{1,0:T(8,128)}, f32[256,5632]{1,0:T(8,128)}, f32[704,2048]{1,0:T(8,128)}) custom-call(bf16[8,256,768]{2,1,0:T(8,128)(2,1)} %bitcast.54, bf16[8,256,1408]{2,1,0:T(8,128)(2,1)} %bitcast.46, bf16[704,2048]{1,0:T(8,128)(2,1)} %bitcast.56, bf16[256,2048]{1,0:T(8,128)(2,1)} %bitcast.59), custom_call_target="tpu_custom_call" | custom-call | tf_op jit(solution)/shard_map/assemble/pallas_call | solution.py:1405
  522.8 0.0 copy-done.2
  522.8 0.8 copy.40
  523.6 1.9 copy.41
  525.4 0.0 copy-done.1
  (2 shorter events, 0.0 us)
Async XLA Ops:
  0.6 6.4 %copy-start = (bf16[256,6144]{1,0:T(8,128)(2,1)S(1)}, bf16[256,6144]{1,0:T(8,128)(2,1)}, u32[]{:S(2)}) copy-start(bf16[256,6144]{1,0:T(8,128)(2,1)} %param.13) | copy-start | bytes 9437188
  4.9 2.9 copy-start.3
  508.8 14.0 %copy-start.2 = (bf16[128,2048]{1,0:T(8,128)(2,1)S(1)}, bf16[128,2048]{1,0:T(8,128)(2,1)}, u32[]{:S(2)}) copy-start(bf16[128,2048]{1,0:T(8,128)(2,1)} %get-tuple-element.40) | copy-start | bytes 1572868
  508.8 16.6 %copy-start.1 = (bf16[256,6144]{1,0:T(8,128)(2,1)S(1)}, bf16[256,6144]{1,0:T(8,128)(2,1)}, u32[]{:S(2)}) copy-start(bf16[256,6144]{1,0:T(8,128)(2,1)} %param.13) | copy-start | bytes 9437188

commit v6 on v5

--- a/solution.py
+++ b/solution.py
@@ -3,6 +3,7 @@
 
 import jax
 import jax.numpy as jnp
+import numpy as np
 from jax import lax
 from jax.experimental import pallas as pl
 from jax.experimental.pallas import tpu as pltpu
@@ -841,18 +842,34 @@
     return value * cosine + swapped * sine_part
 
 
+def mark_places(n, doc_lens, rows, first_key, query_place, key_place):
+    place = ring_place(lax.axis_index("blk"), n)
+    for slot in range(n):
+        offset = (slot + 1) // 2 * (1 if slot % 2 == 0 else -1)
+        first_row = at_offset(place, offset, n) * rows
+        part = slice(slot * rows, (slot + 1) * rows)
+        here = first_row + lax.broadcasted_iota(jnp.int32, (rows, 1), 0)
+        query_place[part, :] = here
+        key_place[:, part] = first_row + lax.broadcasted_iota(jnp.int32, (1, rows), 1)
+        start = jnp.int32(0)
+        found = jnp.zeros((rows, 1), jnp.int32)
+        for index in range(doc_lens.shape[1]):
+            found = jnp.maximum(found, jnp.where(here >= start, start, 0))
+            start = start + doc_lens[0, index]
+        first_key[part, :] = found
+
+
 def attend_kernel(
     n,
     heads,
+    doc_lens,
     x_own,
-    cosine,
-    sine_part,
-    first_key,
-    query_place,
-    key_place,
-    slab_qkv,
-    slab_gate_up,
-    gains,
+    freqs,
+    norm_attn,
+    norm_mlp,
+    w_qkv,
+    w_gate,
+    w_up,
     seed_own,
     gains_all,
     columns_qkv,
@@ -861,10 +878,21 @@
     attended,
     attended_b,
     log_total,
+    cosine,
+    sine_part,
     gate_up,
     seed,
     x_all,
     gain_row,
+    gains,
+    raw_qkv,
+    raw_gate,
+    raw_up,
+    slab_qkv,
+    slab_gate_up,
+    first_key,
+    query_place,
+    key_place,
     local,
     s_gain,
     r_gain,
@@ -880,11 +908,22 @@
     rows, columns = x_own.shape
     spread_qkv = Spread(n, slab_qkv, columns_qkv, spread_all[:6])
     spread_gu = Spread(n, slab_gate_up, gate_up, spread_all[6:])
-    near_gain = pltpu.make_async_copy(gains, gains_all.at[me], local.at[0])
-    near_gain.start()
-    near_qkv = spread_qkv.own(local.at[1])
-    near_qkv.start()
+    over, core, _, _ = team(grp)
+    quarter = slab_qkv.shape[1]
+    own_rows = pl.ds(pl.multiple_of((2 * core + over) * quarter, quarter), quarter)
+    loads = [
+        pltpu.make_async_copy(weight.at[own_rows], raw, local.at[index])
+        for index, (weight, raw) in enumerate(
+            ((w_qkv, raw_qkv), (w_gate, raw_gate), (w_up, raw_up))
+        )
+    ]
+    for load in loads:
+        load.start()
     x_all[0] = x_own[...]
+    gains[...] = jnp.zeros_like(gains)
+    gains[0:1, :] = norm_attn[...].astype(f32)
+    gains[1:2, :] = norm_mlp[...].astype(f32)
+    gains_all[me] = gains[...]
     greet(team_and_ring(n))
 
     def gain(k):
@@ -893,25 +932,50 @@
     each(n, lambda k: gain(k).start(), 1)
     x_ring = Gather(n, x_all, s_x, r_x, ends)
     x_ring.start()
+    share = heads * HEAD
+    loads[0].wait()
+    for to in range(n):
+        for part in range(3):
+            slab_qkv[to, :, part * share : (part + 1) * share] = raw_qkv[
+                :, (part * n + to) * share : (part * n + to + 1) * share
+            ]
+    near_qkv = spread_qkv.own(local.at[3])
+    near_qkv.start()
     each(n, lambda k: spread_qkv.first(k).start(), 1)
     spread_qkv.pass_own()
-    near_gu = spread_gu.own(local.at[2])
+    units = raw_gate.shape[1] // n
+    loads[1].wait()
+    loads[2].wait()
+    for to in range(n):
+        lane = slice(to * units, (to + 1) * units)
+        slab_gate_up[to] = jnp.concatenate(
+            [raw_gate[:, lane].astype(f32), raw_up[:, lane].astype(f32)], axis=1
+        ).astype(bf16)
+    near_gu = spread_gu.own(local.at[4])
     near_gu.start()
-
+    mark_places(n, doc_lens, rows, first_key, query_place, key_place)
 
     def norm(slot):
         value = x_all[slot].astype(f32)
         inv = lax.rsqrt(jnp.mean(value * value, axis=-1, keepdims=True) + EPS)
         normed[slot] = (value * inv * gain_row[...]).astype(bf16)
 
-    near_gain.wait()
     each(n, lambda k: gain(k).wait_recv(), 1)
     fill_row(gain_row, gains_all, 0, columns // n)
+
+    def table(slot):
+        at = pl.ds(pl.multiple_of(slot * rows, rows), rows)
+        angle = (query_place[at, :] - first_key[at, :]).astype(f32) * freqs[...]
+        lane = lax.broadcasted_iota(jnp.int32, (rows, HEAD), 1)
+        sine = jnp.sin(angle)
+        cosine[at, :] = jnp.cos(angle)
+        sine_part[at, :] = jnp.where(lane < HEAD // 2, -sine, sine)
 
     def arrive(t):
         pl.when(t > 0)(lambda: x_ring.advance(t - 1))
         low = jnp.maximum(2 * t - 1, 0)
         each(jnp.minimum(2 * t + 1, n), norm, low)
+        each(jnp.minimum(2 * t + 1, n), table, low)
         pl.when(t == 2)(lambda: each(n, spread_qkv.pass_on, 1))
         pl.when(t == 3)(lambda: each(n, spread_qkv.pass_far))
 
@@ -976,35 +1040,53 @@
     seed_ring.finish()
 
 
-def attend(slab_qkv, slab_gate_up, gains, x_own, seed_own, cosine, sine_part, first_key, places):
+def attend(doc_lens, x_own, norm_attn, norm_mlp, w_qkv, w_gate, w_up, seed_own):
     n = lax.axis_size("blk")
     rows, columns = x_own.shape
     seq = n * rows
-    lanes = slab_qkv.shape[2]
+    lanes = w_qkv.shape[1] // n
+    quarter = w_qkv.shape[0] // 4
+    both = 2 * w_gate.shape[1] // n
     head_lanes = lanes // 3
     heads = head_lanes // HEAD
-    f32, bf16 = jnp.float32, jnp.bfloat16
+    share = norm_attn.shape[0]
+    f32, bf16, i32 = jnp.float32, jnp.bfloat16, jnp.int32
     vmem, dma = pltpu.VMEM, pltpu.SemaphoreType.DMA
     in_vmem, anywhere = pl.BlockSpec(memory_space=vmem), pl.BlockSpec(memory_space=pl.ANY)
+    half_freqs = np.exp(
+        np.arange(HEAD // 2, dtype=np.float32) * np.float32(-2.0 * math.log(10000.0) / HEAD)
+    )
+    freqs = jnp.asarray(np.concatenate([half_freqs, half_freqs])[None].astype(np.float32))
     return pl.pallas_call(
         functools.partial(attend_kernel, n, heads),
         out_shape=(
-            jax.ShapeDtypeStruct((n,) + gains.shape, f32),
-            jax.ShapeDtypeStruct((n, 4) + slab_qkv.shape[1:], bf16),
+            jax.ShapeDtypeStruct((n, 8, share), f32),
+            jax.ShapeDtypeStruct((n, 4, quarter, lanes), bf16),
             jax.ShapeDtypeStruct((n, rows, columns), bf16),
             jax.ShapeDtypeStruct((seq, lanes), bf16),
             jax.ShapeDtypeStruct((seq, head_lanes), f32),
             jax.ShapeDtypeStruct((seq, head_lanes), bf16),
             jax.ShapeDtypeStruct((heads, seq, 1), f32),
-            jax.ShapeDtypeStruct((n, 4) + slab_gate_up.shape[1:], bf16),
+            jax.ShapeDtypeStruct((seq, HEAD), f32),
+            jax.ShapeDtypeStruct((seq, HEAD), f32),
+            jax.ShapeDtypeStruct((n, 4, quarter, both), bf16),
             jax.ShapeDtypeStruct((n, rows, columns), bf16),
         ),
-        in_specs=[in_vmem] * 6 + [anywhere] * 4,
-        out_specs=[in_vmem] * 7 + [anywhere] * 2,
+        in_specs=[pl.BlockSpec(memory_space=pltpu.SMEM)] + [in_vmem] * 4 + [anywhere] * 4,
+        out_specs=[in_vmem] * 9 + [anywhere] * 2,
         scratch_shapes=[
             vmem((n, rows, columns), bf16),
             vmem((1, columns), f32),
-            dma((3,)),
+            vmem((8, share), f32),
+            vmem((quarter, n * lanes), bf16),
+            vmem((quarter, w_gate.shape[1]), bf16),
+            vmem((quarter, w_gate.shape[1]), bf16),
+            vmem((n, quarter, lanes), bf16),
+            vmem((n, quarter, both), bf16),
+            vmem((seq, 1), i32),
+            vmem((seq, 1), i32),
+            vmem((1, seq), i32),
+            dma((5,)),
             dma((n,)),
             dma((n,)),
         ]
@@ -1013,15 +1095,14 @@
         compiler_params=kernel_params(0),
         name="attend",
     )(
+        doc_lens,
         x_own,
-        cosine,
-        sine_part,
-        first_key,
-        places.reshape(seq, 1),
-        places.reshape(1, seq),
-        slab_qkv,
-        slab_gate_up,
-        gains,
+        freqs,
+        norm_attn.reshape(1, share),
+        norm_mlp.reshape(1, share),
+        w_qkv,
+        w_gate,
+        w_up,
         seed_own,
     )
 
@@ -1035,9 +1116,7 @@
     log_total,
     cosine,
     sine_part,
-    first_key,
-    query_place,
-    key_place,
+    doc_lens,
     x_own,
     gain,
     dresid,
@@ -1058,6 +1137,9 @@
     dqkv,
     dkeys,
     dvalues,
+    first_key,
+    query_place,
+    key_place,
     held,
     terms,
     wide,
@@ -1120,6 +1202,7 @@
     down_x.start()
     down_c.start()
 
+    mark_places(n, doc_lens, rows, first_key, query_place, key_place)
     pair = 2 * rows
     head_lanes = heads * HEAD
     scale = HEAD ** (-0.5)
@@ -1330,7 +1413,10 @@
             jax.ShapeDtypeStruct((4,) + down_sum.shape, bf16),
             jax.ShapeDtypeStruct((4, out_rows, columns), bf16),
         ),
-        in_specs=[in_vmem] * 14 + [anywhere] * 4,
+        in_specs=[in_vmem] * 6
+        + [pl.BlockSpec(memory_space=pltpu.SMEM)]
+        + [in_vmem] * 5
+        + [anywhere] * 4,
         out_specs=[in_vmem] * 2 + [anywhere] * 4,
         scratch_shapes=[
             vmem((n, rows, columns), bf16),
@@ -1338,6 +1424,9 @@
             vmem((n, rows, lanes), bf16),
             vmem((seq, HEAD), f32),
             vmem((seq, HEAD), f32),
+            vmem((seq, 1), jnp.int32),
+            vmem((seq, 1), jnp.int32),
+            vmem((1, seq), jnp.int32),
             vmem((2, n, rows, columns // 2), bf16),
             vmem((2, rows, columns // 2), f32),
             vmem((n, 2, 2, quarter, lanes), bf16),
@@ -1430,12 +1519,6 @@
     )(qkv, gate_up, down, out)
 
 
-def pad_to(array, axis, size):
-    widths = [(0, 0)] * array.ndim
-    widths[axis] = (0, size - array.shape[axis])
-    return jnp.pad(array, widths)
-
-
 def per_device(block_input, doc_lens, norm_attn, w_qkv, w_out, norm_mlp, w_gate, w_up, w_down, cot):
     n = lax.axis_size("blk")
     tok_rows, width = block_input.shape[1:]
@@ -1445,52 +1528,20 @@
     qkv_lanes = 3 * head_lanes
     units = w_down.shape[0]
     lanes = units
-    bf16 = jnp.bfloat16
-
-    over, core, _, _ = team(lax.axis_index("grp"))
     quarter = w_qkv.shape[0] // 4
-    first_row = (2 * core + over) * quarter
-
-    def quarter_of(weight):
-        return lax.dynamic_slice_in_dim(weight, first_row, quarter, 0)
-
-    slab_qkv = (
-        quarter_of(w_qkv)
-        .reshape(quarter, 3, n, head_lanes)
-        .transpose(2, 0, 1, 3)
-        .reshape(n, quarter, qkv_lanes)
-    )
-    slab_gate_up = jnp.concatenate(
-        [
-            quarter_of(w).reshape(quarter, n, units).transpose(1, 0, 2)
-            for w in (w_gate, w_up)
-        ],
-        axis=2,
-    )
-    gains = pad_to(jnp.stack([norm_attn, norm_mlp]).astype(jnp.float32), 0, 8)
-    place = ring_place(lax.axis_index("blk"), n)
-    offsets = [0] + [k * sign for k in range(1, n // 2) for sign in (-1, 1)] + [n // 2]
-    blocks = jnp.stack([at_offset(place, offset, n) for offset in offsets])
-    places = (blocks[:, None] * tok_rows + jnp.arange(tok_rows, dtype=jnp.int32)).reshape(seq)
-    lengths = doc_lens[0]
-    starts = jnp.cumsum(lengths) - lengths
-    first_key = start_of(places, starts)
-    half_cosine, half_sine = angle_tables(places - first_key)
-    first_key = first_key.reshape(seq, 1)
-    half_cosine, half_sine = half_cosine[:, 0], half_sine[:, 0]
-    cosine = jnp.concatenate([half_cosine, half_cosine], axis=1)
-    sine_part = jnp.concatenate([-half_sine, half_sine], axis=1)
-    gains_all, qkv_columns, normed_one, qkv, attended, attended_b, log_total, gate_up, seed = attend(
-        slab_qkv,
-        slab_gate_up,
-        gains,
-        block_input[0],
-        cot[0],
+    (
+        gains_all,
+        qkv_columns,
+        normed_one,
+        qkv,
+        attended,
+        attended_b,
+        log_total,
         cosine,
         sine_part,
-        first_key,
-        places,
-    )
+        gate_up,
+        seed,
+    ) = attend(doc_lens, block_input[0], norm_attn, norm_mlp, w_qkv, w_gate, w_up, cot[0])
     gain_one = gains_all[:, 0].reshape(1, width)
     gain_two = gains_all[:, 1].reshape(1, width)
     qkv_columns = qkv_columns.reshape(width, qkv_lanes)
@@ -1514,9 +1565,7 @@
             log_total,
             cosine,
             sine_part,
-            first_key,
-            places.reshape(seq, 1),
-            places.reshape(1, seq),
+            doc_lens,
         ),
         block_input[0],
         gain_one,

time: 535 us -> 509 us (0.951); the launches traced: 526 us -> 509 us
  local copies, waits for them, and re-layouts: 14.3 us -> 6.91 us
  other arithmetic: 7.33 us -> 0 us
where the time goes in v6:
time: 509 us
  Pallas kernels  501 us (98%)
  local copies, waits for them, and re-layouts  6.91 us (1%)
    pallas_call x1, Pallas kernels, mlp_and_back(): pl.pallas_call(functools.partial(mlp_kernel, n, lanes), out_shape=(jax.Sh...  215 us
    pallas_call x1, Pallas kernels, attend(): pl.pallas_call(functools.partial(attend_kernel, n, heads), out_shape=(jax...  148 us
    pallas_call x1, Pallas kernels, finish(): pl.pallas_call(functools.partial(finish_kernel, n, heads), out_shape=(jax...  126 us
    pallas_call x1, Pallas kernels, assemble(): pl.pallas_call(functools.partial(assemble_kernel, n, units, lanes, head_l...  12.8 us

profile of v6, /device:TPU:1, one launch (start us, length us, event | category | flops | bytes accessed | tf_op | source)
XLA Modules:
  0.0 509.0 jit_solution(9658993997884083114)
XLA Ops:
  0.6 1.2 reshape.51.norm_attn
  1.9 1.2 reshape.52.norm_mlp
  3.1 148.4 %attend.1 = (f32[8,8,256]{2,1,0:T(8,128)}, bf16[8,4,64,768]{3,2,1,0:T(8,128)(2,1)}, bf16[8,128,2048]{2,1,0:T(8,128)(2,1)}, bf16[1024,768]{1,0:T(8,128)(2,1)}, f3...) custom-call(s32[1,8]{1,0:T(1,128)} %doc_lens.3, ...), custom_call_target="tpu_custom_call" | custom-call | tf_op jit(solution)/shard_map/attend/pallas_call | solution.py:1060
  151.5 1.5 fusion
  153.0 214.6 %mlp_and_back.1 = (bf16[128,2048]{1,0:T(8,128)(2,1)}, f32[128,2048]{1,0:T(8,128)}, bf16[8,128,256]{2,1,0:T(8,128)(2,1)}, f32[1,2048]{1,0:T(1,128)}, bf16[8,64,14...) custom-call(bf16[8,128,256]{2,1,0:T(8,128)(2,1)} %bitcast.29, bf16[256,2048]{1,0:T(8,128)(2,1)} %w_out.1, ...), custom_call_target="tpu_custom_call" | custom-call | tf_op jit(solution)/shard_map/mlp_and_back/pallas_call | solution.py:723
  367.7 125.5 %finish.1 = (bf16[128,2048]{1,0:T(8,128)(2,1)}, f32[8,256]{1,0:T(8,128)}, bf16[8,4,64,1408]{3,2,1,0:T(8,128)(2,1)}, bf16[8,4,64,768]{3,2,1,0:T(8,128)(2,1)}, bf1...) custom-call(bf16[1024,768]{1,0:T(8,128)(2,1)} %get-tuple-element.43.qkv, ...), custom_call_target="tpu_custom_call" | custom-call | tf_op jit(solution)/shard_map/finish/pallas_call | solution.py:1406
  493.2 1.3 fusion.1
  494.6 0.0 copy-start
  494.6 0.0 copy-start.1
  494.6 12.8 %assemble.1 = (f32[256,6144]{1,0:T(8,128)}, f32[256,2048]{1,0:T(8,128)}, f32[256,5632]{1,0:T(8,128)}, f32[256,5632]{1,0:T(8,128)}, f32[704,2048]{1,0:T(8,128)}) custom-call(bf16[8,256,768]{2,1,0:T(8,128)(2,1)} %bitcast.22, bf16[8,256,1408]{2,1,0:T(8,128)(2,1)} %bitcast.18, bf16[704,2048]{1,0:T(8,128)(2,1)} %bitcast.24, bf16[256,2048]{1,0:T(8,128)(2,1)} %bitcast.27), custom_call_target="tpu_custom_call" | custom-call | tf_op jit(solution)/shard_map/assemble/pallas_call | solution.py:1494
  507.4 0.0 copy-done
  507.4 0.8 copy.22
  508.2 0.0 copy-done.1
  508.2 0.8 copy.23
Async XLA Ops:
  494.6 12.8 %copy-start = (bf16[128,2048]{1,0:T(8,128)(2,1)S(1)}, bf16[128,2048]{1,0:T(8,128)(2,1)}, u32[]{:S(2)}) copy-start(bf16[128,2048]{1,0:T(8,128)(2,1)} %get-tuple-element.42) | copy-start | bytes 1572868
  494.6 13.6 %copy-start.1 = (bf16[128,2048]{1,0:T(8,128)(2,1)S(1)}, bf16[128,2048]{1,0:T(8,128)(2,1)}, u32[]{:S(2)}) copy-start(bf16[128,2048]{1,0:T(8,128)(2,1)} %get-tuple-element.56) | copy-start | bytes 1572868

commit v7 on v6

--- a/solution.py
+++ b/solution.py
@@ -871,7 +871,8 @@
     w_gate,
     w_up,
     seed_own,
-    gains_all,
+    gain_row,
+    gain_two,
     columns_qkv,
     normed,
     qkv,
@@ -883,7 +884,7 @@
     gate_up,
     seed,
     x_all,
-    gain_row,
+    gains_all,
     gains,
     raw_qkv,
     raw_gate,
@@ -962,6 +963,7 @@
 
     each(n, lambda k: gain(k).wait_recv(), 1)
     fill_row(gain_row, gains_all, 0, columns // n)
+    fill_row(gain_two, gains_all, 1, columns // n)
 
     def table(slot):
         at = pl.ds(pl.multiple_of(slot * rows, rows), rows)
@@ -1028,9 +1030,9 @@
             attended_b[at, lane] = out.astype(bf16)
             log_total[head, at, :] = peak + jnp.log(total)
         seed_ring.advance(i)
+        pl.when(i == 1)(lambda: each(n, spread_gu.pass_far))
 
     each(n // 2, tile)
-    each(n, spread_gu.pass_far)
     each(n, spread_gu.arrived)
     near_gu.wait()
     for spread in (spread_qkv, spread_gu):
@@ -1060,7 +1062,8 @@
     return pl.pallas_call(
         functools.partial(attend_kernel, n, heads),
         out_shape=(
-            jax.ShapeDtypeStruct((n, 8, share), f32),
+            jax.ShapeDtypeStruct((1, columns), f32),
+            jax.ShapeDtypeStruct((1, columns), f32),
             jax.ShapeDtypeStruct((n, 4, quarter, lanes), bf16),
             jax.ShapeDtypeStruct((n, rows, columns), bf16),
             jax.ShapeDtypeStruct((seq, lanes), bf16),
@@ -1073,10 +1076,10 @@
             jax.ShapeDtypeStruct((n, rows, columns), bf16),
         ),
         in_specs=[pl.BlockSpec(memory_space=pltpu.SMEM)] + [in_vmem] * 4 + [anywhere] * 4,
-        out_specs=[in_vmem] * 9 + [anywhere] * 2,
+        out_specs=[in_vmem] * 10 + [anywhere] * 2,
         scratch_shapes=[
             vmem((n, rows, columns), bf16),
-            vmem((1, columns), f32),
+            vmem((n, 8, share), f32),
             vmem((8, share), f32),
             vmem((quarter, n * lanes), bf16),
             vmem((quarter, w_gate.shape[1]), bf16),
@@ -1308,6 +1311,7 @@
         pl.when(k < n - 2)(lambda: ring.step(k + 1))
         each(jnp.minimum(2 * k + 3, n), spread_gu.pass_on, jnp.minimum(2 * k + 1, n))
         pl.when(k < n - 1)(lambda: take_and_push(k + 1))
+        pl.when(k >= 2)(lambda: spread_qkv.pass_on(k - 1))
 
         @pl.when(k == n - 2)
         def _():
@@ -1317,6 +1321,7 @@
     each(n - 1, turn)
     near_qkv = spread_qkv.own(load_sem.at[5])
     near_qkv.start()
+    each(n, spread_qkv.pass_on, n - 2)
 
     x_float = x_own[...].astype(f32)
     inv = lax.rsqrt(jnp.mean(x_float * x_float, axis=-1, keepdims=True) + EPS)
@@ -1354,7 +1359,6 @@
     out_own.start()
     out_to_x.start()
     out_to_c.start()
-    each(n, spread_qkv.pass_on, 1)
     each(n, spread_gu.pass_far)
     down_x.wait_recv()
     down_far.start()
@@ -1530,7 +1534,8 @@
     lanes = units
     quarter = w_qkv.shape[0] // 4
     (
-        gains_all,
+        gain_one,
+        gain_two,
         qkv_columns,
         normed_one,
         qkv,
@@ -1542,8 +1547,6 @@
         gate_up,
         seed,
     ) = attend(doc_lens, block_input[0], norm_attn, norm_mlp, w_qkv, w_gate, w_up, cot[0])
-    gain_one = gains_all[:, 0].reshape(1, width)
-    gain_two = gains_all[:, 1].reshape(1, width)
     qkv_columns = qkv_columns.reshape(width, qkv_lanes)
     gate_up = gate_up.reshape(width, 2 * lanes)
     block_out, dresid, dattended, terms_two, gate_up_sum, down_sum, out_grad = mlp_and_back(

time: 509 us -> 490 us (0.963)
  Pallas kernels: 501 us -> 484 us
    pallas_call x1, Pallas kernels: 126 us -> 114 us  [finish(): pl.pallas_call(functools.partial(finish_kernel, n, heads), out_shape=(jax...]
    pallas_call x1, Pallas kernels: 148 us -> 143 us  [attend(): pl.pallas_call(functools.partial(attend_kernel, n, heads), out_shape=(jax...]
where the time goes in v7:
time: 490 us
  Pallas kernels  484 us (99%)
  local copies, waits for them, and re-layouts  5.38 us (1%)
    pallas_call x1, Pallas kernels, mlp_and_back(): pl.pallas_call(functools.partial(mlp_kernel, n, lanes), out_shape=(jax.Sh...  214 us
    pallas_call x1, Pallas kernels, attend(): pl.pallas_call(functools.partial(attend_kernel, n, heads), out_shape=(jax...  143 us
    pallas_call x1, Pallas kernels, finish(): pl.pallas_call(functools.partial(finish_kernel, n, heads), out_shape=(jax...  114 us
    pallas_call x1, Pallas kernels, assemble(): pl.pallas_call(functools.partial(assemble_kernel, n, units, lanes, head_l...  12.8 us

profile of v7, /device:TPU:1, one launch (start us, length us, event | category | flops | bytes accessed | tf_op | source)
XLA Modules:
  0.0 489.6 jit_solution(4686014480806585775)
XLA Ops:
  0.6 1.2 reshape.51.norm_attn
  1.9 1.2 reshape.52.norm_mlp
  3.1 142.6 %attend.1 = (f32[1,2048]{1,0:T(1,128)}, f32[1,2048]{1,0:T(1,128)}, bf16[8,4,64,768]{3,2,1,0:T(8,128)(2,1)}, bf16[8,128,2048]{2,1,0:T(8,128)(2,1)}, bf16[1024,768...) custom-call(s32[1,8]{1,0:T(1,128)} %doc_lens.3, ...), custom_call_target="tpu_custom_call" | custom-call | tf_op jit(solution)/shard_map/attend/pallas_call | solution.py:1062
  145.7 214.4 %mlp_and_back.1 = (bf16[128,2048]{1,0:T(8,128)(2,1)}, f32[128,2048]{1,0:T(8,128)}, bf16[8,128,256]{2,1,0:T(8,128)(2,1)}, f32[1,2048]{1,0:T(1,128)}, bf16[8,64,14...) custom-call(bf16[8,128,256]{2,1,0:T(8,128)(2,1)} %bitcast.28, bf16[256,2048]{1,0:T(8,128)(2,1)} %w_out.1, ...), custom_call_target="tpu_custom_call" | custom-call | tf_op jit(solution)/shard_map/mlp_and_back/pallas_call | solution.py:723
  360.1 113.7 %finish.1 = (bf16[128,2048]{1,0:T(8,128)(2,1)}, f32[8,256]{1,0:T(8,128)}, bf16[8,4,64,1408]{3,2,1,0:T(8,128)(2,1)}, bf16[8,4,64,768]{3,2,1,0:T(8,128)(2,1)}, bf1...) custom-call(bf16[1024,768]{1,0:T(8,128)(2,1)} %get-tuple-element.44.qkv, ...), custom_call_target="tpu_custom_call" | custom-call | tf_op jit(solution)/shard_map/finish/pallas_call | solution.py:1410
  473.8 1.3 fusion
  475.1 0.0 copy-start
  475.1 0.0 copy-start.1
  475.1 12.8 %assemble.1 = (f32[256,6144]{1,0:T(8,128)}, f32[256,2048]{1,0:T(8,128)}, f32[256,5632]{1,0:T(8,128)}, f32[256,5632]{1,0:T(8,128)}, f32[704,2048]{1,0:T(8,128)}) custom-call(bf16[8,256,768]{2,1,0:T(8,128)(2,1)} %bitcast.20, bf16[8,256,1408]{2,1,0:T(8,128)(2,1)} %bitcast.16, bf16[704,2048]{1,0:T(8,128)(2,1)} %bitcast.22, bf16[256,2048]{1,0:T(8,128)(2,1)} %bitcast.25), custom_call_target="tpu_custom_call" | custom-call | tf_op jit(solution)/shard_map/assemble/pallas_call | solution.py:1498
  488.0 0.0 copy-done
  488.0 0.8 copy.22
  488.8 0.0 copy-done.1
  488.8 0.8 copy.23
Async XLA Ops:
  475.1 12.8 %copy-start = (bf16[128,2048]{1,0:T(8,128)(2,1)S(1)}, bf16[128,2048]{1,0:T(8,128)(2,1)}, u32[]{:S(2)}) copy-start(bf16[128,2048]{1,0:T(8,128)(2,1)} %get-tuple-element.43) | copy-start | bytes 1572868
  475.1 13.6 %copy-start.1 = (bf16[128,2048]{1,0:T(8,128)(2,1)S(1)}, bf16[128,2048]{1,0:T(8,128)(2,1)}, u32[]{:S(2)}) copy-start(bf16[128,2048]{1,0:T(8,128)(2,1)} %get-tuple-element.58) | copy-start | bytes 1572868

commit v8 on v7

--- a/solution.py
+++ b/solution.py
@@ -922,8 +922,8 @@
         load.start()
     x_all[0] = x_own[...]
     gains[...] = jnp.zeros_like(gains)
-    gains[0:1, :] = norm_attn[...].astype(f32)
-    gains[1:2, :] = norm_mlp[...].astype(f32)
+    gains[0:1, :] = norm_attn[...].astype(f32).reshape(1, -1)
+    gains[1:2, :] = norm_mlp[...].astype(f32).reshape(1, -1)
     gains_all[me] = gains[...]
     greet(team_and_ring(n))
 
@@ -1101,8 +1101,8 @@
         doc_lens,
         x_own,
         freqs,
-        norm_attn.reshape(1, share),
-        norm_mlp.reshape(1, share),
+        norm_attn,
+        norm_mlp,
         w_qkv,
         w_gate,
         w_up,
@@ -1464,8 +1464,10 @@
     )
 
 
-def assemble_kernel(n, units, lanes, head_lanes, qkv, gate_up, down, out, *grads):
-    grad_qkv, grad_out, grad_gate, grad_up, grad_down = grads
+def assemble_kernel(n, units, lanes, head_lanes, qkv, gate_up, down, out, blocks, shift, *grads):
+    grad_qkv, grad_out, grad_gate, grad_up, grad_down, block_out, x_grad = grads
+    block_out[...] = blocks[...]
+    x_grad[...] = shift[...]
     f32 = jnp.float32
     for source in range(n):
         for part in range(3):
@@ -1480,13 +1482,14 @@
     grad_down[...] = down[...].astype(f32)
 
 
-def assemble(qkv, gate_up, down, out, units, steps=4):
+def assemble(qkv, gate_up, down, out, block_out, x_grad, units, steps=4):
     n, rows, qkv_lanes = qkv.shape
     columns = down.shape[1]
     lanes = gate_up.shape[2] // 2
     head_lanes = qkv_lanes // 3
     step = rows // steps
     down_step = units // steps
+    tokens = x_grad.shape[0] // steps
     f32 = jnp.float32
 
     def wide(width):
@@ -1504,12 +1507,16 @@
             jax.ShapeDtypeStruct((rows, n * units), f32),
             jax.ShapeDtypeStruct((rows, n * units), f32),
             jax.ShapeDtypeStruct((units, columns), f32),
+            jax.ShapeDtypeStruct(block_out.shape, block_out.dtype),
+            jax.ShapeDtypeStruct(x_grad.shape, x_grad.dtype),
         ),
         in_specs=[
             wide(qkv_lanes),
             wide(2 * lanes),
             flat(down_step, columns),
             flat(out.shape[0] // steps, columns),
+            flat(tokens, columns),
+            flat(tokens, columns),
         ],
         out_specs=[
             flat(step, n * qkv_lanes),
@@ -1517,10 +1524,12 @@
             flat(step, n * units),
             flat(step, n * units),
             flat(down_step, columns),
+            flat(tokens, columns),
+            flat(tokens, columns),
         ],
         compiler_params=pltpu.CompilerParams(vmem_limit_bytes=VMEM_BYTES),
         name="assemble",
-    )(qkv, gate_up, down, out)
+    )(qkv, gate_up, down, out, block_out, x_grad)
 
 
 def per_device(block_input, doc_lens, norm_attn, w_qkv, w_out, norm_mlp, w_gate, w_up, w_down, cot):
@@ -1581,11 +1590,13 @@
         down_sum,
     )
     shard_rows = 4 * quarter
-    grad_qkv, grad_out, grad_gate, grad_up, grad_down = assemble(
+    grad_qkv, grad_out, grad_gate, grad_up, grad_down, block_out, x_grad = assemble(
         wide_qkv.reshape(n, shard_rows, qkv_lanes),
         wide_gate_up.reshape(n, shard_rows, 2 * lanes),
         tall_down.reshape(lanes, width),
         tall_out.reshape(head_lanes, width),
+        block_out,
+        x_grad,
         units,
     )
     return (

time: 490 us -> 487 us (level)
  no operation moved by 1% of the time
where the time goes in v8:
time: 487 us; the launch traced here: 486 us
  Pallas kernels  484 us (99%)
    pallas_call x1, Pallas kernels, mlp_and_back(): pl.pallas_call(functools.partial(mlp_kernel, n, lanes), out_shape=(jax.Sh...  214 us
    pallas_call x1, Pallas kernels, attend(): pl.pallas_call(functools.partial(attend_kernel, n, heads), out_shape=(jax...  143 us
    pallas_call x1, Pallas kernels, finish(): pl.pallas_call(functools.partial(finish_kernel, n, heads), out_shape=(jax...  114 us
    pallas_call x1, Pallas kernels, assemble(): pl.pallas_call(functools.partial(assemble_kernel, n, units, lanes, head_l...  13.4 us

profile of v8, /device:TPU:1, one launch (start us, length us, event | category | flops | bytes accessed | tf_op | source)
XLA Modules:
  0.0 486.3 jit_solution(13563784878080820007)
XLA Ops:
  0.6 142.7 %attend.1 = (f32[1,2048]{1,0:T(1,128)}, f32[1,2048]{1,0:T(1,128)}, bf16[8,4,64,768]{3,2,1,0:T(8,128)(2,1)}, bf16[8,128,2048]{2,1,0:T(8,128)(2,1)}, bf16[1024,768...) custom-call(s32[1,8]{1,0:T(1,128)} %doc_lens.3, ...), custom_call_target="tpu_custom_call" | custom-call | tf_op jit(solution)/shard_map/attend/pallas_call | solution.py:1062
  143.3 214.4 %mlp_and_back.1 = (bf16[128,2048]{1,0:T(8,128)(2,1)}, f32[128,2048]{1,0:T(8,128)}, bf16[8,128,256]{2,1,0:T(8,128)(2,1)}, f32[1,2048]{1,0:T(1,128)}, bf16[8,64,14...) custom-call(bf16[8,128,256]{2,1,0:T(8,128)(2,1)} %bitcast.28, bf16[256,2048]{1,0:T(8,128)(2,1)} %w_out.1, ...), custom_call_target="tpu_custom_call" | custom-call | tf_op jit(solution)/shard_map/mlp_and_back/pallas_call | solution.py:723
  357.7 113.7 %finish.1 = (bf16[128,2048]{1,0:T(8,128)(2,1)}, f32[8,256]{1,0:T(8,128)}, bf16[8,4,64,1408]{3,2,1,0:T(8,128)(2,1)}, bf16[8,4,64,768]{3,2,1,0:T(8,128)(2,1)}, bf1...) custom-call(bf16[1024,768]{1,0:T(8,128)(2,1)} %get-tuple-element.41.qkv, ...), custom_call_target="tpu_custom_call" | custom-call | tf_op jit(solution)/shard_map/finish/pallas_call | solution.py:1410
  471.4 1.3 fusion
  472.7 13.4 %assemble.1 = (f32[256,6144]{1,0:T(8,128)}, f32[256,2048]{1,0:T(8,128)}, f32[256,5632]{1,0:T(8,128)}, f32[256,5632]{1,0:T(8,128)}, f32[704,2048]{1,0:T(8,128)}, ...) custom-call(bf16[8,256,768]{2,1,0:T(8,128)(2,1)} %bitcast.20, bf16[8,256,1408]{2,1,0:T(8,128)(2,1)} %bitcast.16, ...), custom_call_target="tpu_custom_call" | custom-call | tf_op jit(solution)/shard_map/assemble/pallas_call | solution.py:1501

commit v9 on v8

--- a/solution.py
+++ b/solution.py
@@ -578,6 +578,12 @@
         for tile in tiles[index :: n // 2 - 1]:
             tall_grad(tile)
         two.step(step)
+    def down_term(step, way):
+        return dot_f32(hidden[behind(step, way, n)], down[:, way * half : (way + 1) * half])
+
+    three = Scatter(n, held_one, terms, s_three, r_three, ends, down_term)
+
+    three.step(0)
     tall_one = push(tall.at[tall_at(2 - 2 * core, 2)], tall_c, s_tall.at[0], r_tall.at[0], (grp_c, me))
     tall_one.start()
 
@@ -601,11 +607,6 @@
     back.start()
     two.finish()
 
-    def down_term(step, way):
-        return dot_f32(hidden[behind(step, way, n)], down[:, way * half : (way + 1) * half])
-
-    three = Scatter(n, held_one, terms, s_three, r_three, ends, down_term)
-
     def dob(slot, _):
         dattended[slot] = nt_dot(dresid[slot], w_out[...]).astype(bf16)
         return 0
@@ -660,7 +661,7 @@
         lax.fori_loop(low, jnp.minimum(2 * t + 1, n), dob, 0)
 
         def inner(step, _):
-            pl.when(step < n - 1)(lambda: three.step(step))
+            pl.when(step < n - 2)(lambda: three.step(step + 1))
 
             @pl.when(step < n // 2)
             def _():
@@ -1464,8 +1465,10 @@
     )
 
 
-def assemble_kernel(n, units, lanes, head_lanes, qkv, gate_up, down, out, blocks, shift, *grads):
-    grad_qkv, grad_out, grad_gate, grad_up, grad_down, block_out, x_grad = grads
+def assemble_kernel(n, units, lanes, head_lanes, qkv, gate_up, down, out, blocks, shift, gains, *grads):
+    grad_qkv, grad_out, grad_gate, grad_up, grad_down, block_out, x_grad, gain_one, gain_two = grads
+    gain_one[...] = gains[0]
+    gain_two[...] = gains[1]
     block_out[...] = blocks[...]
     x_grad[...] = shift[...]
     f32 = jnp.float32
@@ -1482,7 +1485,7 @@
     grad_down[...] = down[...].astype(f32)
 
 
-def assemble(qkv, gate_up, down, out, block_out, x_grad, units, steps=4):
+def assemble(qkv, gate_up, down, out, block_out, x_grad, gains, units, steps=4):
     n, rows, qkv_lanes = qkv.shape
     columns = down.shape[1]
     lanes = gate_up.shape[2] // 2
@@ -1509,6 +1512,8 @@
             jax.ShapeDtypeStruct((units, columns), f32),
             jax.ShapeDtypeStruct(block_out.shape, block_out.dtype),
             jax.ShapeDtypeStruct(x_grad.shape, x_grad.dtype),
+            jax.ShapeDtypeStruct(gains.shape[1:], f32),
+            jax.ShapeDtypeStruct(gains.shape[1:], f32),
         ),
         in_specs=[
             wide(qkv_lanes),
@@ -1517,6 +1522,7 @@
             flat(out.shape[0] // steps, columns),
             flat(tokens, columns),
             flat(tokens, columns),
+            pl.BlockSpec(gains.shape, lambda i: (0, 0)),
         ],
         out_specs=[
             flat(step, n * qkv_lanes),
@@ -1526,10 +1532,12 @@
             flat(down_step, columns),
             flat(tokens, columns),
             flat(tokens, columns),
+            pl.BlockSpec(gains.shape[1:], lambda i: (0,)),
+            pl.BlockSpec(gains.shape[1:], lambda i: (0,)),
         ],
         compiler_params=pltpu.CompilerParams(vmem_limit_bytes=VMEM_BYTES),
         name="assemble",
-    )(qkv, gate_up, down, out, block_out, x_grad)
+    )(qkv, gate_up, down, out, block_out, x_grad, gains)
 
 
 def per_device(block_input, doc_lens, norm_attn, w_qkv, w_out, norm_mlp, w_gate, w_up, w_down, cot):
@@ -1590,22 +1598,33 @@
         down_sum,
     )
     shard_rows = 4 * quarter
-    grad_qkv, grad_out, grad_gate, grad_up, grad_down, block_out, x_grad = assemble(
+    (
+        grad_qkv,
+        grad_out,
+        grad_gate,
+        grad_up,
+        grad_down,
+        block_out,
+        x_grad,
+        grad_norm_attn,
+        grad_norm_mlp,
+    ) = assemble(
         wide_qkv.reshape(n, shard_rows, qkv_lanes),
         wide_gate_up.reshape(n, shard_rows, 2 * lanes),
         tall_down.reshape(lanes, width),
         tall_out.reshape(head_lanes, width),
         block_out,
         x_grad,
+        gain_grads,
         units,
     )
     return (
         block_out[None],
         x_grad[None],
-        gain_grads[0],
+        grad_norm_attn,
         grad_qkv,
         grad_out,
-        gain_grads[1],
+        grad_norm_mlp,
         grad_gate,
         grad_up,
         grad_down,

time: 487 us -> 485 us (level)
  no operation moved by 1% of the time
where the time goes in v9:
time: 485 us
  Pallas kernels  484 us (100%)
    pallas_call x1, Pallas kernels, mlp_and_back(): pl.pallas_call(functools.partial(mlp_kernel, n, lanes), out_shape=(jax.Sh...  215 us
    pallas_call x1, Pallas kernels, attend(): pl.pallas_call(functools.partial(attend_kernel, n, heads), out_shape=(jax...  143 us
    pallas_call x1, Pallas kernels, finish(): pl.pallas_call(functools.partial(finish_kernel, n, heads), out_shape=(jax...  113 us
    pallas_call x1, Pallas kernels, assemble(): pl.pallas_call(functools.partial(assemble_kernel, n, units, lanes, head_l...  13.4 us

profile of v9, /device:TPU:1, one launch (start us, length us, event | category | flops | bytes accessed | tf_op | source)
XLA Modules:
  0.0 485.0 jit_solution(15156792624649215050)
XLA Ops:
  0.6 142.6 %attend.1 = (f32[1,2048]{1,0:T(1,128)}, f32[1,2048]{1,0:T(1,128)}, bf16[8,4,64,768]{3,2,1,0:T(8,128)(2,1)}, bf16[8,128,2048]{2,1,0:T(8,128)(2,1)}, bf16[1024,768...) custom-call(s32[1,8]{1,0:T(1,128)} %doc_lens.3, ...), custom_call_target="tpu_custom_call" | custom-call | tf_op jit(solution)/shard_map/attend/pallas_call | solution.py:1063
  143.3 215.2 %mlp_and_back.1 = (bf16[128,2048]{1,0:T(8,128)(2,1)}, f32[128,2048]{1,0:T(8,128)}, bf16[8,128,256]{2,1,0:T(8,128)(2,1)}, f32[1,2048]{1,0:T(1,128)}, bf16[8,64,14...) custom-call(bf16[8,128,256]{2,1,0:T(8,128)(2,1)} %bitcast.26, bf16[256,2048]{1,0:T(8,128)(2,1)} %w_out.1, ...), custom_call_target="tpu_custom_call" | custom-call | tf_op jit(solution)/shard_map/mlp_and_back/pallas_call | solution.py:724
  358.5 112.9 %finish.1 = (bf16[128,2048]{1,0:T(8,128)(2,1)}, f32[8,256]{1,0:T(8,128)}, bf16[8,4,64,1408]{3,2,1,0:T(8,128)(2,1)}, bf16[8,4,64,768]{3,2,1,0:T(8,128)(2,1)}, bf1...) custom-call(bf16[1024,768]{1,0:T(8,128)(2,1)} %get-tuple-element.43.qkv, ...), custom_call_target="tpu_custom_call" | custom-call | tf_op jit(solution)/shard_map/finish/pallas_call | solution.py:1411
  471.4 13.4 %assemble.1 = (f32[256,6144]{1,0:T(8,128)}, f32[256,2048]{1,0:T(8,128)}, f32[256,5632]{1,0:T(8,128)}, f32[256,5632]{1,0:T(8,128)}, f32[704,2048]{1,0:T(8,128)}, ...) custom-call(bf16[8,256,768]{2,1,0:T(8,128)(2,1)} %bitcast.18, ...), custom_call_target="tpu_custom_call" | custom-call | tf_op jit(solution)/shard_map/assemble/pallas_call | solution.py:1504
